TPU v7x, 32 devices: a whole 2x2x4 slice. The times are simulated.
32 devices in a mesh: dp: 16 (over z, x, core), blk: 2 (over y).
Axes of the slice: x: 2, y: 2, z: 4, core: 2. Of those that a mesh axis runs over, the one named last changes fastest.
Arguments:
- segment: bfloat16 [16, 960, 1024], P('dp', 'blk'), may hold values from -6 to 6
- memory: bfloat16 [16, 960, 1024], P('dp', 'blk'), may hold values from -6 to 6
- comp_memory: bfloat16 [16, 512, 1024], P('dp', 'blk'), may hold values from -6 to 6
- mem_start: int32 [16], P('dp'), may hold values from 0 to 512
- first_gain: bfloat16 [1024], replicated, may hold values from 0.5 to 1.5
- first_bias: bfloat16 [1024], replicated, may hold values from -1.25 to 1.25
- w_query: bfloat16 [1024, 1024], replicated, may hold values from -0.1875 to 0.1875
- w_key: bfloat16 [1024, 1024], replicated, may hold values from -0.1875 to 0.1875
- w_value: bfloat16 [1024, 1024], replicated, may hold values from -0.1875 to 0.1875
- w_rel: bfloat16 [1024, 1024], replicated, may hold values from -0.1875 to 0.1875
- u_bias: bfloat16 [1024], replicated, may hold values from -3 to 3
- v_bias: bfloat16 [1024], replicated, may hold values from -3 to 3
- w_out: bfloat16 [1024, 1024], replicated, may hold values from -1.5 to 1.5
- second_gain: bfloat16 [1024], replicated, may hold values from 0.5 to 1.5
- second_bias: bfloat16 [1024], replicated, may hold values from -1.25 to 1.25
- w_up: bfloat16 [1024, 4096], replicated, may hold values from -0.1875 to 0.1875
- b_up: bfloat16 [4096], replicated, may hold values from -1.25 to 1.25
- w_down: bfloat16 [4096, 1024], replicated, may hold values from -0.09375 to 0.09375
- b_down: bfloat16 [1024], replicated, may hold values from -1.75 to 1.75
- w_comp: bfloat16 [3072, 1024], replicated, may hold values from -0.109375 to 0.109375
- b_comp: bfloat16 [1024], replicated, may hold values from -1.75 to 1.75
- cot_out: bfloat16 [16, 960, 1024], P('dp', 'blk'), may hold values from -6 to 6
- cot_comp: bfloat16 [16, 320, 1024], P('dp', 'blk'), may hold values from -6 to 6
Outputs:
- layer_out: bfloat16 [16, 960, 1024], P('dp', 'blk')
- d_segment: bfloat16 [16, 960, 1024], P('dp', 'blk')
- new_compressed: bfloat16 [16, 320, 1024], P('dp', 'blk')
- grad_first_gain: float32 [1024], replicated
- grad_first_bias: float32 [1024], replicated
- grad_w_query: float32 [1024, 1024], replicated
- grad_w_key: float32 [1024, 1024], replicated
- grad_w_value: float32 [1024, 1024], replicated
- grad_w_rel: float32 [1024, 1024], replicated
- grad_u_bias: float32 [1024], replicated
- grad_v_bias: float32 [1024], replicated
- grad_w_out: float32 [1024, 1024], replicated
- grad_second_gain: float32 [1024], replicated
- grad_second_bias: float32 [1024], replicated
- grad_w_up: float32 [1024, 4096], replicated
- grad_b_up: float32 [4096], replicated
- grad_w_down: float32 [4096, 1024], replicated
- grad_b_down: float32 [1024], replicated
- grad_w_comp: float32 [3072, 1024], replicated
- grad_b_comp: float32 [1024], replicated
All inputs are finite; a program needn't handle non-finite values.
Results may differ from a plain program's by a relative error of at most 0.017.
Values may be sent and summed in bfloat16 or wider, within the bound.
No kernel may reach another device: no remote copies, remote signals or barrier semaphores. Data moves between devices by JAX's collectives and lax.ppermute only.
A program may use at most 448 MiB of HBM per device.

v0:
```python
from functools import partial

import jax
import jax.numpy as jnp
from jax import lax
from jax.sharding import PartitionSpec as P

D = 1024
H = 8
DH = 128
MEM = 960
CMEM = 512
RATE = 3
KEYS = 2432
NREL = 3391


epsilon = 1e-05
negative = -1e30


def from_behind(value, axis, steps):
    count = lax.axis_size(axis)
    pairs = [(source, (source + steps) % count) for source in range(count)]
    return lax.ppermute(value, axis, pairs)


def layer_norm(values, gain, bias):
    centred = values - jnp.mean(values, -1, keepdims=True)
    inverse = lax.rsqrt(jnp.mean(centred * centred, -1, keepdims=True) + epsilon)
    normal = centred * inverse
    return (normal * gain + bias, normal, inverse)


def norm_back(grad, normal, inverse, gain):
    scaled = grad * gain
    inner = (
        scaled
        - jnp.mean(scaled, -1, keepdims=True)
        - normal * jnp.mean(scaled * normal, -1, keepdims=True)
    )
    return (inner * inverse, jnp.sum(grad * normal, axis=(0, 1)), jnp.sum(grad, axis=(0, 1)))


def sinus_table():
    offsets = jnp.arange(NREL, dtype=jnp.float32)
    distance = KEYS - 1 - offsets
    frequency = 10000.0 ** (-2.0 * jnp.arange(D // 2, dtype=jnp.float32) / D)
    angles = distance[:, None] * frequency[None, :]
    return jnp.concatenate([jnp.sin(angles), jnp.cos(angles)], -1).astype(jnp.bfloat16)


def skew(table_scores, row_count, col_count):
    leading = table_scores.shape[:-2]
    padded = jnp.pad(table_scores, [(0, 0)] * len(leading) + [(0, 0), (0, 1)])
    flattened = padded.reshape(leading + (row_count * (row_count + col_count),))
    flattened = flattened[
        ..., row_count - 1 : row_count - 1 + row_count * (row_count + col_count - 1)
    ]
    return flattened.reshape(leading + (row_count, row_count + col_count - 1))[..., :col_count]


def unskew(grid, row_count, col_count):
    leading = grid.shape[:-2]
    padded = jnp.pad(grid, [(0, 0)] * len(leading) + [(0, 0), (0, row_count - 1)])
    flattened = padded.reshape(leading + (row_count * (row_count + col_count - 1),))
    flattened = jnp.pad(flattened, [(0, 0)] * len(leading) + [(row_count - 1, 1)])
    return flattened.reshape(leading + (row_count, row_count + col_count))[
        ..., : row_count + col_count - 1
    ]


def outer(left, right):
    return jnp.einsum("srk,srn->kn", left, right, preferred_element_type=jnp.float32)


def back_through(grad, weight):
    return jnp.einsum("srn,kn->srk", grad, weight, preferred_element_type=jnp.float32)


def on_device(
    segment,
    memory,
    comp_memory,
    mem_start,
    first_gain,
    first_bias,
    w_query,
    w_key,
    w_value,
    w_rel,
    u_bias,
    v_bias,
    w_out,
    second_gain,
    second_bias,
    w_up,
    b_up,
    w_down,
    b_down,
    w_comp,
    b_comp,
    cot_out,
    cot_comp,
):
    wide = jnp.float32
    narrow = jnp.bfloat16
    streams, seg_rows, width = segment.shape
    mem_rows = memory.shape[1]
    comp_rows = comp_memory.shape[1]
    local_rows = comp_rows + mem_rows + seg_rows
    past_rows = comp_rows + mem_rows
    blocks = lax.axis_size("blk")
    here = lax.axis_index("blk")
    scale = DH ** (-0.5)
    q_first = CMEM + MEM + here * seg_rows
    query_place = q_first + jnp.arange(seg_rows, dtype=jnp.int32)
    keys_in = jnp.concatenate([comp_memory, memory, segment], 1).astype(wide)
    normed_wide, normal_first, inverse_first = layer_norm(
        keys_in, first_gain.astype(wide), first_bias.astype(wide)
    )
    normed = normed_wide.astype(narrow)
    seg_normed = normed[:, past_rows:]
    query_rows = jnp.dot(seg_normed, w_query, preferred_element_type=wide)
    q_content = (query_rows + u_bias.astype(wide)).astype(narrow).reshape(streams, seg_rows, H, DH)
    q_position = (query_rows + v_bias.astype(wide)).astype(narrow).reshape(streams, seg_rows, H, DH)
    sinus = sinus_table()
    relative = (
        jnp.dot(sinus, w_rel, preferred_element_type=wide).astype(narrow).reshape(NREL, H, DH)
    )

    def spans(source):
        return [
            (0, comp_rows, source * comp_rows),
            (comp_rows, mem_rows, CMEM + source * mem_rows),
            (past_rows, seg_rows, CMEM + MEM + source * seg_rows),
        ]

    def run_scores(key_run, key_first, length):
        span_max = q_first + seg_rows - 1 - key_first
        table_first = KEYS - 1 - span_max
        window = lax.dynamic_slice_in_dim(relative, table_first, seg_rows + length - 1, 0)
        content = jnp.einsum("sqhd,skhd->shqk", q_content, key_run, preferred_element_type=wide)
        table_scores = jnp.einsum("sqhd,whd->shqw", q_position, window, preferred_element_type=wide)
        scores = (content + skew(table_scores, seg_rows, length)) * scale
        key_place = key_first + jnp.arange(length, dtype=jnp.int32)
        allowed = (key_place[None, None, None, :] >= mem_start[:, None, None, None]) & (
            key_place[None, None, None, :] <= query_place[None, None, :, None]
        )
        return (scores, allowed, window, table_first)

    def attend(state, key_run, value_run, key_first, length):
        running_max, running_sum, running_out = state
        scores, allowed, window, table_first = run_scores(key_run, key_first, length)
        new_max = jnp.maximum(running_max, jnp.max(jnp.where(allowed, scores, negative), -1))
        unnormed = jnp.where(
            allowed, jnp.exp(jnp.where(allowed, scores - new_max[..., None], negative)), 0.0
        )
        factor = jnp.exp(running_max - new_max)
        running_sum = running_sum * factor + jnp.sum(unnormed, -1)
        running_out = running_out * factor[..., None] + jnp.einsum(
            "shqk,skhd->shqd", unnormed.astype(narrow), value_run, preferred_element_type=wide
        )
        return (new_max, running_sum, running_out)

    def attend_block(state, key_block, value_block, source):
        for offset, length, key_first in spans(source)[:2]:
            state = attend(
                state,
                key_block[:, offset : offset + length],
                value_block[:, offset : offset + length],
                key_first,
                length,
            )
        offset, length, key_first = spans(source)[2]

        def attend_visit(inner):
            return attend(
                inner,
                key_block[:, offset : offset + length],
                value_block[:, offset : offset + length],
                key_first,
                length,
            )

        return lax.cond(source <= here, attend_visit, lambda inner: inner, state)

    key_heads = jnp.dot(normed, w_key, preferred_element_type=wide).astype(narrow)
    value_heads = jnp.dot(normed, w_value, preferred_element_type=wide).astype(narrow)
    own_keys = key_heads.reshape(streams, local_rows, H, DH)
    own_values = value_heads.reshape(streams, local_rows, H, DH)
    state = (
        jnp.full((streams, H, seg_rows), negative, wide),
        jnp.zeros((streams, H, seg_rows), wide),
        jnp.zeros((streams, H, seg_rows, DH), wide),
    )
    state = attend_block(state, own_keys, own_values, here)
    kept = [(own_keys, own_values, here)]
    far_keys, far_values = (own_keys, own_values)
    cycle_step = 1
    far_keys, far_values = from_behind((far_keys, far_values), "blk", 1)
    source = jnp.mod(here - cycle_step, blocks)
    kept.append((far_keys, far_values, source))
    state = attend_block(state, far_keys, far_values, source)
    running_max, running_sum, running_out = state
    attended = running_out / running_sum[..., None]
    log_total = running_max + jnp.log(running_sum)
    attended_low = (
        jnp.transpose(attended, (0, 2, 1, 3)).reshape(streams, seg_rows, width).astype(narrow)
    )
    branch = jnp.dot(attended_low, w_out, preferred_element_type=wide)
    hidden = segment.astype(wide) + branch
    second_wide, normal_second, inverse_second = layer_norm(
        hidden, second_gain.astype(wide), second_bias.astype(wide)
    )
    second_normed = second_wide.astype(narrow)
    pre_gelu = jnp.dot(second_normed, w_up, preferred_element_type=wide) + b_up.astype(wide)
    gelu_wide, gelu_back = jax.vjp(partial(jax.nn.gelu, approximate=True), pre_gelu)
    gelu_out = gelu_wide.astype(narrow)
    layer_out = (
        hidden + jnp.dot(gelu_out, w_down, preferred_element_type=wide) + b_down.astype(wide)
    ).astype(narrow)
    windows = memory.reshape(streams, mem_rows // RATE, RATE * width)
    new_compressed = (
        jnp.dot(windows, w_comp, preferred_element_type=wide) + b_comp.astype(wide)
    ).astype(narrow)
    grad_b_down = jnp.sum(cot_out.astype(wide), axis=(0, 1))
    grad_w_down = outer(gelu_out, cot_out)
    d_gelu = back_through(cot_out, w_down)
    d_pre = gelu_back(d_gelu)[0].astype(narrow)
    grad_b_up = jnp.sum(d_pre.astype(wide), axis=(0, 1))
    grad_w_up = outer(second_normed, d_pre)
    d_second, grad_second_gain, grad_second_bias = norm_back(
        back_through(d_pre, w_up), normal_second, inverse_second, second_gain.astype(wide)
    )
    d_hidden = cot_out.astype(wide) + d_second
    d_branch = d_hidden.astype(narrow)
    grad_w_out = outer(attended_low, d_branch)
    d_attended = back_through(d_branch, w_out).astype(narrow).reshape(streams, seg_rows, H, DH)
    delta = jnp.einsum("sqhd,shqd->shq", d_attended.astype(wide), attended)

    def attend_back(carry, key_run, value_run, key_first, length):
        d_content, d_position, d_relative = carry
        scores, allowed, window, table_first = run_scores(key_run, key_first, length)
        probs = jnp.where(
            allowed, jnp.exp(jnp.where(allowed, scores - log_total[..., None], negative)), 0.0
        )
        d_probs = jnp.einsum("sqhd,skhd->shqk", d_attended, value_run, preferred_element_type=wide)
        d_scores = (probs * (d_probs - delta[..., None])).astype(narrow)
        d_content = d_content + scale * jnp.einsum(
            "shqk,skhd->sqhd", d_scores, key_run, preferred_element_type=wide
        )
        d_keys = scale * jnp.einsum(
            "shqk,sqhd->skhd", d_scores, q_content, preferred_element_type=wide
        )
        d_values = jnp.einsum(
            "shqk,sqhd->skhd", probs.astype(narrow), d_attended, preferred_element_type=wide
        )
        d_table = unskew(d_scores, seg_rows, length)
        d_position = d_position + scale * jnp.einsum(
            "shqw,whd->sqhd", d_table, window, preferred_element_type=wide
        )
        d_window = scale * jnp.einsum(
            "shqw,sqhd->whd", d_table, q_position, preferred_element_type=wide
        )
        span_rows = seg_rows + length - 1
        d_relative = lax.dynamic_update_slice_in_dim(
            d_relative,
            lax.dynamic_slice_in_dim(d_relative, table_first, span_rows, 0) + d_window,
            table_first,
            0,
        )
        return ((d_content, d_position, d_relative), d_keys, d_values)

    def back_block(carry, key_block, value_block, source):
        key_parts = []
        value_parts = []
        for offset, length, key_first in spans(source)[:2]:
            carry, d_keys, d_values = attend_back(
                carry,
                key_block[:, offset : offset + length],
                value_block[:, offset : offset + length],
                key_first,
                length,
            )
            key_parts.append(d_keys)
            value_parts.append(d_values)
        offset, length, key_first = spans(source)[2]

        def back_visit(inner):
            return attend_back(
                inner,
                key_block[:, offset : offset + length],
                value_block[:, offset : offset + length],
                key_first,
                length,
            )

        def passby(inner):
            empty = jnp.zeros((streams, length, H, DH), wide)
            return (inner, empty, empty)

        carry, d_keys, d_values = lax.cond(source <= here, back_visit, passby, carry)
        key_parts.append(d_keys)
        value_parts.append(d_values)
        return (carry, jnp.concatenate(key_parts, 1), jnp.concatenate(value_parts, 1))

    carry = (
        jnp.zeros((streams, seg_rows, H, DH), wide),
        jnp.zeros((streams, seg_rows, H, DH), wide),
        jnp.zeros((NREL, H, DH), wide),
    )
    carry, home_keys, home_values = back_block(carry, own_keys, own_values, here)
    cycle_step = 1
    held_keys, held_values, source = kept[cycle_step]
    carry, d_far_keys, d_far_values = back_block(carry, held_keys, held_values, source)
    back_keys = from_behind(d_far_keys.astype(jnp.bfloat16), "blk", -cycle_step).astype(
        d_far_keys.dtype
    )
    back_values = from_behind(d_far_values.astype(jnp.bfloat16), "blk", -cycle_step).astype(
        d_far_values.dtype
    )
    home_keys = home_keys + back_keys
    home_values = home_values + back_values
    d_content, d_position, d_relative = carry
    d_key_low = home_keys.astype(narrow).reshape(streams, local_rows, width)
    d_value_low = home_values.astype(narrow).reshape(streams, local_rows, width)
    d_query = (d_content + d_position).astype(narrow).reshape(streams, seg_rows, width)
    grad_u_bias = jnp.sum(d_content, axis=(0, 1)).reshape(width)
    grad_v_bias = jnp.sum(d_position, axis=(0, 1)).reshape(width)
    grad_w_query = outer(seg_normed, d_query)
    grad_w_key = outer(normed, d_key_low)
    grad_w_value = outer(normed, d_value_low)
    rel_flat = d_relative.reshape(NREL, width)
    rel_upper = rel_flat.astype(narrow)
    rel_lower = (rel_flat - rel_upper.astype(wide)).astype(narrow)
    grad_w_rel = jnp.einsum(
        "wk,wn->kn", sinus, rel_upper, preferred_element_type=wide
    ) + jnp.einsum("wk,wn->kn", sinus, rel_lower, preferred_element_type=wide)
    d_normed = back_through(d_key_low, w_key) + back_through(d_value_low, w_value)
    query_part = back_through(d_query, w_query)
    d_normed = jnp.concatenate([d_normed[:, :past_rows], d_normed[:, past_rows:] + query_part], 1)
    d_keys_in, grad_first_gain, grad_first_bias = norm_back(
        d_normed, normal_first, inverse_first, first_gain.astype(wide)
    )
    d_segment = (d_hidden + d_keys_in[:, past_rows:]).astype(narrow)
    grad_w_comp = outer(windows, cot_comp)
    grad_b_comp = jnp.sum(cot_comp.astype(wide), axis=(0, 1))
    shares = (
        lax.psum_scatter(grad_first_gain, ("dp", "blk"), scatter_dimension=0, tiled=True),
        lax.psum_scatter(grad_first_bias, ("dp", "blk"), scatter_dimension=0, tiled=True),
        lax.psum_scatter(grad_w_query, ("dp", "blk"), scatter_dimension=0, tiled=True),
        lax.psum_scatter(grad_w_key, ("dp", "blk"), scatter_dimension=0, tiled=True),
        lax.psum_scatter(grad_w_value, ("dp", "blk"), scatter_dimension=0, tiled=True),
        lax.psum_scatter(grad_w_rel, ("dp", "blk"), scatter_dimension=0, tiled=True),
        lax.psum_scatter(grad_u_bias, ("dp", "blk"), scatter_dimension=0, tiled=True),
        lax.psum_scatter(grad_v_bias, ("dp", "blk"), scatter_dimension=0, tiled=True),
        lax.psum_scatter(grad_w_out, ("dp", "blk"), scatter_dimension=0, tiled=True),
        lax.psum_scatter(grad_second_gain, ("dp", "blk"), scatter_dimension=0, tiled=True),
        lax.psum_scatter(grad_second_bias, ("dp", "blk"), scatter_dimension=0, tiled=True),
        lax.psum_scatter(grad_w_up, ("dp", "blk"), scatter_dimension=0, tiled=True),
        lax.psum_scatter(grad_b_up, ("dp", "blk"), scatter_dimension=0, tiled=True),
        lax.psum_scatter(grad_w_down, ("dp", "blk"), scatter_dimension=0, tiled=True),
        lax.psum_scatter(grad_b_down, ("dp", "blk"), scatter_dimension=0, tiled=True),
        lax.psum_scatter(grad_w_comp, ("dp", "blk"), scatter_dimension=0, tiled=True),
        lax.psum_scatter(grad_b_comp, ("dp", "blk"), scatter_dimension=0, tiled=True),
    )
    totals = (
        lax.all_gather(shares[0].astype(jnp.bfloat16), ("dp", "blk"), axis=0, tiled=True).astype(
            jnp.float32
        ),
        lax.all_gather(shares[1].astype(jnp.bfloat16), ("dp", "blk"), axis=0, tiled=True).astype(
            jnp.float32
        ),
        lax.all_gather(shares[2].astype(jnp.bfloat16), ("dp", "blk"), axis=0, tiled=True).astype(
            jnp.float32
        ),
        lax.all_gather(shares[3].astype(jnp.bfloat16), ("dp", "blk"), axis=0, tiled=True).astype(
            jnp.float32
        ),
        lax.all_gather(shares[4].astype(jnp.bfloat16), ("dp", "blk"), axis=0, tiled=True).astype(
            jnp.float32
        ),
        lax.all_gather(shares[5].astype(jnp.bfloat16), ("dp", "blk"), axis=0, tiled=True).astype(
            jnp.float32
        ),
        lax.all_gather(shares[6].astype(jnp.bfloat16), ("dp", "blk"), axis=0, tiled=True).astype(
            jnp.float32
        ),
        lax.all_gather(shares[7].astype(jnp.bfloat16), ("dp", "blk"), axis=0, tiled=True).astype(
            jnp.float32
        ),
        lax.all_gather(shares[8].astype(jnp.bfloat16), ("dp", "blk"), axis=0, tiled=True).astype(
            jnp.float32
        ),
        lax.all_gather(shares[9].astype(jnp.bfloat16), ("dp", "blk"), axis=0, tiled=True).astype(
            jnp.float32
        ),
        lax.all_gather(shares[10].astype(jnp.bfloat16), ("dp", "blk"), axis=0, tiled=True).astype(
            jnp.float32
        ),
        lax.all_gather(shares[11].astype(jnp.bfloat16), ("dp", "blk"), axis=0, tiled=True).astype(
            jnp.float32
        ),
        lax.all_gather(shares[12].astype(jnp.bfloat16), ("dp", "blk"), axis=0, tiled=True).astype(
            jnp.float32
        ),
        lax.all_gather(shares[13].astype(jnp.bfloat16), ("dp", "blk"), axis=0, tiled=True).astype(
            jnp.float32
        ),
        lax.all_gather(shares[14].astype(jnp.bfloat16), ("dp", "blk"), axis=0, tiled=True).astype(
            jnp.float32
        ),
        lax.all_gather(shares[15].astype(jnp.bfloat16), ("dp", "blk"), axis=0, tiled=True).astype(
            jnp.float32
        ),
        lax.all_gather(shares[16].astype(jnp.bfloat16), ("dp", "blk"), axis=0, tiled=True).astype(
            jnp.float32
        ),
    )
    return (
        layer_out,
        d_segment,
        new_compressed,
        totals[0],
        totals[1],
        totals[2],
        totals[3],
        totals[4],
        totals[5],
        totals[6],
        totals[7],
        totals[8],
        totals[9],
        totals[10],
        totals[11],
        totals[12],
        totals[13],
        totals[14],
        totals[15],
        totals[16],
    )


def solution(mesh):
    in_specs = (
        P("dp", "blk", None),
        P("dp", "blk", None),
        P("dp", "blk", None),
        P("dp"),
        P(),
        P(),
        P(),
        P(),
        P(),
        P(),
        P(),
        P(),
        P(),
        P(),
        P(),
        P(),
        P(),
        P(),
        P(),
        P(),
        P(),
        P("dp", "blk", None),
        P("dp", "blk", None),
    )
    out_specs = (
        P("dp", "blk", None),
        P("dp", "blk", None),
        P("dp", "blk", None),
        P(),
        P(),
        P(),
        P(),
        P(),
        P(),
        P(),
        P(),
        P(),
        P(),
        P(),
        P(),
        P(),
        P(),
        P(),
        P(),
        P(),
    )
    return jax.shard_map(
        on_device, mesh=mesh, in_specs=in_specs, out_specs=out_specs, check_vma=False
    )
```

profile of v0, /device:TPU:0, one launch (start us, length us, event | category | flops | bytes accessed | tf_op | source)
XLA Modules:
  0.0 3727.0 jit_solution(8066699019859289633)
XLA Ops:
  49.7 26.3 fusion.92
  112.4 15.6 reshape.2387
  163.3 16.0 reshape.2265
  245.9 16.3 reshape.2274
  275.1 15.6 copy.328
  305.5 19.0 reshape.2383
  349.1 17.9 reshape.2385
  367.1 16.9 reshape.2268
  408.3 15.6 copy.329
  438.7 19.2 reshape.2379
  482.5 17.9 reshape.2381
  500.5 16.8 reshape.2271
  594.4 19.2 reshape.2371
  638.3 18.0 reshape.2373
  656.3 16.8 reshape.2277
  1370.0 368.6 %collective-permute-start.2 = (bf16[1,1216,8,128]{3,1,2,0:T(8,128)(2,1)}, bf16[1,1216,8,128]{3,1,2,0:T(8,128)(2,1)}, u32[]{:S(2)}, u32[]{:S(2)}) collective-permute-start(bf16[1,1216,8,128]{3,1,2,0:T(8,128)(2,1)} %pad_maximum_fusion.3), channel_id=1, source_target_pairs={{0,1},{1,0},{2,3},{3,2},{4,5},{5,4},{6,7},{7,6},{8,9},{9,8},{10,11... | collective-permute-start | bytes 7471112 | tf_op jit(solution)/shard_map/ppermute | solution.py:25
  1746.3 98.5 %collective-permute-done.2 = bf16[1,1216,8,128]{3,1,2,0:T(8,128)(2,1)} collective-permute-done((bf16[1,1216,8,128]{3,1,2,0:T(8,128)(2,1)}, bf16[1,1216,8,128]{3,1,2,0:T(8,128)(2,1)}, u32[]{:S(2)}, u32[]{:S(2)}) %collective-permute-start.2) | collective-permute-done | bytes 2490400 | tf_op jit(solution)/shard_map/ppermute | solution.py:25
  1888.5 92.1 %collective-permute-done.3 = bf16[1,1216,8,128]{3,1,2,0:T(8,128)(2,1)} collective-permute-done((bf16[1,1216,8,128]{3,1,2,0:T(8,128)(2,1)}, bf16[1,1216,8,128]{3,1,2,0:T(8,128)(2,1)}, u32[]{:S(2)}, u32[]{:S(2)}) %collective-permute-start.3) | collective-permute-done | bytes 2490400 | tf_op jit(solution)/shard_map/ppermute | solution.py:25
  2005.0 15.6 fusion.342
  2040.1 116.4 %reduce-scatter.11.cloned.1.call-done = f32[32,1024]{1,0:T(8,128)} async-done(((f32[1024,1024]{1,0:T(8,128)}), f32[32,1024]{1,0:T(8,128)}) %reduce-scatter.11.cloned.1.call-update) | async-done | bytes 131088 | tf_op jit(solution)/shard_map/reduce_scatter | solution.py:353
  2158.1 140.0 %reduce-scatter.13.cloned.1.call-done = f32[32,1024]{1,0:T(8,128)} async-done(((f32[1024,1024]{1,0:T(8,128)}), f32[32,1024]{1,0:T(8,128)}) %reduce-scatter.13.cloned.1.call-update) | async-done | bytes 131088 | tf_op jit(solution)/shard_map/reduce_scatter | solution.py:354
  2299.7 157.7 %reduce-scatter.23.cloned.1.call-done = f32[96,1024]{1,0:T(8,128)} async-done(((f32[3072,1024]{1,0:T(8,128)}), f32[96,1024]{1,0:T(8,128)}) %reduce-scatter.23.cloned.1.call-update) | async-done | bytes 393232 | tf_op jit(solution)/shard_map/reduce_scatter | solution.py:365
  2459.1 357.7 %reduce-scatter.21.cloned.1.call-done = f32[128,1024]{1,0:T(8,128)} async-done(((f32[4096,1024]{1,0:T(8,128)}), f32[128,1024]{1,0:T(8,128)}) %reduce-scatter.21.cloned.1.call-update) | async-done | bytes 524304 | tf_op jit(solution)/shard_map/reduce_scatter | solution.py:363
  2818.7 359.6 %reduce-scatter.19.cloned.1.call-done = f32[32,4096]{1,0:T(8,128)} async-done(((f32[1024,4096]{1,0:T(8,128)}), f32[32,4096]{1,0:T(8,128)}) %reduce-scatter.19.cloned.1.call-update) | async-done | bytes 524304 | tf_op jit(solution)/shard_map/reduce_scatter | solution.py:361
  3212.9 41.5 %all-reduce.36 = (bf16[1024]{0:T(1024)(128)(2,1)S(1)}, bf16[1024]{0:T(1024)(128)(2,1)S(1)}, bf16[1024]{0:T(1024)(128)(2,1)S(1)}, bf16[1024]{0:T(1024)(128)(2,1)S...) all-reduce(f32[1024]{0:T(1024)S(1)} %get-tuple-element.247, ...), channel_id=2, replica_groups=mesh['dp'=16,'blk'=2] {'dp','blk'}, use_global_device_ids=true, to_apply=%region_25.26.clone | all-reduce | flops 12288 | bytes 73728
  3256.6 40.5 %all-reduce.37 = (bf16[1024]{0:T(1024)(128)(2,1)S(1)}, bf16[1024]{0:T(1024)(128)(2,1)S(1)}, bf16[1024]{0:T(1024)(128)(2,1)S(1)}, bf16[1024]{0:T(1024)(128)(2,1)S...) all-reduce(bf16[1024]{0:T(1024)(128)(2,1)S(1)} %dynamic-update-slic, ...), channel_id=1, replica_groups=mesh['dp'=16,'blk'=2] {'dp','blk'}, use_global_device_ids=true, to_apply=%add.19 | all-reduce | flops 8192 | bytes 32768
  3302.1 65.7 %all-gather = bf16[32,1,128]{2,1,0:T(2,128)(2,1)S(1)} all-gather(bf16[1,1,128]{2,1,0:T(2,128)(2,1)S(1)} %fusion.374), channel_id=1, replica_groups=mesh['dp'=16,'blk'=2] {'dp','blk'}, dimensions={0}, use_global_device_ids=true | all-gather | bytes 8448 | tf_op jit(solution)/shard_map/all_gather | solution.py:405
  3384.8 32.7 all-gather.12.cloned.1.call-done
  3421.6 55.5 %all-gather.14.cloned.1.call-done = bf16[1024,1024]{1,0:T(8,128)(2,1)} async-done(((bf16[32,1024]{1,0:T(8,128)(2,1)}), bf16[1024,1024]{1,0:T(8,128)(2,1)}) %all-gather.14.cloned.1.call-update) | async-done | bytes 2097168 | tf_op jit(solution)/shard_map/all_gather | solution.py:381
  3481.1 67.5 %all-gather.24.cloned.1.call-done = bf16[3072,1024]{1,0:T(8,128)(2,1)} async-done(((bf16[96,1024]{1,0:T(8,128)(2,1)}), bf16[3072,1024]{1,0:T(8,128)(2,1)}) %all-gather.24.cloned.1.call-update) | async-done | bytes 6291472 | tf_op jit(solution)/shard_map/all_gather | solution.py:414
  3557.7 70.3 %all-gather.22.cloned.1.call-done = bf16[4096,1024]{1,0:T(8,128)(2,1)} async-done(((bf16[128,1024]{1,0:T(8,128)(2,1)}), bf16[4096,1024]{1,0:T(8,128)(2,1)}) %all-gather.22.cloned.1.call-update) | async-done | bytes 8388624 | tf_op jit(solution)/shard_map/all_gather | solution.py:408
  3639.7 68.3 %all-gather.20.cloned.1.call-done = bf16[1024,4096]{1,0:T(8,128)(2,1)} async-done(((bf16[32,4096]{1,0:T(8,128)(2,1)}), bf16[1024,4096]{1,0:T(8,128)(2,1)}) %all-gather.20.cloned.1.call-update) | async-done | bytes 8388624 | tf_op jit(solution)/shard_map/all_gather | solution.py:402
  (623 shorter events, 1295.9 us)
Async XLA Ops:
  7.2 2027.9 %reduce-scatter.17.cloned.1.call-start = ((), (), s32[]{:S(2)}) async-start(), calls=%async_computation.16 | async-start | bytes 4325376 | tf_op jit(solution)/shard_map/reduce_scatter | solution.py:358
  21.7 690.7 %collective-permute-start = (bf16[1,1216,8,128]{3,1,2,0:T(8,128)(2,1)}, bf16[1,1216,8,128]{3,1,2,0:T(8,128)(2,1)}, u32[]{:S(2)}, u32[]{:S(2)}) collective-permute-start(bf16[1,1216,8,128]{3,1,2,0:T(8,128)(2,1)} %copy.211), channel_id=1, source_target_pairs={{0,1},{1,0},{2,3},{3,2},{4,5},{5,4},{6,7},{7,6},{8,9},{9,8},{10,11... | collective-permute-start | bytes 7471112 | tf_op jit(solution)/shard_map/ppermute | solution.py:25
  32.4 690.9 %collective-permute-start.1 = (bf16[1,1216,8,128]{3,1,2,0:T(8,128)(2,1)}, bf16[1,1216,8,128]{3,1,2,0:T(8,128)(2,1)}, u32[]{:S(2)}, u32[]{:S(2)}) collective-permute-start(bf16[1,1216,8,128]{3,1,2,0:T(8,128)(2,1)} %copy.236), channel_id=1, source_target_pairs={{0,1},{1,0},{2,3},{3,2},{4,5},{5,4},{6,7},{7,6},{8,9},{9,8},{10,11... | collective-permute-start | bytes 7471112 | tf_op jit(solution)/shard_map/ppermute | solution.py:25
  47.2 508.8 %copy-start.2 = (bf16[60,8,8,128]{3,2,1,0:T(8,128)(2,1)}, bf16[60,8,8,128]{3,2,1,0:T(8,128)(2,1)S(1)}, u32[]{:S(2)}) copy-start(bf16[60,8,8,128]{3,2,1,0:T(8,128)(2,1)S(1)} %get-tuple-element.292) | copy-start | bytes 2949124
  95.3 84.0 %copy-start.35 = (bf16[735,8,128]{2,1,0:T(8,128)(2,1)}, bf16[735,8,128]{2,1,0:T(8,128)(2,1)S(1)}, u32[]{:S(2)}) copy-start(bf16[735,8,128]{2,1,0:T(8,128)(2,1)S(1)} %get-tuple-element.285) | copy-start | bytes 4515844
  533.9 160.0 %copy-start.75 = (pred[480,256]{1,0:T(8,128)(4,1)}, pred[480,256]{1,0:T(8,128)(4,1)S(1)}, u32[]{:S(2)}) copy-start(pred[480,256]{1,0:T(8,128)(4,1)S(1)} %get-tuple-element.308) | copy-start | bytes 368644
  533.9 189.4 %copy-start.78 = (pred[480,256]{1,0:T(8,128)(4,1)}, pred[480,256]{1,0:T(8,128)(4,1)S(1)}, u32[]{:S(2)}) copy-start(pred[480,256]{1,0:T(8,128)(4,1)S(1)} %get-tuple-element.309) | copy-start | bytes 368644
  540.2 162.2 %copy-start.62 = (pred[480,480]{0,1:T(8,128)(4,1)}, pred[480,480]{0,1:T(8,128)(4,1)S(1)}, u32[]{:S(2)}) copy-start(pred[480,480]{0,1:T(8,128)(4,1)S(1)} %get-tuple-element.310) | copy-start | bytes 691204
  540.2 167.2 %copy-start.65 = (pred[480,480]{0,1:T(8,128)(4,1)}, pred[480,480]{0,1:T(8,128)(4,1)S(1)}, u32[]{:S(2)}) copy-start(pred[480,480]{0,1:T(8,128)(4,1)S(1)} %get-tuple-element.312) | copy-start | bytes 691204
  540.2 185.5 %copy-start.68 = (pred[480,480]{0,1:T(8,128)(4,1)}, pred[480,480]{0,1:T(8,128)(4,1)S(1)}, u32[]{:S(2)}) copy-start(pred[480,480]{0,1:T(8,128)(4,1)S(1)} %get-tuple-element.311) | copy-start | bytes 691204
  783.6 191.4 %copy-start.37 = (bf16[480,1024]{1,0:T(8,128)(2,1)}, bf16[480,1024]{1,0:T(8,128)(2,1)S(1)}, u32[]{:S(2)}) copy-start(bf16[480,1024]{1,0:T(8,128)(2,1)S(1)} %convolution_convert_fusion.3) | copy-start | bytes 2949124
  812.6 1224.2 %reduce-scatter.9.cloned.1.call-start = ((), (), s32[]{:S(2)}) async-start(), calls=%async_computation.8 | async-start | bytes 4325376 | tf_op jit(solution)/shard_map/reduce_scatter | solution.py:352
  1312.0 726.4 %reduce-scatter.15.cloned.1.call-start = ((), (), s32[]{:S(2)}) async-start(), calls=%async_computation.14 | async-start | bytes 4325376 | tf_op jit(solution)/shard_map/reduce_scatter | solution.py:355
  1358.8 797.6 %reduce-scatter.11.cloned.1.call-start = ((), (), s32[]{:S(2)}) async-start(), calls=%async_computation.10 | async-start | bytes 4325376 | tf_op jit(solution)/shard_map/reduce_scatter | solution.py:353
  1368.4 370.2 %copy-start.16 = (bf16[1,8,480,256]{3,2,1,0:T(8,128)(2,1)S(1)}, bf16[1,8,480,256]{3,2,1,0:T(8,128)(2,1)}, u32[]{:S(2)}) copy-start(bf16[1,8,480,256]{3,2,1,0:T(8,128)(2,1)} %fusion.152) | copy-start | bytes 5898244
  1370.0 474.8 %collective-permute-start.2 = (bf16[1,1216,8,128]{3,1,2,0:T(8,128)(2,1)}, bf16[1,1216,8,128]{3,1,2,0:T(8,128)(2,1)}, u32[]{:S(2)}, u32[]{:S(2)}) collective-permute-start(bf16[1,1216,8,128]{3,1,2,0:T(8,128)(2,1)} %pad_maximum_fusion.3), channel_id=1, source_target_pairs={{0,1},{1,0},{2,3},{3,2},{4,5},{5,4},{6,7},{7,6},{8,9},{9,8},{10,11... | collective-permute-start | bytes 7471112 | tf_op jit(solution)/shard_map/ppermute | solution.py:25
  1860.9 437.2 %reduce-scatter.13.cloned.1.call-start = ((), (), s32[]{:S(2)}) async-start(), calls=%async_computation.12 | async-start | bytes 4325376 | tf_op jit(solution)/shard_map/reduce_scatter | solution.py:354
  1872.2 108.4 %collective-permute-start.3 = (bf16[1,1216,8,128]{3,1,2,0:T(8,128)(2,1)}, bf16[1,1216,8,128]{3,1,2,0:T(8,128)(2,1)}, u32[]{:S(2)}, u32[]{:S(2)}) collective-permute-start(bf16[1,1216,8,128]{3,1,2,0:T(8,128)(2,1)} %pad_maximum_fusion.4), channel_id=1, source_target_pairs={{0,1},{1,0},{2,3},{3,2},{4,5},{5,4},{6,7},{7,6},{8,9},{9,8},{10,11... | collective-permute-start | bytes 7471112 | tf_op jit(solution)/shard_map/ppermute | solution.py:25
  1883.5 97.2 %copy-start.47 = (f32[1,256,8,128]{3,1,2,0:T(8,128)S(1)}, f32[1,256,8,128]{3,1,2,0:T(8,128)}, u32[]{:S(2)}) copy-start(f32[1,256,8,128]{3,1,2,0:T(8,128)} %copy.283) | copy-start | bytes 3145732
  1996.7 460.7 %reduce-scatter.23.cloned.1.call-start = ((), (), s32[]{:S(2)}) async-start(), calls=%async_computation.22 | async-start | bytes 12976128 | tf_op jit(solution)/shard_map/reduce_scatter | solution.py:365
  2004.3 812.5 %reduce-scatter.21.cloned.1.call-start = ((), (), s32[]{:S(2)}) async-start(), calls=%async_computation.20 | async-start | bytes 17301504 | tf_op jit(solution)/shard_map/reduce_scatter | solution.py:363
  2020.6 1157.6 %reduce-scatter.19.cloned.1.call-start = ((), (), s32[]{:S(2)}) async-start(), calls=%async_computation.18 | async-start | bytes 17301504 | tf_op jit(solution)/shard_map/reduce_scatter | solution.py:361
  2034.9 1145.2 %copy-start.125 = (bf16[1024]{0:T(1024)(128)(2,1)S(1)}, bf16[1024]{0:T(1024)(128)(2,1)}, u32[]{:S(2)}) copy-start(bf16[1024]{0:T(1024)(128)(2,1)} %param.45) | copy-start | bytes 6148
  2034.9 1145.2 %copy-start.126 = (bf16[1024]{0:T(1024)(128)(2,1)S(1)}, bf16[1024]{0:T(1024)(128)(2,1)}, u32[]{:S(2)}) copy-start(bf16[1024]{0:T(1024)(128)(2,1)} %param.47) | copy-start | bytes 6148
  2034.9 1337.7 %all-gather.18.cloned.1.call-start = ((), (), s32[]{:S(2)}) async-start(), calls=%async_computation.17 | async-start | bytes 2162688 | tf_op jit(solution)/shard_map/all_gather | solution.py:393
  2036.7 1340.0 %all-gather.10.cloned.1.call-start = ((), (), s32[]{:S(2)}) async-start(), calls=%async_computation.9 | async-start | bytes 2162688 | tf_op jit(solution)/shard_map/all_gather | solution.py:375
  2038.4 1342.4 %all-gather.16.cloned.1.call-start = ((), (), s32[]{:S(2)}) async-start(), calls=%async_computation.15 | async-start | bytes 2162688 | tf_op jit(solution)/shard_map/all_gather | solution.py:384
  2040.0 1377.5 %all-gather.12.cloned.1.call-start = ((), (), s32[]{:S(2)}) async-start(), calls=%async_computation.11 | async-start | bytes 2162688 | tf_op jit(solution)/shard_map/all_gather | solution.py:378
  2158.0 1319.1 %all-gather.14.cloned.1.call-start = ((), (), s32[]{:S(2)}) async-start(), calls=%async_computation.13 | async-start | bytes 2162688 | tf_op jit(solution)/shard_map/all_gather | solution.py:381
  2299.6 1249.0 %all-gather.24.cloned.1.call-start = ((), (), s32[]{:S(2)}) async-start(), calls=%async_computation.23 | async-start | bytes 6488064 | tf_op jit(solution)/shard_map/all_gather | solution.py:414
  2459.1 1168.9 %all-gather.22.cloned.1.call-start = ((), (), s32[]{:S(2)}) async-start(), calls=%async_computation.21 | async-start | bytes 8650752 | tf_op jit(solution)/shard_map/all_gather | solution.py:408
  2818.6 889.4 %all-gather.20.cloned.1.call-start = ((), (), s32[]{:S(2)}) async-start(), calls=%async_computation.19 | async-start | bytes 8650752 | tf_op jit(solution)/shard_map/all_gather | solution.py:402
  (140 other events, 1133.6 us)
Sparse Core Ops, SparseCore 0:
  812.7 285.0 reduce-scatter.16
  1312.1 533.4 reduce-scatter.8
  1848.5 164.4 reduce-scatter.14
  2015.7 140.7 reduce-scatter.10
  2159.1 138.8 reduce-scatter.12
  2304.5 152.7 reduce-scatter.22
  2460.3 356.4 reduce-scatter.20
  2819.8 358.4 reduce-scatter.18
  3181.8 57.6 all-gather.17
  3243.5 55.5 all-gather.9
  3302.7 55.3 all-gather.15
  3362.2 55.3 all-gather.11
  3421.7 55.3 all-gather.13
  3480.2 68.3 all-gather.23
  3552.0 75.9 all-gather.21
  3632.0 75.9 all-gather.19
where the time goes:
time: 3750 us; the launch traced here: 3730 us
  waiting for transfers between devices  1620 us (43%)
  local copies, waits for them, and re-layouts  1000 us (27%)
  matrix products  383 us (10%)
  starting transfers between devices  374 us (10%)
  other arithmetic  170 us (5%)
  blocking collectives  148 us (4%)
    unnamed x364, local copies, waits for them, and re-layouts  398 us
    ppermute x4, starting transfers between devices, from_behind(): return lax.ppermute(value, axis, pairs)  372 us
    reduce_scatter x1, waiting for transfers between devices, on_device(): lax.psum_scatter(grad_w_up, ('dp', 'blk'), scatter_dimension=0, tiled=True)  360 us
    reduce_scatter x1, waiting for transfers between devices, on_device(): lax.psum_scatter(grad_w_down, ('dp', 'blk'), scatter_dimension=0, tiled=T...  358 us
    ppermute x4, waiting for transfers between devices, from_behind(): return lax.ppermute(value, axis, pairs)  191 us
    reduce_scatter x1, waiting for transfers between devices, on_device(): lax.psum_scatter(grad_w_comp, ('dp', 'blk'), scatter_dimension=0, tiled=T...  158 us
    reduce_scatter x1, waiting for transfers between devices, on_device(): lax.psum_scatter(grad_w_value, ('dp', 'blk'), scatter_dimension=0, tiled=...  140 us
    reduce_scatter x1, waiting for transfers between devices, on_device(): lax.psum_scatter(grad_w_key, ('dp', 'blk'), scatter_dimension=0, tiled=True)  116 us
  transfers between devices with their start and end apart: 20, of which 12 were waited for; matrix products, arithmetic and copies ran while one was open for 39% of the time, Pallas kernels for 0%

commit v1 on v0

v1 whole, which is shorter than its diff:
```python
from functools import partial

import jax
import jax.numpy as jnp
from jax import lax
from jax.experimental import pallas as pl
from jax.experimental.pallas import tpu as pltpu
from jax.sharding import PartitionSpec as P

D = 1024
H = 8
DH = 128
MEM = 960
CMEM = 512
RATE = 3
KEYS = 2432

TILE = 192
epsilon = 1e-05
negative = -1e30
wide = jnp.float32
narrow = jnp.bfloat16


def tiles_of(seg, keys, tile):
    tiles = []
    for first in range(0, seg, tile):
        used = keys - seg + first + tile
        cols = -(-used // 128) * 128
        tiles.append((first, cols, keys - cols, cols - used))
    return tiles


def dot(left, right, left_dim, right_dim):
    return lax.dot_general(
        left, right, (((left_dim,), (right_dim,)), ((), ())), preferred_element_type=wide
    )


def unskew(grid, tile, cols, pad):
    parts = []
    for group in range(tile // 8):
        shift = tile - 1 + pad - 8 * group - 7
        rows = grid[8 * group : 8 * group + 8]
        parts.append(pltpu.roll(rows, shift, 1) if shift else rows)
    moved = jnp.concatenate(parts, 0)
    left = 7 - (lax.broadcasted_iota(jnp.int32, (tile, cols), 0) & 7)
    for bit in range(3):
        moved = jnp.where((left & (1 << bit)) != 0, pltpu.roll(moved, 1 << bit, 1), moved)
    return moved


def attend_kernel(seg, keys, start_ref, qc_ref, qp_ref, kv_ref, rel_ref, out_ref, probs_ref):
    past = keys - seg
    factor = DH**-0.5 * 1.4426950408889634
    start = start_ref[0]
    for first, cols, base, pad in tiles_of(seg, keys, TILE):
        rows = pl.ds(first, TILE)
        content = dot(qc_ref[rows, :], kv_ref[0:cols, 0:DH], 1, 1)
        table = dot(qp_ref[rows, :], rel_ref[base : base + cols, :], 1, 1)
        table = pltpu.roll(table, cols - (TILE - 1 + pad), 1, stride=1, stride_axis=0)
        scores = content + table
        left = scores[:, :CMEM]
        lane = lax.broadcasted_iota(jnp.int32, left.shape, 1)
        left = jnp.where(lane >= start, left, negative)
        edge = (past + first) // 128 * 128
        right = scores[:, edge:]
        lane = lax.broadcasted_iota(jnp.int32, right.shape, 1) + (edge - past - first)
        row = lax.broadcasted_iota(jnp.int32, right.shape, 0)
        right = jnp.where(lane <= row, right, negative)
        scores = jnp.concatenate([left, scores[:, CMEM:edge], right], 1)
        largest = jnp.max(scores, -1, keepdims=True)
        probs = jnp.exp2(scores * factor - largest * factor)
        probs = (probs * (1.0 / jnp.sum(probs, -1, keepdims=True))).astype(narrow)
        probs_ref[0, rows, 0:cols] = probs
        out_ref[rows, :] = dot(probs, kv_ref[0:cols, DH:], 1, 0).astype(narrow)


def attend(start, q_content, q_position, key_value, relative):
    seg, width = q_content.shape
    keys, heads = key_value.shape[0], width // DH
    per_query = pl.BlockSpec((seg, DH), lambda h: (0, h))
    flops = 6 * heads * seg * keys * DH
    return pl.pallas_call(
        partial(attend_kernel, seg, keys),
        grid=(heads,),
        in_specs=[
            pl.BlockSpec(memory_space=pltpu.SMEM),
            per_query,
            per_query,
            pl.BlockSpec((keys, 2 * DH), lambda h: (0, h)),
            pl.BlockSpec((keys, DH), lambda h: (0, h)),
        ],
        out_specs=[per_query, pl.BlockSpec((1, seg, keys), lambda h: (h, 0, 0))],
        out_shape=[
            jax.ShapeDtypeStruct((seg, width), narrow),
            jax.ShapeDtypeStruct((heads, seg, keys), narrow),
        ],
        compiler_params=pltpu.CompilerParams(vmem_limit_bytes=56 << 20),
        cost_estimate=pl.CostEstimate(
            flops=flops, bytes_accessed=32 << 20, transcendentals=heads * seg * keys
        ),
        name="attend",
    )(start, q_content, q_position, key_value, relative)


def attend_back_kernel(
    seg,
    keys,
    probs_ref,
    qc_ref,
    qp_ref,
    kv_ref,
    rel_ref,
    da_ref,
    dq_ref,
    dkv_ref,
    drel_ref,
    gu_ref,
    gv_ref,
    key_sum,
    value_sum,
    rel_sum,
):
    scale = DH**-0.5
    grad_u = jnp.zeros((1, DH), wide)
    grad_v = jnp.zeros((1, DH), wide)
    for step, (first, cols, base, pad) in enumerate(tiles_of(seg, keys, TILE)[::-1]):
        rows = pl.ds(first, TILE)
        probs = probs_ref[0, rows, 0:cols]
        probs_wide = probs.astype(wide)
        d_out, qc, qp = da_ref[rows, :], qc_ref[rows, :], qp_ref[rows, :]
        d_probs = dot(d_out, kv_ref[0:cols, DH:], 1, 1)
        weighted = probs_wide * d_probs
        d_scores = weighted - probs_wide * jnp.sum(weighted, -1, keepdims=True)
        d_low = d_scores.astype(narrow)
        d_table = unskew(d_scores, TILE, cols, pad).astype(narrow)
        d_content = dot(d_low, kv_ref[0:cols, 0:DH], 1, 0)
        d_position = dot(d_table, rel_ref[base : base + cols, :], 1, 0)
        grad_u += jnp.sum(d_content, 0, keepdims=True)
        grad_v += jnp.sum(d_position, 0, keepdims=True)
        dq_ref[rows, :] = ((d_content + d_position) * scale).astype(narrow)
        d_key = dot(qc, d_low, 0, 0)
        d_value = dot(d_out, probs, 0, 0)
        d_rel = dot(qp, d_table, 0, 0)
        if step == 0:
            key_sum[...] = d_key
            value_sum[...] = d_value
            rel_sum[...] = d_rel
        else:
            key_sum[:, 0:cols] += d_key
            value_sum[:, 0:cols] += d_value
            rel_sum[:, base : base + cols] += d_rel
    dkv_ref[:, 0:DH] = (key_sum[...] * scale).T.astype(narrow)
    dkv_ref[:, DH:] = value_sum[...].T.astype(narrow)
    drel_ref[...] = (rel_sum[...] * scale).T.astype(narrow)
    gu_ref[...] = grad_u * scale
    gv_ref[...] = grad_v * scale


def attend_back(probs, q_content, q_position, key_value, relative, d_attended):
    seg, width = q_content.shape
    keys, heads = key_value.shape[0], width // DH
    per_query = pl.BlockSpec((seg, DH), lambda h: (0, h))
    per_pair = pl.BlockSpec((keys, 2 * DH), lambda h: (0, h))
    per_key = pl.BlockSpec((keys, DH), lambda h: (0, h))
    per_head = pl.BlockSpec((1, DH), lambda h: (0, h))
    return pl.pallas_call(
        partial(attend_back_kernel, seg, keys),
        grid=(heads,),
        in_specs=[
            pl.BlockSpec((1, seg, keys), lambda h: (h, 0, 0)),
            per_query,
            per_query,
            per_pair,
            per_key,
            per_query,
        ],
        out_specs=[per_query, per_pair, per_key, per_head, per_head],
        out_shape=[
            jax.ShapeDtypeStruct((seg, width), narrow),
            jax.ShapeDtypeStruct((keys, 2 * width), narrow),
            jax.ShapeDtypeStruct((keys, width), narrow),
            jax.ShapeDtypeStruct((1, width), wide),
            jax.ShapeDtypeStruct((1, width), wide),
        ],
        scratch_shapes=[pltpu.VMEM((DH, keys), wide)] * 3,
        compiler_params=pltpu.CompilerParams(vmem_limit_bytes=60 << 20),
        cost_estimate=pl.CostEstimate(
            flops=12 * heads * seg * keys * DH, bytes_accessed=40 << 20, transcendentals=0
        ),
        name="attend_back",
    )(probs, q_content, q_position, key_value, relative, d_attended)


def swap(value, axis, bit=0):
    pairs = [(source, source ^ (1 << bit)) for source in range(lax.axis_size(axis))]
    return lax.ppermute(value, axis, pairs)


def side(axis, bit=0):
    return (lax.axis_index(axis) >> bit) & 1


def axis_bits():
    count = lax.axis_size("dp").bit_length() - 1
    core = [("dp", 0)]
    near = [("dp", bit) for bit in range(1, min(2, count))]
    rest = [("dp", bit) for bit in range(2, count)]
    return core, near, [("blk", 0)], rest


def scatter_sum(value, steps):
    for axis, bit in steps:
        half = value.shape[0] // 2
        which = side(axis, bit)
        theirs = lax.dynamic_slice_in_dim(value, (1 - which) * half, half, 0)
        ours = lax.dynamic_slice_in_dim(value, which * half, half, 0)
        value = (ours.astype(wide) + swap(theirs, axis, bit).astype(wide)).astype(narrow)
    return value


def in_order(which, ours, theirs, dim=0):
    return jnp.where(
        which == 0,
        jnp.concatenate([ours, theirs], dim),
        jnp.concatenate([theirs, ours], dim),
    )


def gather_back(value, steps):
    for axis, bit in reversed(steps):
        value = in_order(side(axis, bit), value, swap(value, axis, bit))
    return value


def sum_over_all(value):
    core, near, blk, rest = axis_bits()
    for axis, bit in core + near + blk + rest:
        value = value + swap(value, axis, bit)
    return value


def moments(values):
    centred = values - jnp.mean(values, -1, keepdims=True)
    inverse = lax.rsqrt(jnp.mean(centred * centred, -1, keepdims=True) + epsilon)
    return centred * inverse, inverse


def norm_back(grad, normal, inverse, gain):
    scaled = grad * gain
    inner = (
        scaled
        - jnp.mean(scaled, -1, keepdims=True)
        - normal * jnp.mean(scaled * normal, -1, keepdims=True)
    )
    return inner * inverse


def sinus_table():
    fine = 64
    frequency = 10000.0 ** (-2.0 * jnp.arange(D // 2, dtype=wide) / D)
    coarse_place = KEYS - 1 - fine * jnp.arange(KEYS // fine, dtype=wide)
    fine_place = jnp.arange(fine, dtype=wide)
    coarse = (coarse_place[:, None] * frequency[None, :])[:, None, :]
    little = (fine_place[:, None] * frequency[None, :])[None, :, :]
    sin_a, cos_a, sin_b, cos_b = lax.optimization_barrier(
        (jnp.sin(coarse), jnp.cos(coarse), jnp.sin(little), jnp.cos(little))
    )
    sine = sin_a * cos_b - cos_a * sin_b
    cosine = cos_a * cos_b + sin_a * sin_b
    return jnp.concatenate([sine, cosine], -1).astype(narrow).reshape(KEYS, D)


def matmul(left, right):
    return jnp.dot(left, right, preferred_element_type=wide)


def outer(left, right):
    return dot(left, right, 0, 0)


def back_through(grad, weight):
    return dot(grad, weight, 1, 1)


def on_device(
    segment,
    memory,
    comp_memory,
    mem_start,
    first_gain,
    first_bias,
    w_query,
    w_key,
    w_value,
    w_rel,
    u_bias,
    v_bias,
    w_out,
    second_gain,
    second_bias,
    w_up,
    b_up,
    w_down,
    b_down,
    w_comp,
    b_comp,
    cot_out,
    cot_comp,
):
    here = lax.axis_index("blk")
    blocks = lax.axis_size("blk")
    segment, memory, comp_memory = segment[0], memory[0], comp_memory[0]
    cot_out, cot_comp = cot_out[0], cot_comp[0]
    rows, width = segment.shape
    seg = rows * blocks
    past = KEYS - seg
    heads = H // blocks
    cols = heads * DH
    core, near, blk, rest = axis_bits()

    def my_cols(weight):
        return lax.dynamic_slice_in_dim(weight, here * cols, cols, 1)

    far = [swap(value, "blk") for value in (segment, memory, comp_memory)]

    windows = memory.reshape(memory.shape[0] // RATE, RATE * width)
    new_compressed = (matmul(windows, w_comp) + b_comp.astype(wide)).astype(narrow)
    grad_w_comp = outer(windows, cot_comp).astype(narrow)
    grad_b_comp = jnp.sum(cot_comp.astype(wide), 0)

    sinus = sinus_table()
    relative = matmul(sinus, my_cols(w_rel)).astype(narrow)
    w_query_mine = my_cols(w_query)
    w_kv = jnp.stack(
        [my_cols(w_key).reshape(width, heads, DH), my_cols(w_value).reshape(width, heads, DH)], 2
    ).reshape(width, 2 * cols)

    keys_in = jnp.concatenate(
        [
            in_order(here, comp_memory, far[2]),
            in_order(here, memory, far[1]),
            in_order(here, segment, far[0]),
        ],
        0,
    )
    normal, inverse = moments(keys_in.astype(wide))
    normed = (normal * first_gain.astype(wide) + first_bias.astype(wide)).astype(narrow)
    seg_normed = normed[past:]
    query_rows = matmul(seg_normed, w_query_mine)
    u_mine = lax.dynamic_slice_in_dim(u_bias, here * cols, cols, 0).astype(wide)
    v_mine = lax.dynamic_slice_in_dim(v_bias, here * cols, cols, 0).astype(wide)
    q_content = (query_rows + u_mine).astype(narrow)
    q_position = (query_rows + v_mine).astype(narrow)
    key_value = matmul(normed, w_kv).astype(narrow)
    attended_heads, probs = attend(mem_start, q_content, q_position, key_value, relative)

    ours = lax.dynamic_slice_in_dim(attended_heads, here * rows, rows, 0)
    theirs = lax.dynamic_slice_in_dim(attended_heads, (1 - here) * rows, rows, 0)
    attended = in_order(here, ours, swap(theirs, "blk"), 1)
    hidden = segment.astype(wide) + matmul(attended, w_out)
    normal_second, inverse_second = moments(hidden)
    second_normed = (
        normal_second * second_gain.astype(wide) + second_bias.astype(wide)
    ).astype(narrow)
    pre_gelu = matmul(second_normed, w_up) + b_up.astype(wide)
    gelu_wide, gelu_back = jax.vjp(partial(jax.nn.gelu, approximate=True), pre_gelu)
    gelu_out = gelu_wide.astype(narrow)
    layer_out = (hidden + matmul(gelu_out, w_down) + b_down.astype(wide)).astype(narrow)

    cot_wide = cot_out.astype(wide)
    d_pre = gelu_back(back_through(cot_out, w_down))[0].astype(narrow)
    d_second = back_through(d_pre, w_up)
    d_hidden = cot_wide + norm_back(
        d_second, normal_second, inverse_second, second_gain.astype(wide)
    )
    d_branch = d_hidden.astype(narrow)
    d_rows = back_through(d_branch, w_out).astype(narrow)
    ours = lax.dynamic_slice_in_dim(d_rows, here * cols, cols, 1)
    theirs = lax.dynamic_slice_in_dim(d_rows, (1 - here) * cols, cols, 1)
    d_attended = in_order(here, ours, swap(theirs, "blk"), 0)
    grad_b_down = jnp.sum(cot_wide, 0)
    grad_b_up = jnp.sum(d_pre.astype(wide), 0)
    grad_second_gain = jnp.sum(d_second * normal_second, 0)
    grad_second_bias = jnp.sum(d_second, 0)
    grad_w_down = outer(gelu_out, cot_out).astype(narrow)
    grad_w_up = outer(second_normed, d_pre).astype(narrow)
    grad_w_out = outer(attended, d_branch).astype(narrow)

    d_query, d_kv, d_relative, grad_u, grad_v = attend_back(
        probs, q_content, q_position, key_value, relative, d_attended
    )
    d_normed = back_through(d_kv[past:], w_kv) + back_through(d_query, w_query_mine)
    ours = lax.dynamic_slice_in_dim(d_normed, here * rows, rows, 0)
    theirs = lax.dynamic_slice_in_dim(d_normed, (1 - here) * rows, rows, 0).astype(narrow)
    d_normed_rows = ours + swap(theirs, "blk").astype(wide)
    normal_rows, inverse_rows = moments(segment.astype(wide))
    d_segment = (
        d_hidden + norm_back(d_normed_rows, normal_rows, inverse_rows, first_gain.astype(wide))
    ).astype(narrow)
    grad_w_kv = outer(normed, d_kv)
    grad_w_query = outer(seg_normed, d_query)
    grad_w_rel = outer(sinus, d_relative)

    def norm_sums(weight, grad, d_heads):
        column_sums = jnp.sum(d_heads.astype(wide), 0)
        weight = weight.astype(wide)
        by_bias = jnp.sum(weight * column_sums[None, :], 1)
        return jnp.sum(weight * grad, 1), by_bias

    kv_gain, kv_bias = norm_sums(w_kv, grad_w_kv, d_kv)
    q_gain, q_bias = norm_sums(w_query_mine, grad_w_query, d_query)
    grad_first_bias = kv_bias + q_bias
    grad_first_gain = (
        kv_gain + q_gain - first_bias.astype(wide) * grad_first_bias
    ) / first_gain.astype(wide)

    def spread(vector):
        return lax.dynamic_update_slice_in_dim(
            jnp.zeros((width,), wide), vector.reshape(cols), here * cols, 0
        )

    vectors = [
        grad_first_gain,
        grad_first_bias,
        spread(grad_u),
        spread(grad_v),
        grad_second_gain,
        grad_second_bias,
        grad_b_up,
        grad_b_down,
        grad_b_comp,
    ]
    total = sum_over_all(jnp.concatenate(vectors).reshape(-1, 128)).reshape(-1)
    split = []
    at = 0
    for vector in vectors:
        split.append(total[at : at + vector.shape[0]])
        at += vector.shape[0]

    x_first = core + near + blk + rest
    y_first = core + blk + rest + near
    z_first = core + rest + near + blk

    def reduced(value, steps):
        return gather_back(scatter_sum(value, steps), steps).astype(wide)

    full_comp = reduced(grad_w_comp, x_first)
    full_up = reduced(grad_w_up, x_first)
    full_down = reduced(grad_w_down, z_first)
    full_out = reduced(grad_w_out, y_first)

    def reduced_heads(value, steps):
        value = scatter_sum(value.astype(narrow), steps)
        value = jnp.stack([value, swap(value, "blk")], 0)
        value = jnp.where(here == 0, value, value[::-1])
        value = jnp.moveaxis(value, 0, 1)
        return gather_back(value, steps)

    kv = reduced_heads(grad_w_kv, core + near + rest).astype(wide)
    kv = kv.reshape(width, blocks, heads, 2, DH)
    full_key = kv[:, :, :, 0].reshape(width, width)
    full_value = kv[:, :, :, 1].reshape(width, width)
    pair = jnp.concatenate([grad_w_query, grad_w_rel], 1)
    pair = reduced_heads(pair, core + rest + near).astype(wide).reshape(width, blocks, 2, cols)
    full_query = pair[:, :, 0].reshape(width, width)
    full_rel = pair[:, :, 1].reshape(width, width)

    return (
        layer_out[None],
        d_segment[None],
        new_compressed[None],
        split[0],
        split[1],
        full_query,
        full_key,
        full_value,
        full_rel,
        split[2],
        split[3],
        full_out,
        split[4],
        split[5],
        full_up,
        split[6],
        full_down,
        split[7],
        full_comp,
        split[8],
    )


def solution(mesh):
    rows = P("dp", "blk", None)
    in_specs = (rows,) * 3 + (P("dp"),) + (P(),) * 17 + (rows,) * 2
    out_specs = (rows,) * 3 + (P(),) * 17
    return jax.shard_map(
        on_device, mesh=mesh, in_specs=in_specs, out_specs=out_specs, check_vma=False
    )
```

time: 3750 us -> 912 us (0.24)
  waiting for transfers between devices: 1620 us -> 316 us
  local copies, waits for them, and re-layouts: 1000 us -> 122 us
  starting transfers between devices: 374 us -> 58.8 us
  matrix products: 383 us -> 118 us
  blocking collectives: 148 us -> 0 us
  Pallas kernels: 0 us -> 91.2 us
    reduce_scatter x8 -> x0, waiting for transfers between devices: 1130 us -> none  [the longest x1 360 us: on_device(): lax.psum_scatter(grad_w_up, ('dp', 'blk'), scatter_dimension=0, tiled=True)]
    unnamed x364 -> x176, local copies, waits for them, and re-layouts: 398 us -> 20.8 us
    ppermute x4 -> x69, starting transfers between devices: 372 us -> 58.8 us  [swap(): return lax.ppermute(value, axis, pairs)]
    all_gather x8 -> x0, waiting for transfers between devices: 294 us -> none  [the longest x1 70.3 us: on_device(): lax.all_gather(shares[13].astype(jnp.bfloat16), ('dp', 'blk'), axis=0, ti...]
    reshape x23 -> x1, local copies, waits for them, and re-layouts: 284 us -> 4.44 us  [on_device(): w_kv = jnp.stack([my_cols(w_key).reshape(width, heads, DH), my_cols(w_val...]
    dot_general x68 -> x19, matrix products: 383 us -> 118 us  [the longest x12 75.8 us: dot(): lax.dot_general(left, right, (((left_dim,), (right_dim,)), ((), ())), pre...]
    pad x15 -> x0, local copies, waits for them, and re-layouts: 132 us -> none  [the longest x5 63.9 us: skew(): padded = jnp.pad(table_scores, [(0, 0)] * len(leading) + [(0, 0), (0, 1)])]
    ppermute x4 -> x69, waiting for transfers between devices: 191 us -> 316 us  [swap(): return lax.ppermute(value, axis, pairs)]
  transfers between devices with their start and end apart: 20 -> 69, of which waited for: 12 -> 33; matrix products, arithmetic and copies ran while one was open for 39% -> 46% of each run, Pallas kernels for 0% -> 10%
where the time goes in v1:
time: 912 us; the launch traced here: 902 us
  waiting for transfers between devices  316 us (35%)
  other arithmetic  192 us (21%)
  local copies, waits for them, and re-layouts  122 us (13%)
  matrix products  118 us (13%)
  Pallas kernels  91.2 us (10%)
  starting transfers between devices  58.8 us (6%)
    ppermute x69, waiting for transfers between devices, swap(): return lax.ppermute(value, axis, pairs)  316 us
    dot_general x12, matrix products, dot(): lax.dot_general(left, right, (((left_dim,), (right_dim,)), ((), ())), pre...  75.8 us
    select_n x32, other arithmetic, in_order(): jnp.where(which == 0, jnp.concatenate([ours, theirs], dim), jnp.concatena...  75.3 us
    ppermute x69, starting transfers between devices, swap(): return lax.ppermute(value, axis, pairs)  58.8 us
    pallas_call x1, Pallas kernels, attend_back(): pl.pallas_call(partial(attend_back_kernel, seg, keys), grid=(heads,), in_...  51.7 us
    dot_general x7, matrix products, matmul(): return jnp.dot(left, right, preferred_element_type=wide)  42.4 us
    pallas_call x1, Pallas kernels, attend(): pl.pallas_call(partial(attend_kernel, seg, keys), grid=(heads,), in_specs...  39.5 us
    convert_element_type x4, other arithmetic, reduced(): return gather_back(scatter_sum(value, steps), steps).astype(wide)  39.1 us
  transfers between devices with their start and end apart: 69, of which 33 were waited for; matrix products, arithmetic and copies ran while one was open for 46% of the time, Pallas kernels for 10%

profile of v1, /device:TPU:0, one launch (start us, length us, event | category | flops | bytes accessed | tf_op | source)
XLA Modules:
  0.0 902.1 jit_solution(2086324181496048573)
XLA Ops:
  74.8 7.0 convolution_convert_fusion.3.kv_ref
  84.2 39.5 %attend.1 = (bf16[960,512]{1,0:T(8,128)(2,1)}, bf16[4,960,2432]{2,1,0:T(8,128)(2,1)}) custom-call(s32[1]{0:T(128)S(6)} %copy.91.start_ref, bf16[960,512]{1,0:T(8,128)(2,1)} %get-tuple-element.59.qc_ref, bf16[960,512]{1,0:T(8,128)(2,1)} %get-tuple-element.58.qp_ref, bf16[2432,1024]{1,0:T(8,128)(2,1)} %convolution_convert_fusion.3.kv_ref, ...), custom_call_target="tpu_custom_call" | custom-call | flops 7172259840 | bytes 33554432 | tf_op jit(solution)/shard_map/attend/pallas_call | solution.py:84
  131.0 8.8 collective-permute-done.3
  149.7 15.2 %convert_reduce_fusion.2 = (f32[4096]{0:T(1024)S(1)}, bf16[480,4096]{1,0:T(8,128)(2,1)}) fusion(f32[480,4096]{1,0:T(8,128)} %fusion.64, f32[4096]{0:T(1024)S(1)} %convert_element_type.411, bf16[4096,1024]{1,0:T(8,128)(2,1)} %param.40, bf16[1,480,1024]{2,1,0:T(8,128)(2,1)S(1)} %copy-done.44), kind=kOutput, calls=%fused_computation.26 | convolution fusion | flops 4071747584 | bytes 21200896 | tf_op jit(solution)/shard_map/dot_general | solution.py:35
  164.9 6.8 multiply_reduce_fusion.2
  171.7 9.6 %convolution_convert_fusion.1 = bf16[1024,4096]{1,0:T(8,128)(2,1)} fusion(bf16[480,4096]{1,0:T(8,128)(2,1)} %get-tuple-element.85, f32[480,1024]{1,0:T(8,128)S(1)} %get-tuple-element.81, f32[1024]{0:T(1024)S(1)} %convert_element_type.409, f32[1024]{0:T(1024)S(1)} %convert_element_type.408, f32[480]{0:T(512)S(1)} %add_rsqrt_fusion.2, ...), kind=kOutput, calls=%fused_computation.29 | convolution fusion | flops 4033183744 | bytes 14298880 | tf_op jit(solution)/shard_map/dot_general | solution.py:35
  181.3 9.5 %convolution_convert_fusion = bf16[4096,1024]{1,0:T(8,128)(2,1)S(1)} fusion(bf16[1,480,1024]{2,1,0:T(8,128)(2,1)S(1)} %copy-done.44, f32[480,4096]{1,0:T(8,128)} %fusion.64, f32[4096]{0:T(1024)S(1)} %convert_element_type.411), kind=kOutput, calls=%fused_computation.28 | convolution fusion | flops 4050386944 | bytes 17252352 | tf_op jit(solution)/shard_map/dot_general | solution.py:35
  190.8 14.7 %fusion.39 = bf16[1,480,1024]{2,1,0:T(8,128)(2,1)} fusion(f32[480,1024]{1,0:T(8,128)S(1)} %get-tuple-element.81, bf16[4096,1024]{1,0:T(8,128)(2,1)} %param.40, f32[1024]{0:T(1024)S(1)} %convert_element_type.413, f32[480,4096]{1,0:T(8,128)} %fusion.64, f32[4096]{0:T(1024)S(1)} %convert_element_type.411), kind=kOutput, calls=%fused_computation.116 | convolution fusion | flops 4047667200 | bytes 19222528 | tf_op jit(solution)/shard_map/dot_general | solution.py:276
  222.8 51.7 %attend_back.1 = (bf16[960,512]{1,0:T(8,128)(2,1)}, bf16[2432,1024]{1,0:T(8,128)(2,1)}, bf16[2432,512]{1,0:T(8,128)(2,1)}, f32[1,512]{1,0:T(1,128)}, f32[1,512]{1,0:T(1,128)}) custom-call(bf16[4,960,2432]{2,1,0:T(8,128)(2,1)} %get-tuple-element.36.probs_ref, bf16[960,512]{1,0:T(8,128)(2,1)} %get-tuple-element.59.qc_ref, ...), custom_call_target="tpu_custom_call" | custom-call | flops 14344519680 | bytes 41943040 | tf_op jit(solution)/shard_map/attend_back/pallas_call | solution.py:168
  281.1 9.4 %fusion.67 = (bf16[1024,1024]{1,0:T(8,128)(2,1)}, f32[1024]{0:T(1024)S(1)}) fusion(bf16[1024,1024]{1,0:T(8,128)(2,1)S(1)} %copy-done.40, bf16[2432,1024]{1,0:T(8,128)(2,1)} %copy-done.21, bf16[2432,1024]{1,0:T(8,128)(2,1)S(1)} %copy-done.22), kind=kOutput, calls=%fused_computation.255 | convolution fusion | flops 5104466944 | bytes 14159872 | tf_op jit(solution)/shard_map/dot_general | solution.py:35
  307.7 20.7 %collective-permute-done.8 = f32[96,128]{1,0:T(8,128)S(1)} collective-permute-done((f32[96,128]{1,0:T(8,128)S(1)}, f32[96,128]{1,0:T(8,128)S(1)}, u32[]{:S(2)}, u32[]{:S(2)}) %collective-permute-start.8) | collective-permute-done | bytes 49184 | tf_op jit(solution)/shard_map/ppermute | solution.py:198
  347.5 7.8 collective-permute-done.30
  358.1 15.8 %collective-permute-done.31 = bf16[128,1024]{1,0:T(8,128)(2,1)S(1)} collective-permute-done((bf16[128,1024]{1,0:T(8,128)(2,1)S(1)}, bf16[128,1024]{1,0:T(8,128)(2,1)S(1)}, u32[]{:S(2)}, u32[]{:S(2)}) %collective-permute-start.31) | collective-permute-done | bytes 262176 | tf_op jit(solution)/shard_map/ppermute | solution.py:198
  389.8 32.9 %collective-permute-done.34 = bf16[32,1024]{1,0:T(8,128)(2,1)S(1)} collective-permute-done((bf16[32,1024]{1,0:T(8,128)(2,1)S(1)}, bf16[32,1024]{1,0:T(8,128)(2,1)S(1)}, u32[]{:S(2)}, u32[]{:S(2)}) %collective-permute-start.34) | collective-permute-done | bytes 65568 | tf_op jit(solution)/shard_map/ppermute | solution.py:198
  425.9 13.7 %collective-permute-done.35 = bf16[64,1024]{1,0:T(8,128)(2,1)S(1)} collective-permute-done((bf16[64,1024]{1,0:T(8,128)(2,1)S(1)}, bf16[64,1024]{1,0:T(8,128)(2,1)S(1)}, u32[]{:S(2)}, u32[]{:S(2)}) %collective-permute-start.35) | collective-permute-done | bytes 131104 | tf_op jit(solution)/shard_map/ppermute | solution.py:198
  441.8 7.0 collective-permute-done.22
  480.3 13.8 %collective-permute-done.25 = bf16[64,2,1024]{2,0,1:T(8,128)(2,1)S(1)} collective-permute-done((bf16[64,2,1024]{2,0,1:T(8,128)(2,1)S(1)}, bf16[64,2,1024]{2,0,1:T(8,128)(2,1)S(1)}, u32[]{:S(2)}, u32[]{:S(2)}) %collective-permute-start.25) | collective-permute-done | bytes 262176 | tf_op jit(solution)/shard_map/ppermute | solution.py:198
  565.1 30.2 %collective-permute-done.40 = bf16[256,4096]{1,0:T(8,128)(2,1)} collective-permute-done((bf16[256,4096]{1,0:T(8,128)(2,1)}, bf16[256,4096]{1,0:T(8,128)(2,1)}, u32[]{:S(2)}, u32[]{:S(2)}) %collective-permute-start.40) | collective-permute-done | bytes 2097184 | tf_op jit(solution)/shard_map/ppermute | solution.py:198
  624.5 17.2 %collective-permute-done.64 = bf16[96,1024]{1,0:T(8,128)(2,1)S(1)} collective-permute-done((bf16[96,1024]{1,0:T(8,128)(2,1)S(1)}, bf16[96,1024]{1,0:T(8,128)(2,1)S(1)}, u32[]{:S(2)}, u32[]{:S(2)}) %collective-permute-start.64) | collective-permute-done | bytes 196640 | tf_op jit(solution)/shard_map/ppermute | solution.py:198
  641.9 20.5 %collective-permute-done.51 = bf16[512,1024]{1,0:T(8,128)(2,1)S(1)} collective-permute-done((bf16[512,1024]{1,0:T(8,128)(2,1)S(1)}, bf16[512,1024]{1,0:T(8,128)(2,1)S(1)}, u32[]{:S(2)}, u32[]{:S(2)}) %collective-permute-start.51) | collective-permute-done | bytes 1048608 | tf_op jit(solution)/shard_map/ppermute | solution.py:198
  664.7 10.2 %collective-permute-done.52 = bf16[256,1024]{1,0:T(8,128)(2,1)S(1)} collective-permute-done((bf16[256,1024]{1,0:T(8,128)(2,1)S(1)}, bf16[256,1024]{1,0:T(8,128)(2,1)S(1)}, u32[]{:S(2)}, u32[]{:S(2)}) %collective-permute-start.52) | collective-permute-done | bytes 524320 | tf_op jit(solution)/shard_map/ppermute | solution.py:198
  696.9 7.2 collective-permute-done.54
  723.2 9.3 %fusion.16 = f32[1024,2,2,512]{3,2,0,1:T(2,128)} fusion(pred[]{:T(512)S(6)} %eq.13, bf16[512,2,2,512]{3,2,0,1:T(2,128)(2,1)S(1)} %copy-done.17, bf16[512,2,2,512]{3,2,0,1:T(2,128)(2,1)S(1)} %broadcast_select_fusion.3), kind=kLoop, calls=%fused_computation.40 | loop fusion | flops 8388608 | bytes 12582913 | tf_op jit(solution)/shard_map/convert_element_type | solution.py:466
  741.9 23.8 %collective-permute-done.56 = bf16[512,1024]{1,0:T(8,128)(2,1)} collective-permute-done((bf16[512,1024]{1,0:T(8,128)(2,1)}, bf16[512,1024]{1,0:T(8,128)(2,1)}, u32[]{:S(2)}, u32[]{:S(2)}) %collective-permute-start.56) | collective-permute-done | bytes 1048608 | tf_op jit(solution)/shard_map/ppermute | solution.py:198
  769.1 8.3 fusion.17
  782.1 13.0 %collective-permute-done.47 = bf16[256,4096]{1,0:T(8,128)(2,1)S(1)} collective-permute-done((bf16[256,4096]{1,0:T(8,128)(2,1)S(1)}, bf16[256,4096]{1,0:T(8,128)(2,1)S(1)}, u32[]{:S(2)}, u32[]{:S(2)}) %collective-permute-start.47) | collective-permute-done | bytes 2097184 | tf_op jit(solution)/shard_map/ppermute | solution.py:198
  798.4 16.3 %collective-permute-done.57 = bf16[1024,1024]{1,0:T(8,128)(2,1)S(1)} collective-permute-done((bf16[1024,1024]{1,0:T(8,128)(2,1)S(1)}, bf16[1024,1024]{1,0:T(8,128)(2,1)S(1)}, u32[]{:S(2)}, u32[]{:S(2)}) %collective-permute-start.57) | collective-permute-done | bytes 2097184 | tf_op jit(solution)/shard_map/ppermute | solution.py:198
  818.5 7.5 fusion.65
  832.2 7.4 fusion.66
  866.9 9.7 %fusion.15 = f32[3072,1024]{1,0:T(8,128)} fusion(bf16[1536,1024]{1,0:T(8,128)(2,1)} %collective-permute-done.68, bf16[1536,1024]{1,0:T(8,128)(2,1)} %maximum_select_fusion.5, pred[]{:T(512)S(6)} %eq.13), kind=kLoop, calls=%fused_computation.31 | loop fusion | flops 31457280 | bytes 18874368 | tf_op jit(solution)/shard_map/convert_element_type | solution.py:447
  876.6 13.0 %fusion.6 = f32[1024,4096]{1,0:T(8,128)} fusion(bf16[512,4096]{1,0:T(8,128)(2,1)} %collective-permute-done.48, bf16[512,4096]{1,0:T(8,128)(2,1)} %maximum_select_fusion.3, pred[]{:T(512)S(6)} %eq.13), kind=kLoop, calls=%fused_computation.12 | loop fusion | flops 41943040 | bytes 25165824 | tf_op jit(solution)/shard_map/convert_element_type | solution.py:447
  889.6 12.0 %fusion.7 = f32[4096,1024]{1,0:T(8,128)} fusion(bf16[2048,1024]{1,0:T(8,128)(2,1)} %collective-permute-done.58, bf16[2048,1024]{1,0:T(8,128)(2,1)} %maximum_select_fusion.4, pred[]{:T(512)S(6)} %eq.13), kind=kLoop, calls=%fused_computation.14 | loop fusion | flops 41943040 | bytes 25165824 | tf_op jit(solution)/shard_map/convert_element_type | solution.py:447
  (484 shorter events, 409.1 us)
Async XLA Ops:
  0.7 60.7 %collective-permute-start.2 = (bf16[480,1024]{1,0:T(8,128)(2,1)}, bf16[480,1024]{1,0:T(8,128)(2,1)}, u32[]{:S(2)}, u32[]{:S(2)}) collective-permute-start(bf16[480,1024]{1,0:T(8,128)(2,1)} %bitcast.129), channel_id=1, source_target_pairs={{0,1},{1,0},{2,3},{3,2},{4,5},{5,4},{6,7},{7,6},{8,9},{9,8},{10,11... | collective-permute-start | bytes 2949128 | tf_op jit(solution)/shard_map/ppermute | solution.py:198
  3.7 60.1 %collective-permute-start.1 = (bf16[480,1024]{1,0:T(8,128)(2,1)}, bf16[480,1024]{1,0:T(8,128)(2,1)}, u32[]{:S(2)}, u32[]{:S(2)}) collective-permute-start(bf16[480,1024]{1,0:T(8,128)(2,1)} %bitcast.145), channel_id=1, source_target_pairs={{0,1},{1,0},{2,3},{3,2},{4,5},{5,4},{6,7},{7,6},{8,9},{9,8},{10,11... | collective-permute-start | bytes 2949128 | tf_op jit(solution)/shard_map/ppermute | solution.py:198
  3.8 55.9 %collective-permute-start = (bf16[256,1024]{1,0:T(8,128)(2,1)}, bf16[256,1024]{1,0:T(8,128)(2,1)}, u32[]{:S(2)}, u32[]{:S(2)}) collective-permute-start(bf16[256,1024]{1,0:T(8,128)(2,1)} %bitcast.151), channel_id=1, source_target_pairs={{0,1},{1,0},{2,3},{3,2},{4,5},{5,4},{6,7},{7,6},{8,9},{9,8},{10,11... | collective-permute-start | bytes 1572872 | tf_op jit(solution)/shard_map/ppermute | solution.py:198
  17.0 358.5 %collective-permute-start.59 = (bf16[1536,1024]{1,0:T(8,128)(2,1)}, bf16[1536,1024]{1,0:T(8,128)(2,1)}, u32[]{:S(2)}, u32[]{:S(2)}) collective-permute-start(bf16[1536,1024]{1,0:T(8,128)(2,1)} %constant_dynamic-slice_fusion.4), channel_id=1, source_target_pairs={{0,2},{2,0},{4,6},{6,4},{8,10},{10,8},{12,14},{14,12},{16,18},{18,... | collective-permute-start | bytes 9437192 | tf_op jit(solution)/shard_map/ppermute | solution.py:198
  212.8 126.3 %collective-permute-start.29 = (bf16[512,1024]{1,0:T(8,128)(2,1)}, bf16[512,1024]{1,0:T(8,128)(2,1)}, u32[]{:S(2)}, u32[]{:S(2)}) collective-permute-start(bf16[512,1024]{1,0:T(8,128)(2,1)} %constant_dynamic-slice_fusion.19), channel_id=1, source_target_pairs={{0,2},{2,0},{4,6},{6,4},{8,10},{10,8},{12,14},{14,12},{16,18},{18,... | collective-permute-start | bytes 3145736 | tf_op jit(solution)/shard_map/ppermute | solution.py:198
  215.2 312.9 %collective-permute-start.39 = (bf16[512,4096]{1,0:T(8,128)(2,1)}, bf16[512,4096]{1,0:T(8,128)(2,1)}, u32[]{:S(2)}, u32[]{:S(2)}) collective-permute-start(bf16[512,4096]{1,0:T(8,128)(2,1)} %constant_dynamic-slice_fusion.14), channel_id=1, source_target_pairs={{0,2},{2,0},{4,6},{6,4},{8,10},{10,8},{12,14},{14,12},{16,18},{18,... | collective-permute-start | bytes 12582920 | tf_op jit(solution)/shard_map/ppermute | solution.py:198
  302.7 38.7 %collective-permute-start.5 = (bf16[480,1024]{1,0:T(8,128)(2,1)}, bf16[480,1024]{1,0:T(8,128)(2,1)}, u32[]{:S(2)}, u32[]{:S(2)}) collective-permute-start(bf16[480,1024]{1,0:T(8,128)(2,1)} %dynamic-slice_convert_fusion), channel_id=1, source_target_pairs={{0,1},{1,0},{2,3},{3,2},{4,5},{5,4},{6,7},{7,6},{8,9},{9,8},{10,11... | collective-permute-start | bytes 2949128 | tf_op jit(solution)/shard_map/ppermute | solution.py:198
  347.0 199.1 %collective-permute-start.49 = (bf16[2048,1024]{1,0:T(8,128)(2,1)}, bf16[2048,1024]{1,0:T(8,128)(2,1)}, u32[]{:S(2)}, u32[]{:S(2)}) collective-permute-start(bf16[2048,1024]{1,0:T(8,128)(2,1)} %constant_dynamic-slice_fusion.9), channel_id=1, source_target_pairs={{0,2},{2,0},{4,6},{6,4},{8,10},{10,8},{12,14},{14,12},{16,18},{18,... | collective-permute-start | bytes 12582920 | tf_op jit(solution)/shard_map/ppermute | solution.py:198
  355.3 33.6 %collective-permute-start.12 = (bf16[256,1024]{1,0:T(8,128)(2,1)S(1)}, bf16[256,1024]{1,0:T(8,128)(2,1)S(1)}, u32[]{:S(2)}, u32[]{:S(2)}) collective-permute-start(bf16[256,1024]{1,0:T(8,128)(2,1)S(1)} %constant_dynamic-slice_fusion.26), channel_id=1, source_target_pairs={{0,8},{2,10},{4,12},{6,14},{8,0},{10,2},{12,4},{14,6},{16,24},{18,... | collective-permute-start | bytes 1572872 | tf_op jit(solution)/shard_map/ppermute | solution.py:198
  373.9 51.5 %collective-permute-start.21 = (bf16[256,1024]{1,0:T(8,128)(2,1)S(1)}, bf16[256,1024]{1,0:T(8,128)(2,1)S(1)}, u32[]{:S(2)}, u32[]{:S(2)}) collective-permute-start(bf16[256,1024]{1,0:T(8,128)(2,1)S(1)} %constant_dynamic-slice_fusion.22), channel_id=1, source_target_pairs={{0,4},{2,6},{4,0},{6,2},{8,12},{10,14},{12,8},{14,10},{16,20},{18,... | collective-permute-start | bytes 1572872 | tf_op jit(solution)/shard_map/ppermute | solution.py:198
  387.4 114.8 %collective-permute-start.60 = (bf16[768,1024]{1,0:T(8,128)(2,1)}, bf16[768,1024]{1,0:T(8,128)(2,1)}, u32[]{:S(2)}, u32[]{:S(2)}) collective-permute-start(bf16[768,1024]{1,0:T(8,128)(2,1)} %constant_dynamic-slice_fusion.3), channel_id=1, source_target_pairs={{0,4},{2,6},{4,0},{6,2},{8,12},{10,14},{12,8},{14,10},{16,20},{18,... | collective-permute-start | bytes 4718600 | tf_op jit(solution)/shard_map/ppermute | solution.py:198
  388.9 33.7 %collective-permute-start.34 = (bf16[32,1024]{1,0:T(8,128)(2,1)S(1)}, bf16[32,1024]{1,0:T(8,128)(2,1)S(1)}, u32[]{:S(2)}, u32[]{:S(2)}) collective-permute-start(bf16[32,1024]{1,0:T(8,128)(2,1)S(1)} %add_convert_fusion.32), channel_id=1, source_target_pairs={{0,4},{2,6},{4,0},{6,2},{8,12},{10,14},{12,8},{14,10},{16,20},{18,... | collective-permute-start | bytes 196616 | tf_op jit(solution)/shard_map/ppermute | solution.py:198
  467.4 29.8 %collective-permute-start.37 = (bf16[256,1024]{1,0:T(8,128)(2,1)S(1)}, bf16[256,1024]{1,0:T(8,128)(2,1)S(1)}, u32[]{:S(2)}, u32[]{:S(2)}) collective-permute-start(bf16[256,1024]{1,0:T(8,128)(2,1)S(1)} %maximum_select_fusion.25), channel_id=1, source_target_pairs={{0,1},{1,0},{2,3},{3,2},{4,5},{5,4},{6,7},{7,6},{8,9},{9,8},{10,11... | collective-permute-start | bytes 1572872 | tf_op jit(solution)/shard_map/ppermute | solution.py:198
  502.2 37.4 %collective-permute-start.38 = (bf16[512,1024]{1,0:T(8,128)(2,1)S(1)}, bf16[512,1024]{1,0:T(8,128)(2,1)}, u32[]{:S(2)}, u32[]{:S(2)}) collective-permute-start(bf16[512,1024]{1,0:T(8,128)(2,1)S(1)} %maximum_select_fusion.17), channel_id=1, source_target_pairs={{0,2},{2,0},{4,6},{6,4},{8,10},{10,8},{12,14},{14,12},{16,18},{18,... | collective-permute-start | bytes 3145736 | tf_op jit(solution)/shard_map/ppermute | solution.py:198
  514.9 37.2 %collective-permute-start.18 = (bf16[256,2,1024]{2,0,1:T(8,128)(2,1)}, bf16[256,2,1024]{2,0,1:T(8,128)(2,1)}, u32[]{:S(2)}, u32[]{:S(2)}) collective-permute-start(bf16[256,2,1024]{2,0,1:T(8,128)(2,1)} %maximum_select_fusion.15), channel_id=1, source_target_pairs={{0,8},{2,10},{4,12},{6,14},{8,0},{10,2},{12,4},{14,6},{16,24},{18,... | collective-permute-start | bytes 3145736 | tf_op jit(solution)/shard_map/ppermute | solution.py:198
  528.0 29.1 %collective-permute-start.27 = (bf16[256,2,1024]{2,0,1:T(8,128)(2,1)S(1)}, bf16[256,2,1024]{2,0,1:T(8,128)(2,1)S(1)}, u32[]{:S(2)}, u32[]{:S(2)}) collective-permute-start(bf16[256,2,1024]{2,0,1:T(8,128)(2,1)S(1)} %maximum_select_fusion.16), channel_id=1, source_target_pairs={{0,4},{2,6},{4,0},{6,2},{8,12},{10,14},{12,8},{14,10},{16,20},{18,... | collective-permute-start | bytes 3145736 | tf_op jit(solution)/shard_map/ppermute | solution.py:198
  536.2 59.1 %collective-permute-start.40 = (bf16[256,4096]{1,0:T(8,128)(2,1)}, bf16[256,4096]{1,0:T(8,128)(2,1)}, u32[]{:S(2)}, u32[]{:S(2)}) collective-permute-start(bf16[256,4096]{1,0:T(8,128)(2,1)} %constant_dynamic-slice_fusion.13), channel_id=1, source_target_pairs={{0,4},{2,6},{4,0},{6,2},{8,12},{10,14},{12,8},{14,10},{16,20},{18,... | collective-permute-start | bytes 6291464 | tf_op jit(solution)/shard_map/ppermute | solution.py:198
  552.1 59.1 %collective-permute-start.50 = (bf16[1024,1024]{1,0:T(8,128)(2,1)}, bf16[1024,1024]{1,0:T(8,128)(2,1)}, u32[]{:S(2)}, u32[]{:S(2)}) collective-permute-start(bf16[1024,1024]{1,0:T(8,128)(2,1)} %constant_dynamic-slice_fusion.8), channel_id=1, source_target_pairs={{0,8},{2,10},{4,12},{6,14},{8,0},{10,2},{12,4},{14,6},{16,24},{18,... | collective-permute-start | bytes 6291464 | tf_op jit(solution)/shard_map/ppermute | solution.py:198
  557.1 151.8 %collective-permute-start.19 = (bf16[512,2,1024]{2,0,1:T(8,128)(2,1)}, bf16[512,2,1024]{2,0,1:T(8,128)(2,1)}, u32[]{:S(2)}, u32[]{:S(2)}) collective-permute-start(bf16[512,2,1024]{2,0,1:T(8,128)(2,1)} %maximum_select_fusion.6), channel_id=1, source_target_pairs={{0,2},{2,0},{4,6},{6,4},{8,10},{10,8},{12,14},{14,12},{16,18},{18,... | collective-permute-start | bytes 6291464 | tf_op jit(solution)/shard_map/ppermute | solution.py:198
  559.5 173.0 %collective-permute-start.28 = (bf16[512,2,1024]{2,0,1:T(8,128)(2,1)}, bf16[512,2,1024]{2,0,1:T(8,128)(2,1)}, u32[]{:S(2)}, u32[]{:S(2)}) collective-permute-start(bf16[512,2,1024]{2,0,1:T(8,128)(2,1)} %maximum_select_fusion.7), channel_id=1, source_target_pairs={{0,2},{2,0},{4,6},{6,4},{8,10},{10,8},{12,14},{14,12},{16,18},{18,... | collective-permute-start | bytes 6291464 | tf_op jit(solution)/shard_map/ppermute | solution.py:198
  560.1 48.4 %collective-permute-start.63 = (bf16[96,1024]{1,0:T(8,128)(2,1)S(1)}, bf16[96,1024]{1,0:T(8,128)(2,1)S(1)}, u32[]{:S(2)}, u32[]{:S(2)}) collective-permute-start(bf16[96,1024]{1,0:T(8,128)(2,1)S(1)} %constant_dynamic-slice_fusion), channel_id=1, source_target_pairs={{0,16},{2,18},{4,20},{6,22},{8,24},{10,26},{12,28},{14,30},{16,0},... | collective-permute-start | bytes 589832 | tf_op jit(solution)/shard_map/ppermute | solution.py:198
  608.6 33.1 %collective-permute-start.64 = (bf16[96,1024]{1,0:T(8,128)(2,1)S(1)}, bf16[96,1024]{1,0:T(8,128)(2,1)S(1)}, u32[]{:S(2)}, u32[]{:S(2)}) collective-permute-start(bf16[96,1024]{1,0:T(8,128)(2,1)S(1)} %add_convert_fusion.28), channel_id=1, source_target_pairs={{0,16},{2,18},{4,20},{6,22},{8,24},{10,26},{12,28},{14,30},{16,0},... | collective-permute-start | bytes 589832 | tf_op jit(solution)/shard_map/ppermute | solution.py:198
  614.5 48.0 %collective-permute-start.51 = (bf16[512,1024]{1,0:T(8,128)(2,1)S(1)}, bf16[512,1024]{1,0:T(8,128)(2,1)S(1)}, u32[]{:S(2)}, u32[]{:S(2)}) collective-permute-start(bf16[512,1024]{1,0:T(8,128)(2,1)S(1)} %constant_dynamic-slice_fusion.7), channel_id=1, source_target_pairs={{0,16},{2,18},{4,20},{6,22},{8,24},{10,26},{12,28},{14,30},{16,0},... | collective-permute-start | bytes 3145736 | tf_op jit(solution)/shard_map/ppermute | solution.py:198
  623.0 41.4 %collective-permute-start.42 = (bf16[64,4096]{1,0:T(8,128)(2,1)S(1)}, bf16[64,4096]{1,0:T(8,128)(2,1)S(1)}, u32[]{:S(2)}, u32[]{:S(2)}) collective-permute-start(bf16[64,4096]{1,0:T(8,128)(2,1)S(1)} %constant_dynamic-slice_fusion.11), channel_id=1, source_target_pairs={{0,8},{2,10},{4,12},{6,14},{8,0},{10,2},{12,4},{14,6},{16,24},{18,... | collective-permute-start | bytes 1572872 | tf_op jit(solution)/shard_map/ppermute | solution.py:198
  641.8 34.4 %collective-permute-start.65 = (bf16[192,1024]{1,0:T(8,128)(2,1)S(1)}, bf16[192,1024]{1,0:T(8,128)(2,1)S(1)}, u32[]{:S(2)}, u32[]{:S(2)}) collective-permute-start(bf16[192,1024]{1,0:T(8,128)(2,1)S(1)} %maximum_select_fusion.28), channel_id=1, source_target_pairs={{0,8},{2,10},{4,12},{6,14},{8,0},{10,2},{12,4},{14,6},{16,24},{18,... | collective-permute-start | bytes 1179656 | tf_op jit(solution)/shard_map/ppermute | solution.py:198
  707.4 70.0 %collective-permute-start.67 = (bf16[768,1024]{1,0:T(8,128)(2,1)}, bf16[768,1024]{1,0:T(8,128)(2,1)}, u32[]{:S(2)}, u32[]{:S(2)}) collective-permute-start(bf16[768,1024]{1,0:T(8,128)(2,1)} %maximum_select_fusion.13), channel_id=1, source_target_pairs={{0,4},{2,6},{4,0},{6,2},{8,12},{10,14},{12,8},{14,10},{16,20},{18,... | collective-permute-start | bytes 4718600 | tf_op jit(solution)/shard_map/ppermute | solution.py:198
  723.2 42.5 %collective-permute-start.56 = (bf16[512,1024]{1,0:T(8,128)(2,1)}, bf16[512,1024]{1,0:T(8,128)(2,1)}, u32[]{:S(2)}, u32[]{:S(2)}) collective-permute-start(bf16[512,1024]{1,0:T(8,128)(2,1)} %maximum_select_fusion.19), channel_id=1, source_target_pairs={{0,16},{2,18},{4,20},{6,22},{8,24},{10,26},{12,28},{14,30},{16,0},... | collective-permute-start | bytes 3145736 | tf_op jit(solution)/shard_map/ppermute | solution.py:198
  741.6 53.6 %collective-permute-start.47 = (bf16[256,4096]{1,0:T(8,128)(2,1)S(1)}, bf16[256,4096]{1,0:T(8,128)(2,1)S(1)}, u32[]{:S(2)}, u32[]{:S(2)}) collective-permute-start(bf16[256,4096]{1,0:T(8,128)(2,1)S(1)} %maximum_select_fusion.9), channel_id=1, source_target_pairs={{0,4},{2,6},{4,0},{6,2},{8,12},{10,14},{12,8},{14,10},{16,20},{18,... | collective-permute-start | bytes 6291464 | tf_op jit(solution)/shard_map/ppermute | solution.py:198
  769.0 45.7 %collective-permute-start.57 = (bf16[1024,1024]{1,0:T(8,128)(2,1)S(1)}, bf16[1024,1024]{1,0:T(8,128)(2,1)S(1)}, u32[]{:S(2)}, u32[]{:S(2)}) collective-permute-start(bf16[1024,1024]{1,0:T(8,128)(2,1)S(1)} %maximum_select_fusion.10), channel_id=1, source_target_pairs={{0,8},{2,10},{4,12},{6,14},{8,0},{10,2},{12,4},{14,6},{16,24},{18,... | collective-permute-start | bytes 6291464 | tf_op jit(solution)/shard_map/ppermute | solution.py:198
  782.1 84.8 %collective-permute-start.68 = (bf16[1536,1024]{1,0:T(8,128)(2,1)}, bf16[1536,1024]{1,0:T(8,128)(2,1)}, u32[]{:S(2)}, u32[]{:S(2)}) collective-permute-start(bf16[1536,1024]{1,0:T(8,128)(2,1)} %maximum_select_fusion.5), channel_id=1, source_target_pairs={{0,2},{2,0},{4,6},{6,4},{8,10},{10,8},{12,14},{14,12},{16,18},{18,... | collective-permute-start | bytes 9437192 | tf_op jit(solution)/shard_map/ppermute | solution.py:198
  798.4 78.1 %collective-permute-start.48 = (bf16[512,4096]{1,0:T(8,128)(2,1)}, bf16[512,4096]{1,0:T(8,128)(2,1)}, u32[]{:S(2)}, u32[]{:S(2)}) collective-permute-start(bf16[512,4096]{1,0:T(8,128)(2,1)} %maximum_select_fusion.3), channel_id=1, source_target_pairs={{0,2},{2,0},{4,6},{6,4},{8,10},{10,8},{12,14},{14,12},{16,18},{18,... | collective-permute-start | bytes 12582920 | tf_op jit(solution)/shard_map/ppermute | solution.py:198
  818.5 71.1 %collective-permute-start.58 = (bf16[2048,1024]{1,0:T(8,128)(2,1)}, bf16[2048,1024]{1,0:T(8,128)(2,1)}, u32[]{:S(2)}, u32[]{:S(2)}) collective-permute-start(bf16[2048,1024]{1,0:T(8,128)(2,1)} %maximum_select_fusion.4), channel_id=1, source_target_pairs={{0,2},{2,0},{4,6},{6,4},{8,10},{10,8},{12,14},{14,12},{16,18},{18,... | collective-permute-start | bytes 12582920 | tf_op jit(solution)/shard_map/ppermute | solution.py:198
  (118 other events, 1633.7 us)

commit v2 on v1

v2 whole, which is shorter than its diff:
```python
from functools import partial

import jax
import jax.numpy as jnp
from jax import lax
from jax.experimental import pallas as pl
from jax.experimental.pallas import tpu as pltpu
from jax.sharding import PartitionSpec as P

D = 1024
H = 8
DH = 128
FF = 4096
CMEM = 512
RATE = 3
KEYS = 2432

TILE = 192
FF_TILE = 512
epsilon = 1e-05
negative = -1e30
wide = jnp.float32
narrow = jnp.bfloat16
MIB = 1 << 20


def dot(left, right, left_dim, right_dim):
    return lax.dot_general(
        left, right, (((left_dim,), (right_dim,)), ((), ())), preferred_element_type=wide
    )


def shape(rows, cols, dtype=narrow):
    return jax.ShapeDtypeStruct((rows, cols), dtype)


def whole(rows, cols):
    return pl.BlockSpec((rows, cols), lambda *_: (0, 0))


class Order:
    def __init__(self):
        self.last = []

    def call(self, kernel, name, scalars, arrays, grid, in_specs, out_specs, out_shape, scratch=(), after=(), aliases=()):
        count = len(arrays)
        after = list(after) + self.last

        def body(scalar_ref, *refs):
            kernel(scalar_ref, *refs[:count], *refs[count + len(after) :])

        out = pl.pallas_call(
            body,
            grid_spec=pltpu.PrefetchScalarGridSpec(
                num_scalar_prefetch=1,
                grid=grid,
                in_specs=list(in_specs) + [pl.BlockSpec(memory_space=pl.ANY)] * len(after),
                out_specs=out_specs,
                scratch_shapes=list(scratch),
            ),
            out_shape=out_shape,
            input_output_aliases={1 + i: o for i, o in aliases},
            compiler_params=pltpu.CompilerParams(vmem_limit_bytes=60 * MIB),
            cost_estimate=pl.CostEstimate(
                flops=1000, bytes_accessed=1000, transcendentals=0
            ),
            name=name,
        )(jnp.stack([jnp.asarray(s, jnp.int32) for s in scalars]), *arrays, *after)
        self.last = [out[-1] if isinstance(out, (list, tuple)) else out]
        return out


def swap(value, axis, bit=0):
    pairs = [(source, source ^ (1 << bit)) for source in range(lax.axis_size(axis))]
    return lax.ppermute(value, axis, pairs)


def side(axis, bit=0):
    return (lax.axis_index(axis) >> bit) & 1


def place_of(steps):
    place = jnp.int32(0)
    for axis, bit in steps:
        place = place * 2 + side(axis, bit)
    return place


def add_split(order, chains, steps, name):
    in_specs, out_specs, out_shape, arrays = [], [], [], []
    for number, (kept, received, _) in enumerate(chains):
        rows, cols = kept.shape
        block = rows // 2 // steps
        theirs = pl.BlockSpec((block, cols), lambda i, ids, n=number: ((1 - ids[n]) * steps + i, 0))
        ours = pl.BlockSpec((block, cols), lambda i, ids, n=number: (ids[n] * steps + i, 0))
        arrays += [kept, received, kept, received]
        in_specs += [theirs, theirs, ours, ours]
        out_specs += [pl.BlockSpec((block, cols), lambda i, ids: (i, 0))] * 2
        out_shape += [shape(rows // 2, cols)] * 2

    def kernel(ids, *refs):
        ins, outs = refs[: 4 * len(chains)], refs[4 * len(chains) :]
        for number, out in enumerate(outs):
            a, b = ins[2 * number], ins[2 * number + 1]
            out[...] = (a[...].astype(wide) + b[...].astype(wide)).astype(narrow)

    out = order.call(kernel, name, [c[2] for c in chains], arrays, (steps,), in_specs, out_specs, out_shape)
    return [(out[2 * n], out[2 * n + 1]) for n in range(len(chains))]


def add(order, pairs, name):
    arrays = [value for pair in pairs for value in pair]

    def kernel(ids, *refs):
        for number, out in enumerate(refs[len(arrays) :]):
            a, b = refs[2 * number], refs[2 * number + 1]
            out[...] = (a[...].astype(wide) + b[...].astype(wide)).astype(narrow)

    return order.call(
        kernel,
        name,
        [0],
        arrays,
        (1,),
        [whole(*a.shape) for a in arrays],
        [whole(*a.shape) for a, _ in pairs],
        [shape(*a.shape) for a, _ in pairs],
    )


def gate(order, *values):
    place = pl.BlockSpec(memory_space=pl.ANY)
    out = order.call(
        lambda ids, *refs: None,
        "gate",
        [0],
        values,
        (1,),
        [place] * len(values),
        [place] * len(values),
        [jax.ShapeDtypeStruct(value.shape, value.dtype) for value in values],
        aliases=[(n, n) for n in range(len(values))],
    )
    return out[0] if len(values) == 1 else out


class Scatter:
    def __init__(self, order, name, chains):
        self.order, self.name = order, name
        self.steps = [steps for _, _, steps in chains]
        self.keep = [keep for _, keep, _ in chains]
        self.received = [swap(send, *steps[0]) for send, _, steps in chains]
        self.at = 0

    def step(self, blocks=1):
        self.at += 1
        if self.at == len(self.steps[0]):
            self.keep = add(self.order, list(zip(self.keep, self.received)), self.name)
            return self.keep
        chains = [
            (keep, received, side(*steps[self.at]))
            for keep, received, steps in zip(self.keep, self.received, self.steps)
        ]
        halves = add_split(self.order, chains, blocks, self.name)
        self.keep = [keep for _, keep in halves]
        self.received = [swap(send, *steps[self.at]) for (send, _), steps in zip(halves, self.steps)]


def join(order, pairs, name):
    arrays = [value for pair in pairs for value in pair]

    def kernel(ids, *refs):
        for number, out in enumerate(refs[len(arrays) :]):
            a, b = refs[2 * number], refs[2 * number + 1]
            rows = a.shape[0]
            out[0:rows, :] = a[...]
            out[rows:, :] = b[...]

    outs = [(2 * a.shape[0], a.shape[1]) for a, _ in pairs]
    return order.call(
        kernel,
        name,
        [0],
        arrays,
        (1,),
        [whole(*a.shape) for a in arrays],
        [whole(*out) for out in outs],
        [shape(*out) for out in outs],
    )


class Gather:
    def __init__(self, order, name, chains):
        self.order, self.name = order, name
        self.values = [value for value, _ in chains]
        self.steps = [list(steps) for _, steps in chains]
        self.send()

    def send(self):
        self.received = [swap(value, *steps.pop()) for value, steps in zip(self.values, self.steps)]

    def step(self):
        self.values = join(self.order, list(zip(self.values, self.received)), self.name)
        if self.steps[0]:
            self.send()


def two_pieces(value, first):
    return [value, swap(value, *first)]


def four_pieces(value, first, second):
    beside = swap(value, *second)
    return [value, beside, swap(value, *first), swap(beside, *first)]


def assemble(order, pieces, blocks, places, outs, out_block, index, inside, splits, name):
    rows, cols = pieces[0].shape
    chunk, part = rows // blocks, cols // splits
    count = len(pieces)

    def kernel(ids, *refs):
        ins, out_refs = refs[:count], refs[count:]
        piece = pl.program_id(0)

        def copy(ref, out):
            for r in range(blocks):
                row, col = inside(r ^ ids[1])
                out[pl.ds(pl.multiple_of(row, 8), chunk), pl.ds(pl.multiple_of(col, 128), part)] = ref[
                    r * chunk : (r + 1) * chunk, :
                ].astype(wide)

        for p, ref in enumerate(ins):
            for o, out in enumerate(out_refs):
                here = piece == p
                if len(out_refs) > 1:
                    here = here & ((p ^ ids[0]) == o)
                pl.when(here)(partial(copy, ref, out))

    def piece_spec(p):
        return pl.BlockSpec(
            (rows, part), lambda i, j, ids: (0, jnp.where(i == p, j, jnp.where(i < p, 0, splits - 1)))
        )

    return order.call(
        kernel,
        name,
        places,
        pieces,
        (count, splits),
        [piece_spec(p) for p in range(count)],
        [pl.BlockSpec(out_block, lambda i, j, ids: index(i ^ ids[0], j))] * len(outs),
        [shape(*out, wide) for out in outs],
    )


def widen(order, value, name):
    rows, cols = value.shape
    steps = 4

    def kernel(ids, ref, out):
        out[...] = ref[...].astype(wide)

    at = pl.BlockSpec((rows // steps, cols), lambda i, ids: (i, 0))
    return order.call(kernel, name, [0], [value], (steps,), [at], at, shape(rows, cols, wide))


def widen_heads(order, gathered, chunk, extra, width, cols, name):
    arrays = 4
    rows = gathered.shape[0] // arrays
    count = rows // (chunk + extra)

    def kernel(ids, ref, *outs):
        def copy(out):
            for r in range(count):
                at = r * (chunk + extra)
                row, col = r // 2 * chunk, r % 2 * cols
                out[row : row + chunk, col : col + cols] = ref[at : at + chunk, :].astype(wide)

        for number, out in enumerate(outs):
            pl.when(pl.program_id(0) == number)(partial(copy, out))

    return order.call(
        kernel,
        name,
        [0],
        [gathered],
        (arrays,),
        [pl.BlockSpec((rows, cols), lambda i, ids: (i, 0))],
        [whole(width, width)] * arrays,
        [shape(width, width, wide)] * arrays,
    )


def project_kernel(count, lengths, ids, *refs):
    parts, (gain, bias, wq, wk, wv), outs = refs[:count], refs[count : count + 5], refs[count + 5 :]
    if count < len(lengths):
        firsts = [sum(lengths[:n]) for n in range(len(lengths))]
        parts = [parts[0].at[first : first + length, :] for first, length in zip(firsts, lengths)]
        count = len(lengths)
    for number, part in enumerate(parts):
        normed, k, v = outs[3 * number : 3 * number + 3]
        values = part[...].astype(wide)
        centred = values - jnp.mean(values, -1, keepdims=True)
        inverse = lax.rsqrt(jnp.mean(centred * centred, -1, keepdims=True) + epsilon)
        low = (centred * inverse * gain[...].astype(wide) + bias[...].astype(wide)).astype(narrow)
        normed[...] = low
        k[...] = dot(low, wk[...], 1, 0).astype(narrow)
        v[...] = dot(low, wv[...], 1, 0).astype(narrow)
        if number == 0 and len(outs) > 3 * count:
            outs[-1][...] = dot(low, wq[...], 1, 0)


def project(order, here, parts, lengths, query, weights, cols, after=()):
    gain, bias, wq, wk, wv = weights
    width = wq.shape[0]
    weight = pl.BlockSpec((width, cols), lambda i, ids: (0, ids[0]))
    unused = whole(16, 128)
    out_shape = [s for n in lengths for s in (shape(n, width), shape(n, cols), shape(n, cols))]
    if query:
        out_shape.append(shape(lengths[0], cols, wide))
    out = order.call(
        partial(project_kernel, len(parts), lengths),
        "project",
        [here],
        list(parts) + [gain[None], bias[None], wq, wk, wv],
        (1,),
        [whole(*p.shape) for p in parts] + [whole(1, width)] * 2 + [weight if query else unused, weight, weight],
        [whole(*o.shape) for o in out_shape],
        out_shape,
        after=after,
    )
    triples = [tuple(out[3 * n : 3 * n + 3]) for n in range(len(lengths))]
    return triples + ([out[-1]] if query else [])


def tiles_of(seg, keys, tile):
    tiles = []
    for first in range(0, seg, tile):
        used = keys - seg + first + tile
        cols = -(-used // 128) * 128
        tiles.append((first, cols, keys - cols, cols - used))
    return tiles


def unskew(grid, tile, cols, pad):
    parts = []
    for group in range(tile // 8):
        shift = tile - 1 + pad - 8 * group - 7
        rows = grid[8 * group : 8 * group + 8]
        parts.append(pltpu.roll(rows, shift, 1) if shift else rows)
    moved = jnp.concatenate(parts, 0)
    left = 7 - (lax.broadcasted_iota(jnp.int32, (tile, cols), 0) & 7)
    for bit in range(3):
        moved = jnp.where((left & (1 << bit)) != 0, pltpu.roll(moved, 1 << bit, 1), moved)
    return moved


def spans(parts, here):
    out = []
    at = 0
    for length in parts:
        own = pl.multiple_of(2 * at + here * length, 16)
        far = pl.multiple_of(2 * at + (1 - here) * length, 16)
        out.append((pl.ds(at, length), pl.ds(own, length), pl.ds(far, length)))
        at += length
    return out


def place_parts(parts, here, own, far, out):
    for (_, own_rows, far_rows), own_part, far_part in zip(spans(parts, here), own, far):
        out[own_rows, :] = own_part[...]
        out[far_rows, :] = far_part[...]


def place_queries(parts, here, q_own, q_far, u, v, qc, qp):
    ((_, own_rows, far_rows),) = spans(parts[2:], here)
    for ref, rows in ((q_own, own_rows), (q_far, far_rows)):
        qc[rows, :] = (ref[...] + u[...].astype(wide)).astype(narrow)
        qp[rows, :] = (ref[...] + v[...].astype(wide)).astype(narrow)


def attend_kernel(parts, ids, q_own, q_far, u, v, *refs):
    k_own, k_far, v_own, v_far = refs[0:3], refs[3:6], refs[6:9], refs[9:12]
    rel, out_own, out_far, probs_ref, qc, qp, ks, vs, outs = refs[12:]
    here, start = ids[0], ids[1]
    place_queries(parts, here, q_own, q_far, u, v, qc, qp)
    place_parts(parts, here, k_own, k_far, ks)
    place_parts(parts, here, v_own, v_far, vs)
    seg, keys = qc.shape[0], ks.shape[0]
    past = keys - seg
    factor = DH**-0.5 * 1.4426950408889634
    for first, cols, base, pad in tiles_of(seg, keys, TILE):
        rows = pl.ds(first, TILE)
        content = dot(qc[rows, :], ks[0:cols, :], 1, 1)
        table = dot(qp[rows, :], rel[base : base + cols, :], 1, 1)
        table = pltpu.roll(table, cols - (TILE - 1 + pad), 1, stride=1, stride_axis=0)
        scores = content + table
        left = scores[:, :CMEM]
        lane = lax.broadcasted_iota(jnp.int32, left.shape, 1)
        left = jnp.where(lane >= start, left, negative)
        edge = (past + first) // 128 * 128
        right = scores[:, edge:]
        lane = lax.broadcasted_iota(jnp.int32, right.shape, 1) + (edge - past - first)
        row = lax.broadcasted_iota(jnp.int32, right.shape, 0)
        right = jnp.where(lane <= row, right, negative)
        scores = jnp.concatenate([left, scores[:, CMEM:edge], right], 1)
        largest = jnp.max(scores, -1, keepdims=True)
        probs = jnp.exp2(scores * factor - largest * factor)
        probs = (probs * (1.0 / jnp.sum(probs, -1, keepdims=True))).astype(narrow)
        probs_ref[0, rows, 0:cols] = probs
        outs[rows, :] = dot(probs, vs[0:cols, :], 1, 0).astype(narrow)
    ((_, own_rows, far_rows),) = spans(parts[2:], here)
    out_own[...] = outs[own_rows, :]
    out_far[...] = outs[far_rows, :]


def part_specs(parts, first):
    return [pl.BlockSpec((length, DH), lambda h, ids: (0, h + first)) for length in parts]


def attend(order, here, start, parts, inputs, first, heads):
    q_own, q_far, u, v, k_own, k_far, v_own, v_far, rel = inputs
    rows, keys = parts[2], rel.shape[0]
    query = pl.BlockSpec((rows, DH), lambda h, ids: (0, h + first))
    bias = pl.BlockSpec((1, DH), lambda h, ids: (0, h + first + ids[0] * (H // 2)))
    out = pl.BlockSpec((rows, DH), lambda h, ids: (0, h))
    seg = 2 * rows
    return order.call(
        partial(attend_kernel, parts),
        "attend",
        [here, start],
        [q_own, q_far, u[None], v[None], *k_own, *k_far, *v_own, *v_far, rel],
        (heads,),
        [query, query, bias, bias]
        + part_specs(parts, first) * 4
        + [pl.BlockSpec((keys, DH), lambda h, ids: (0, h + first))],
        [out, out, pl.BlockSpec((1, seg, keys), lambda h, ids: (h, 0, 0))],
        [shape(rows, heads * DH)] * 2 + [jax.ShapeDtypeStruct((heads, seg, keys), narrow)],
        [pltpu.VMEM((seg, DH), narrow)] * 2
        + [pltpu.VMEM((keys, DH), narrow)] * 2
        + [pltpu.VMEM((seg, DH), narrow)],
    )


def attend_back_kernel(parts, ids, probs_ref, q_own, q_far, u, v, *refs):
    k_own, k_far, v_own, v_far = refs[0:3], refs[3:6], refs[6:9], refs[9:12]
    rel, da_own, da_far, dq_own, dq_far, dk_ref, dv_ref, drel_ref, gu_ref, gv_ref = refs[12:22]
    qc_ref, qp_ref, ks, vs, das, dqs, stage, key_sum, value_sum, rel_sum = refs[22:]
    here = ids[0]
    place_queries(parts, here, q_own, q_far, u, v, qc_ref, qp_ref)
    place_parts(parts, here, k_own, k_far, ks)
    place_parts(parts, here, v_own, v_far, vs)
    ((_, own_rows, far_rows),) = spans(parts[2:], here)
    das[own_rows, :] = da_own[...]
    das[far_rows, :] = da_far[...]
    seg, keys = qc_ref.shape[0], ks.shape[0]
    scale = DH**-0.5

    grad_u = jnp.zeros((1, DH), wide)
    grad_v = jnp.zeros((1, DH), wide)
    for step, (first, cols, base, pad) in enumerate(tiles_of(seg, keys, TILE)[::-1]):
        rows = pl.ds(first, TILE)
        probs = probs_ref[0, rows, 0:cols]
        probs_wide = probs.astype(wide)
        d_out, qc, qp = das[rows, :], qc_ref[rows, :], qp_ref[rows, :]
        d_probs = dot(d_out, vs[0:cols, :], 1, 1)
        weighted = probs_wide * d_probs
        d_scores = weighted - probs_wide * jnp.sum(weighted, -1, keepdims=True)
        d_low = d_scores.astype(narrow)
        d_table = unskew(d_scores, TILE, cols, pad).astype(narrow)
        d_content = dot(d_low, ks[0:cols, :], 1, 0)
        d_position = dot(d_table, rel[base : base + cols, :], 1, 0)
        grad_u += jnp.sum(d_content, 0, keepdims=True)
        grad_v += jnp.sum(d_position, 0, keepdims=True)
        dqs[rows, :] = ((d_content + d_position) * scale).astype(narrow)
        d_key = dot(qc, d_low, 0, 0)
        d_value = dot(d_out, probs, 0, 0)
        d_rel = dot(qp, d_table, 0, 0)
        if step == 0:
            key_sum[...] = d_key
            value_sum[...] = d_value
            rel_sum[...] = d_rel
        else:
            key_sum[:, 0:cols] += d_key
            value_sum[:, 0:cols] += d_value
            rel_sum[:, base : base + cols] += d_rel
    gu_ref[...] = grad_u * scale
    gv_ref[...] = grad_v * scale
    drel_ref[...] = (rel_sum[...] * scale).T.astype(narrow)
    dq_own[...] = dqs[own_rows, :]
    dq_far[...] = dqs[far_rows, :]
    block = sum(parts)
    for total, factor, out in ((key_sum, scale, dk_ref), (value_sum, 1.0, dv_ref)):
        stage[...] = (total[...] * factor).T.astype(narrow)
        for rows, mine, theirs in spans(parts, here):
            out[rows, :] = stage[mine, :]
            out[pl.ds(block + rows.start, rows.size), :] = stage[theirs, :]


def attend_back(order, here, parts, probs, inputs, da_own, da_far, first, heads):
    q_own, q_far, u, v, k_own, k_far, v_own, v_far, rel = inputs
    rows, keys = parts[2], rel.shape[0]
    seg = 2 * rows
    query = pl.BlockSpec((rows, DH), lambda h, ids: (0, h + first))
    bias = pl.BlockSpec((1, DH), lambda h, ids: (0, h + first + ids[0] * (H // 2)))
    key = pl.BlockSpec((keys, DH), lambda h, ids: (0, h + first))
    query_out = pl.BlockSpec((rows, DH), lambda h, ids: (0, h))
    key_out = pl.BlockSpec((keys, DH), lambda h, ids: (0, h))
    per_head = pl.BlockSpec((1, DH), lambda h, ids: (0, h))
    small, large = pltpu.VMEM((seg, DH), narrow), pltpu.VMEM((keys, DH), narrow)
    return order.call(
        partial(attend_back_kernel, parts),
        "attend_back",
        [here],
        [probs, q_own, q_far, u[None], v[None], *k_own, *k_far, *v_own, *v_far, rel, da_own, da_far],
        (heads,),
        [pl.BlockSpec((1, seg, keys), lambda h, ids: (h, 0, 0)), query, query, bias, bias]
        + part_specs(parts, first) * 4
        + [key, query, query],
        [query_out, query_out, key_out, key_out, key_out, per_head, per_head],
        [shape(rows, heads * DH)] * 2
        + [shape(keys, heads * DH)] * 3
        + [shape(1, heads * DH, wide)] * 2,
        [small, small, large, large, small, small, large] + [pltpu.VMEM((DH, keys), wide)] * 3,
    )


def middle_kernel(own_pieces, far_pieces, ids, *refs):
    mine, refs = refs[:own_pieces], refs[own_pieces:]
    received, refs = refs[:far_pieces], refs[far_pieces:]
    segment, cot, w_out, gain, bias, w_up, b_up, w_down, b_down = refs[:9]
    (layer_out, packed, att_keep, gelu_theirs, gelu_mine, d_theirs, d_mine, d_hidden, da_mine, da_theirs, g_up, g_gain, g_bias, g_down,
     normal, inverse, layer, back) = refs[9:]
    normed, d_branch, att_send = packed.at[:, 0:D], packed.at[:, D : 2 * D], packed.at[:, 2 * D :]
    step = pl.program_id(0)
    steps = pl.num_programs(0)
    here = ids[0]
    half = D // 2

    @pl.when(step == 0)
    def _():
        own = jnp.concatenate([ref[...] for ref in mine], 1)
        far = jnp.concatenate([ref[...] for ref in received], 1)
        own_rows = pl.ds(pl.multiple_of(here * half, 128), half)
        far_rows = pl.ds(pl.multiple_of((1 - here) * half, 128), half)
        hidden = segment[...].astype(wide) + dot(own, w_out[own_rows, :], 1, 0) + dot(far, w_out[far_rows, :], 1, 0)
        same = here == ids[1]
        att_keep[...] = jnp.where(same, own, far)
        att_send[...] = jnp.where(same, far, own)
        centred = hidden - jnp.mean(hidden, -1, keepdims=True)
        scale = lax.rsqrt(jnp.mean(centred * centred, -1, keepdims=True) + epsilon)
        inverse[...] = scale
        normal[...] = centred * scale
        normed[...] = (normal[...] * gain[...].astype(wide) + bias[...].astype(wide)).astype(narrow)
        layer[...] = hidden + b_down[...].astype(wide)
        back[...] = jnp.zeros_like(back)

    t = dot(normed[...], w_up[...], 1, 0) + b_up[...].astype(wide)
    d_gelu = dot(cot[...], w_down[...], 1, 1)
    square = t * t
    slope = 0.7978845608028654
    bent = jnp.tanh(slope * t * (1.0 + 0.044715 * square))
    rise = 0.5 * (1.0 + bent)
    gelu = (t * rise).astype(narrow)
    change = rise + (0.5 * slope) * t * (1.0 - bent * bent) * (1.0 + (3 * 0.044715) * square)
    d_pre = (d_gelu * change).astype(narrow)
    layer[...] += dot(gelu, w_down[...], 1, 0)
    back[...] += dot(d_pre, w_up[...], 1, 1)
    g_up[...] = jnp.sum(d_pre.astype(wide), 0, keepdims=True)

    @pl.when(step < steps // 2)
    def _():
        gelu_theirs[...] = gelu
        d_theirs[...] = d_pre

    @pl.when(step >= steps // 2)
    def _():
        gelu_mine[...] = gelu
        d_mine[...] = d_pre

    @pl.when(step == steps - 1)
    def _():
        layer_out[...] = layer[...].astype(narrow)
        e, n = back[...], normal[...]
        cot_wide = cot[...].astype(wide)
        en = e * n
        g_gain[...] = jnp.sum(en, 0, keepdims=True)
        g_bias[...] = jnp.sum(e, 0, keepdims=True)
        g_down[...] = jnp.sum(cot_wide, 0, keepdims=True)
        by = gain[...].astype(wide)
        inner = e * by - jnp.mean(e * by, -1, keepdims=True) - n * jnp.mean(en * by, -1, keepdims=True)
        d_wide = cot_wide + inner * inverse[...]
        d_hidden[...] = d_wide
        low = d_wide.astype(narrow)
        d_branch[...] = low
        own_rows = pl.ds(pl.multiple_of(here * half, 128), half)
        far_rows = pl.ds(pl.multiple_of((1 - here) * half, 128), half)
        da_theirs[...] = dot(low, w_out[far_rows, :], 1, 1).astype(narrow)
        da_mine[...] = dot(low, w_out[own_rows, :], 1, 1).astype(narrow)


def middle(order, here, core, mine, received, segment, cot, w_out, gain, bias, w_up, b_up, w_down, b_down):
    rows, width = segment.shape
    units = w_up.shape[1]
    steps = units // FF_TILE
    half = steps // 2

    def tile(j, ids):
        return jnp.where(j < half, (1 - ids[1]) * half + j, ids[1] * half + j - half)

    up = pl.BlockSpec((width, FF_TILE), lambda j, ids: (0, tile(j, ids)))
    down = pl.BlockSpec((FF_TILE, width), lambda j, ids: (tile(j, ids), 0))
    unit = pl.BlockSpec((1, FF_TILE), lambda j, ids: (0, tile(j, ids)))
    theirs = pl.BlockSpec((rows, FF_TILE), lambda j, ids: (0, jnp.minimum(j, half - 1)))
    ours = pl.BlockSpec((rows, FF_TILE), lambda j, ids: (0, jnp.maximum(j - half, 0)))
    row, vector = whole(rows, width), whole(1, width)
    heads = whole(rows, width // 2)
    return order.call(
        partial(middle_kernel, len(mine), len(received)),
        "middle",
        [here, core],
        list(mine) + list(received) + [segment, cot, w_out, gain[None], bias[None], w_up, b_up[None], w_down, b_down[None]],
        (steps,),
        [whole(*a.shape) for a in list(mine) + list(received)]
        + [row, row, whole(width, width), vector, vector, up, unit, down, vector],
        [row, whole(rows, 5 * width // 2), heads, theirs, ours, theirs, ours, row, heads, heads, unit]
        + [vector] * 3,
        [shape(rows, width), shape(rows, 5 * width // 2), shape(rows, width // 2)]
        + [shape(rows, units // 2)] * 4
        + [shape(rows, width, wide)]
        + [shape(rows, width // 2)] * 2
        + [shape(1, units, wide)]
        + [shape(1, width, wide)] * 3,
        [pltpu.VMEM((rows, width), wide), pltpu.VMEM((rows, 1), wide)] + [pltpu.VMEM((rows, width), wide)] * 2,
    )


def outer_pair(order, l_own, l_far, r_own, r_far, which, name, after=()):
    count, units, cols = l_own[0].shape[0], l_own[2], r_own[2]
    rows = units // 2
    block = 256 if rows % 256 == 0 else rows
    steps = rows // block

    def kernel(ids, lo, lf, ro, rf, out):
        out[...] = (dot(lo[...], ro[...], 0, 0) + dot(lf[...], rf[...], 0, 0)).astype(narrow)

    def left(first):
        return pl.BlockSpec((count, block), lambda i, ids: (0, first // block + ids[0] * steps + i))

    def right(first):
        return pl.BlockSpec((count, cols), lambda i, ids: (0, first // cols))

    return order.call(
        kernel,
        name,
        [which],
        [l_own[0], l_far[0], r_own[0], r_far[0]],
        (steps,),
        [left(l_own[1]), left(l_far[1]), right(r_own[1]), right(r_far[1])],
        pl.BlockSpec((block, cols), lambda i, ids: (i, 0)),
        shape(rows, cols),
        after=after,
    )


def segment_back_kernel(count, block, ids, *refs):
    dq_own, dq_far, dk, dv = (refs[n * count : (n + 1) * count] for n in range(4))
    wq, wk, wv, own, far = refs[4 * count :]
    rows = dq_own[0].shape[0]

    def through(dq, last):
        at = pl.ds(last - rows, rows)
        total = dot(jnp.concatenate([d[...] for d in dq], 1), wq[...], 1, 1)
        total += dot(jnp.concatenate([d[at, :] for d in dk], 1), wk[...], 1, 1)
        return total + dot(jnp.concatenate([d[at, :] for d in dv], 1), wv[...], 1, 1)

    far[...] = through(dq_far, 2 * block).astype(narrow)
    own[...] = through(dq_own, block)


def segment_back(order, here, dq_own, dq_far, dk, dv, wq, wk, wv, block):
    rows, width, cols = dq_own[0].shape[0], wq.shape[0], wq.shape[1] // 2
    weight = pl.BlockSpec((width, cols), lambda i, ids: (0, ids[0]))
    arrays = [*dq_own, *dq_far, *dk, *dv]
    return order.call(
        partial(segment_back_kernel, len(dk), block),
        "segment_back",
        [here],
        arrays + [wq, wk, wv],
        (1,),
        [whole(*a.shape) for a in arrays] + [weight] * 3,
        [whole(rows, width)] * 2,
        [shape(rows, width, wide), shape(rows, width)],
    )


def grad_heads_kernel(parts, count, chunk, extra, ids, *refs):
    normed, refs = refs[:6], refs[6:]
    sinus, refs = refs[0], refs[1:]
    dq_own, dq_far, dk, dv, drel = (refs[n * count : (n + 1) * count] for n in range(5))
    wq, wk, wv, out, by_gain, by_bias = refs[5 * count :]
    param = pl.program_id(0)

    @pl.when(param == 0)
    def _():
        by_gain[...] = jnp.zeros_like(by_gain)
        by_bias[...] = jnp.zeros_like(by_bias)

    def store(grad):
        for n in range(grad.shape[0] // chunk):
            at = n * (chunk + extra)
            out[at : at + chunk, :] = grad[n * chunk : (n + 1) * chunk, :].astype(narrow)
            out[at + chunk : at + chunk + extra, :] = jnp.zeros((extra, grad.shape[1]), narrow)

    def sums(weight, grad, d_heads):
        weight = weight[...].astype(wide)
        column = sum(jnp.sum(d.astype(wide), 0, keepdims=True) for d in d_heads)
        by_gain[...] += jnp.sum(weight * grad, 1, keepdims=True)
        by_bias[...] += jnp.sum(weight * column, 1, keepdims=True)

    def beside(refs, rows=slice(None)):
        return jnp.concatenate([ref[rows, :] for ref in refs], 1)

    @pl.when(param == 0)
    def _():
        own, far = beside(dq_own), beside(dq_far)
        grad = (dot(own, normed[2][...], 0, 0) + dot(far, normed[5][...], 0, 0)).T
        store(grad)
        sums(wq, grad, (own, far))

    for number, weight, d_heads in ((1, wk, dk), (2, wv, dv)):

        @pl.when(param == number)
        def _(weight=weight, d_heads=d_heads):
            grad = 0.0
            at = 0
            for part in normed:
                rows = part.shape[0]
                grad += dot(beside(d_heads, slice(at, at + rows)), part[...], 0, 0)
                at += rows
            grad = grad.T
            store(grad)
            sums(weight, grad, (beside(d_heads),))

    @pl.when(param == 3)
    def _():
        store(dot(beside(drel), sinus[...], 0, 0).T)


def grad_heads(order, here, parts, normed, sinus, dq_own, dq_far, dk, dv, drel, wq, wk, wv, chunk, extra):
    width, cols = wq.shape[0], wq.shape[1] // 2
    weight = pl.BlockSpec((width, cols), lambda i, ids: (0, ids[0]))
    arrays = [*normed, sinus, *dq_own, *dq_far, *dk, *dv, *drel]
    rows = width // chunk * (chunk + extra)
    return order.call(
        partial(grad_heads_kernel, parts, len(dk), chunk, extra),
        "grad_heads",
        [here],
        arrays + [wq, wk, wv],
        (4,),
        [whole(*a.shape) for a in arrays] + [weight] * 3,
        [pl.BlockSpec((rows, cols), lambda i, ids: (i, 0)), whole(width, 1), whole(width, 1)],
        [shape(4 * rows, cols)] + [shape(width, 1, wide)] * 2,
    )


def finish_kernel(ids, segment, d_hidden, own, received, gain, out):
    values = segment[...].astype(wide)
    centred = values - jnp.mean(values, -1, keepdims=True)
    inverse = lax.rsqrt(jnp.mean(centred * centred, -1, keepdims=True) + epsilon)
    normal = centred * inverse
    scaled = (own[...] + received[...].astype(wide)) * gain[...].astype(wide)
    inner = (
        scaled
        - jnp.mean(scaled, -1, keepdims=True)
        - normal * jnp.mean(scaled * normal, -1, keepdims=True)
    )
    out[...] = (d_hidden[...] + inner * inverse).astype(narrow)


def finish(order, *arrays):
    segment, d_hidden, own, received, gain = arrays
    arrays = [segment, d_hidden, own, received, gain[None]]
    return order.call(
        finish_kernel,
        "finish",
        [0],
        arrays,
        (1,),
        [whole(*a.shape) for a in arrays],
        whole(*segment.shape),
        shape(*segment.shape),
    )


def sinus_table():
    fine = 64
    frequency = 10000.0 ** (-2.0 * jnp.arange(D // 2, dtype=wide) / D)
    coarse_place = KEYS - 1 - fine * jnp.arange(KEYS // fine, dtype=wide)
    fine_place = jnp.arange(fine, dtype=wide)
    coarse = (coarse_place[:, None] * frequency[None, :])[:, None, :]
    little = (fine_place[:, None] * frequency[None, :])[None, :, :]
    sin_a, cos_a, sin_b, cos_b = lax.optimization_barrier(
        (jnp.sin(coarse), jnp.cos(coarse), jnp.sin(little), jnp.cos(little))
    )
    sine = sin_a * cos_b - cos_a * sin_b
    cosine = cos_a * cos_b + sin_a * sin_b
    return jnp.concatenate([sine, cosine], -1).astype(narrow).reshape(KEYS, D)


def matmul(left, right):
    return jnp.dot(left, right, preferred_element_type=wide)


def outer(left, right):
    return dot(left, right, 0, 0)


def on_device(
    segment,
    memory,
    comp_memory,
    mem_start,
    first_gain,
    first_bias,
    w_query,
    w_key,
    w_value,
    w_rel,
    u_bias,
    v_bias,
    w_out,
    second_gain,
    second_bias,
    w_up,
    b_up,
    w_down,
    b_down,
    w_comp,
    b_comp,
    cot_out,
    cot_comp,
):
    here, blocks = lax.axis_index("blk"), lax.axis_size("blk")
    segment, memory, comp_memory = segment[0], memory[0], comp_memory[0]
    cot_out, cot_comp = cot_out[0], cot_comp[0]
    rows, width = segment.shape
    heads = H // blocks
    cols = heads * DH
    parts = (comp_memory.shape[0], memory.shape[0], rows)
    block = sum(parts)
    count = lax.axis_size("dp").bit_length() - 1
    core, blk = ("dp", 0), ("blk", 0)
    near = [("dp", 1)]
    rest = [("dp", bit) for bit in range(2, count)]
    mate = side(*core)

    order = Order()
    weights = (first_gain, first_bias, w_query, w_key, w_value)

    windows = memory.reshape(parts[1] // RATE, RATE * width)
    far_seg = swap(segment, *blk)
    far_rest = swap(jnp.concatenate([memory, comp_memory], 0), *blk)
    cot_mate = swap(cot_out, *core)

    new_compressed = (matmul(windows, w_comp) + b_comp.astype(wide)).astype(narrow)
    grad_b_comp = jnp.sum(cot_comp.astype(wide), 0)
    grad_comp = outer(windows, cot_comp).astype(narrow)

    sinus = sinus_table()
    relative = matmul(sinus, lax.dynamic_slice_in_dim(w_rel, here * cols, cols, 1)).astype(narrow)

    own_seg, own_mem, own_comp, q_own = project(
        order, here, (segment, memory, comp_memory), (rows, parts[1], parts[0]), True, weights, cols
    )
    far_seg, q_far = project(
        order, here, [far_seg], (rows,), True, weights, cols, after=[relative, new_compressed, grad_comp]
    )
    far_mem, far_comp = project(
        order, here, [far_rest], (parts[1], parts[0]), False, weights, cols
    )
    own, other = (own_comp, own_mem, own_seg), (far_comp, far_mem, far_seg)
    comp_share = lax.psum_scatter(gate(order, grad_comp), ("dp", "blk"), scatter_dimension=0, tiled=True)
    inputs = [q_own, q_far, u_bias, v_bias]
    for part in (1, 2):
        inputs += [[t[part] for t in own], [t[part] for t in other]]
    inputs += [relative]
    mine, received, probs = [], [], []
    per = heads // 2
    for first in range(0, heads, per):
        own_heads, far_heads, kept = attend(order, here, mem_start[0], parts, inputs, first, per)
        mine.append(own_heads)
        received.append(swap(far_heads, *blk))
        probs.append(kept)

    (
        layer_out,
        packed,
        attended_keep,
        gelu_theirs,
        gelu_mine,
        d_pre_theirs,
        d_pre_mine,
        d_hidden,
        da_mine,
        da_theirs,
        grad_b_up,
        grad_second_gain,
        grad_second_bias,
        grad_b_down,
    ) = middle(
        order, here, mate, mine, received, segment, cot_out, w_out, second_gain, second_bias, w_up, b_up, w_down, b_down
    )

    gelu_mate = swap(gelu_theirs, *core)
    da_far = swap(da_theirs, *blk)
    d_pre_mate = swap(d_pre_theirs, *core)
    packed_mate = swap(packed, *core)
    units = gelu_mine.shape[1]
    jobs = (
        ("grad_down", near + [blk] + rest, (gelu_mine, 0, units), (gelu_mate, 0, units), (cot_out, 0, width), (cot_mate, 0, width)),
        ("grad_up", [blk] + near + rest, (packed, 0, width), (packed_mate, 0, width), (d_pre_mine, 0, units), (d_pre_mate, 0, units)),
        ("grad_out", rest + near + [blk], (attended_keep, 0, cols), (packed_mate, 2 * width, cols), (packed, width, width), (packed_mate, width, width)),
    )
    send = [
        outer_pair(order, *job[2:], 1 - side(*job[1][0]), job[0], after=[da_far] if job is jobs[1] else [])
        for job in jobs
    ]
    keep = [outer_pair(order, *job[2:], side(*job[1][0]), job[0]) for job in jobs]
    middle_steps = [job[1] for job in jobs]
    middle_sum = Scatter(order, "sum_middle", list(zip(send, keep, middle_steps)))

    back = []
    for number in range(2):
        back.append(attend_back(order, here, parts, probs[number], inputs, da_mine, da_far, number * per, per))
        middle_sum.step(4 if number == 0 else 2)
        if number == 0:
            comp_gathered = lax.all_gather(gate(order, comp_share), ("dp", "blk"), axis=0, tiled=True)
    dq_own, dq_far, d_key, d_value, d_relative, grad_u, grad_v = zip(*back)
    normed = [t[0] for t in own + other]
    chunk, extra = 4 * width // lax.axis_size("dp"), 16
    grads, by_gain, by_bias = grad_heads(
        order, here, parts, normed, sinus, dq_own, dq_far, d_key, d_value, d_relative, w_query, w_key, w_value, chunk, extra
    )
    middle_sum.step()
    grads, by_gain, by_bias = gate(order, grads, by_gain, by_bias)

    grad_first_bias = by_bias.reshape(width)
    grad_first_gain = (by_gain.reshape(width) - first_bias.astype(wide) * grad_first_bias) / first_gain.astype(wide)

    def spread(vectors):
        return lax.dynamic_update_slice_in_dim(
            jnp.zeros((width,), wide), jnp.concatenate(vectors, 1).reshape(cols), here * cols, 0
        )

    vectors = [
        grad_first_gain,
        grad_first_bias,
        spread(grad_u),
        spread(grad_v),
        grad_second_gain.reshape(-1),
        grad_second_bias.reshape(-1),
        grad_b_up.reshape(-1),
        grad_b_down.reshape(-1),
        grad_b_comp,
    ]

    shares = lax.axis_size("dp")
    beside = jnp.concatenate(vectors).reshape(-1, cols)
    upper = beside.astype(narrow)
    beside = jnp.concatenate([upper, (beside - upper.astype(wide)).astype(narrow)], 0)
    per = -(-beside.shape[0] // shares)
    beside = jnp.pad(beside, ((0, per * shares - beside.shape[0]), (0, 0))).reshape(shares, per, cols)
    grads = lax.dynamic_update_slice(grads.reshape(shares, chunk + extra, cols), beside, (0, chunk, 0))
    heads_share = lax.psum_scatter(grads, "dp", scatter_dimension=0, tiled=True)

    d_normed_own, d_normed_far = segment_back(
        order, here, dq_own, dq_far, d_key, d_value, w_query, w_key, w_value, block
    )
    middle_sum.step()
    d_normed_received = swap(gate(order, d_normed_far), *blk)
    middle_gather = Gather(
        order, "join_middle", [(share, steps[1:]) for share, steps in zip(middle_sum.keep, middle_steps)]
    )
    middle_gather.step()
    d_segment = finish(order, segment, d_hidden, d_normed_own, d_normed_received, first_gain)
    full_comp = widen(order, comp_gathered, "full_comp")
    middle_gather.step()
    heads_gathered = lax.all_gather(gate(order, heads_share), ("dp", "blk"), axis=0, tiled=True)
    middle_gather.step()
    down_pieces, up_pieces, out_pieces = (
        four_pieces(value, core, steps[0]) for value, steps in zip(middle_gather.values, middle_steps)
    )
    sums = heads_gathered[:, chunk : chunk + per].astype(wide).reshape(shares, blocks, per, cols)
    sums = jnp.sum(sums, 1).reshape(shares * per, cols)
    small = sum(vector.shape[0] for vector in vectors) // cols
    sums = (sums[:small] + sums[small : 2 * small]).reshape(-1)
    split = []
    at = 0
    for vector in vectors:
        split.append(sums[at : at + vector.shape[0]])
        at += vector.shape[0]

    devices = 2 << count

    def gathered(share, steps):
        return four_pieces(gather_rows(share, steps[1:]), core, steps[0])

    def by_rows(pieces, outer, inner, total_rows, name):
        blocks = 1 << len(inner)
        chunk = total_rows // len(pieces) // blocks
        (out,) = assemble(
            order,
            pieces,
            blocks,
            [place_of(outer), place_of(inner)],
            [(total_rows, width)],
            (total_rows // len(pieces), width // 2),
            lambda outer_place, part: (outer_place, part),
            lambda inner_place: (inner_place * chunk, 0),
            2,
            name,
        )
        return out

    full_out = by_rows(out_pieces, [core, middle_steps[2][0]], middle_steps[2][1:], width, "full_out")
    full_down = by_rows(down_pieces, [core, middle_steps[0][0]], middle_steps[0][1:], FF, "full_down")
    up_rows = width * 2 // devices
    (full_up,) = assemble(
        order,
        up_pieces,
        devices // 4,
        [place_of([core, middle_steps[1][0]]), place_of(middle_steps[1][1:])],
        [(width, FF)],
        (width // 2, FF // 4),
        lambda outer_place, part: (outer_place % 2, outer_place // 2 * 2 + part),
        lambda inner_place: (inner_place * up_rows, 0),
        2,
        "full_up",
    )
    full_query, full_key, full_value, full_rel = widen_heads(
        order, heads_gathered.reshape(-1, cols), chunk, extra, width, cols, "full_heads"
    )

    return (
        layer_out[None],
        d_segment[None],
        new_compressed[None],
        split[0],
        split[1],
        full_query,
        full_key,
        full_value,
        full_rel,
        split[2],
        split[3],
        full_out,
        split[4],
        split[5],
        full_up,
        split[6],
        full_down,
        split[7],
        full_comp,
        split[8],
    )


def solution(mesh):
    rows = P("dp", "blk", None)
    in_specs = (rows,) * 3 + (P("dp"),) + (P(),) * 17 + (rows,) * 2
    out_specs = (rows,) * 3 + (P(),) * 17
    return jax.shard_map(
        on_device, mesh=mesh, in_specs=in_specs, out_specs=out_specs, check_vma=False
    )
```

time: 912 us -> 624 us (0.68)
  Pallas kernels: 91.2 us -> 287 us
  other arithmetic: 192 us -> 20.8 us
  waiting for transfers between devices: 316 us -> 211 us
  matrix products: 118 us -> 15.9 us
  local copies, waits for them, and re-layouts: 122 us -> 24.3 us
  starting transfers between devices: 58.8 us -> 38.4 us
  between operations: 3.53 us -> 15.6 us
    pallas_call x2 -> x34, Pallas kernels: 91.2 us -> 287 us  [call(): pl.pallas_call(body, grid_spec=pltpu.PrefetchScalarGridSpec(num_scalar_pr...]
    ppermute x69 -> x40, waiting for transfers between devices: 316 us -> 211 us  [swap(): return lax.ppermute(value, axis, pairs)]
    convert_element_type x42 -> x1, other arithmetic: 92.9 us -> 0.01 us  [on_device(): (beside - upper.astype(wide)).astype(narrow)]
    select_n x32 -> x0, other arithmetic: 75.3 us -> none  [in_order(): jnp.where(which == 0, jnp.concatenate([ours, theirs], dim), jnp.concatena...]
    dot_general x12 -> x1, matrix products: 75.8 us -> 4.55 us  [dot(): lax.dot_general(left, right, (((left_dim,), (right_dim,)), ((), ())), pre...]
    slice x8 -> x0, local copies, waits for them, and re-layouts: 32.4 us -> none  [the longest x2 12.9 us: on_device(): full_rel = pair[:, :, 1].reshape(width, width)]
    dot_general x7 -> x2, matrix products: 42.4 us -> 11.4 us  [matmul(): return jnp.dot(left, right, preferred_element_type=wide)]
    dynamic_slice x30 -> x0, local copies, waits for them, and re-layouts: 23.3 us -> none  [the longest x27 18 us: scatter_sum(): theirs = lax.dynamic_slice_in_dim(value, (1 - which) * half, half, 0)]
  transfers between devices with their start and end apart: 69 -> 44, of which waited for: 33 -> 19; matrix products, arithmetic and copies ran while one was open for 46% -> 7% of each run, Pallas kernels for 10% -> 44%
where the time goes in v2:
time: 624 us; the launch traced here: 613 us
  Pallas kernels  287 us (46%)
  waiting for transfers between devices  211 us (34%)
  starting transfers between devices  38.4 us (6%)
  local copies, waits for them, and re-layouts  24.3 us (4%)
  other arithmetic  20.8 us (3%)
  matrix products  15.9 us (3%)
  between operations  15.6 us (2%)
    pallas_call x34, Pallas kernels, call(): pl.pallas_call(body, grid_spec=pltpu.PrefetchScalarGridSpec(num_scalar_pr...  287 us
    ppermute x40, waiting for transfers between devices, swap(): return lax.ppermute(value, axis, pairs)  211 us
    ppermute x40, starting transfers between devices, swap(): return lax.ppermute(value, axis, pairs)  38.3 us
    unnamed x126, local copies, waits for them, and re-layouts  15.4 us
  transfers between devices with their start and end apart: 44, of which 19 were waited for; matrix products, arithmetic and copies ran while one was open for 7% of the time, Pallas kernels for 44%

profile of v2, /device:TPU:0, one launch (start us, length us, event | category | flops | bytes accessed | tf_op | source)
XLA Modules:
  0.0 613.3 jit_solution(7418464480257209508)
XLA Ops:
  25.2 7.3 %project.3 = (bf16[480,1024]{1,0:T(8,128)(2,1)}, bf16[480,512]{1,0:T(8,128)(2,1)}, bf16[480,512]{1,0:T(8,128)(2,1)}, bf16[480,1024]{1,0:T(8,128)(2,1)}, bf16[480...) custom-call(s32[1]{0:T(128)} %bitcast.scalar_ref, ...), custom_call_target="tpu_custom_call" | custom-call | flops 1000 | bytes 1000 | tf_op jit(solution)/shard_map/project/pallas_call | solution.py:52
  32.5 6.7 %convolution_convert_fusion.1.refs_6_.refs_16_.refs_17_ = bf16[2432,512]{1,0:T(8,128)(2,1)} fusion(bf16[1024,1024]{1,0:T(8,128)(2,1)S(1)} %copy-done, s32[]{:T(128)S(6)} %select_n.2, bf16[2432,512]{1,0:T(8,128)(2,1)} %bitcast.76, bf16[2432,512]{1,0:T(8,128)(2,1)} %bitcast.74), kind=kOutput, calls=%fused_computation.4 | convolution fusion | flops 2561343488 | bytes 8519684 | tf_op jit(solution)/shard_map/dot_general | solution.py:813
  43.9 5.6 project.4
  49.5 15.2 %collective-permute-done.1.refs_0_ = bf16[736,1024]{1,0:T(8,128)(2,1)} collective-permute-done((bf16[736,1024]{1,0:T(8,128)(2,1)}, bf16[736,1024]{1,0:T(8,128)(2,1)}, u32[]{:S(2)}, u32[]{:S(2)}) %collective-permute-start.1) | collective-permute-done | bytes 1507360 | tf_op jit(solution)/shard_map/ppermute | solution.py:75
  72.2 17.5 %attend.2 = (bf16[480,256]{1,0:T(8,128)(2,1)}, bf16[480,256]{1,0:T(8,128)(2,1)}, bf16[2,960,2432]{2,1,0:T(8,128)(2,1)}) custom-call(s32[2]{0:T(128)} %pad_add_fusion.1.scalar_ref, f32[480,512]{1,0:T(8,128)} %get-tuple-element.120.refs_9_.refs_0_.refs_1_, f32[480,512]{1,0:T(8,128)} %get-tuple-element.125.refs_6_.refs_1_.refs_2_, ...), custom_call_target="tpu_custom_call" | custom-call | flops 1000 | bytes 1000 | tf_op jit(solution)/shard_map/attend/pallas_call | solution.py:52
  91.5 17.8 %attend.3 = (bf16[480,256]{1,0:T(8,128)(2,1)}, bf16[480,256]{1,0:T(8,128)(2,1)}, bf16[2,960,2432]{2,1,0:T(8,128)(2,1)}) custom-call(s32[2]{0:T(128)} %pad_add_fusion.1.scalar_ref, f32[480,512]{1,0:T(8,128)} %get-tuple-element.120.refs_9_.refs_0_.refs_1_, f32[480,512]{1,0:T(8,128)} %get-tuple-element.125.refs_6_.refs_1_.refs_2_, ...), custom_call_target="tpu_custom_call" | custom-call | flops 1000 | bytes 1000 | tf_op jit(solution)/shard_map/attend/pallas_call | solution.py:52
  116.8 32.8 %middle.1 = (bf16[480,1024]{1,0:T(8,128)(2,1)}, bf16[480,2560]{1,0:T(8,128)(2,1)}, bf16[480,512]{1,0:T(8,128)(2,1)}, bf16[480,2048]{1,0:T(8,128)(2,1)}, bf16[480...) custom-call(s32[2]{0:T(128)} %pad_add_fusion.scalar_ref, ...), custom_call_target="tpu_custom_call" | custom-call | flops 1000 | bytes 1000 | tf_op jit(solution)/shard_map/middle/pallas_call | solution.py:52
  151.3 8.7 %collective-permute-done.8.refs_3_ = bf16[480,1024]{1,0:T(8,128)(2,1)} collective-permute-done((bf16[480,1024]{1,0:T(8,128)(2,1)S(1)}, bf16[480,1024]{1,0:T(8,128)(2,1)}, u32[]{:S(2)}, u32[]{:S(2)}) %collective-permute-start.8) | collective-permute-done | bytes 983072 | tf_op jit(solution)/shard_map/ppermute | solution.py:75
  160.1 6.2 %grad_down.2.refs_5_ = bf16[1024,1024]{1,0:T(8,128)(2,1)} custom-call(s32[1]{0:T(128)} %bitcast.19.scalar_ref, bf16[480,2048]{1,0:T(8,128)(2,1)} %get-tuple-element.152.refs_0_, bf16[480,2048]{1,0:T(8,128)(2,1)} %collective-permute-done.7.refs_1_, bf16[480,1024]{1,0:T(8,128)(2,1)} %bitcast.86, bf16[480,1024]{1,0:T(8,128)(2,1)} %collective-permute-done.8.refs_3_, ...), custom_call_target="tpu_custom_call" | custom-call | flops 1000 | bytes 1000 | tf_op jit(solution)/shard_map/grad_down/pallas_call | solution.py:52
  170.7 6.0 grad_up.2.refs_4_
  182.1 6.1 %grad_down.3.refs_4_.refs_0_.refs_2_ = bf16[1024,1024]{1,0:T(8,128)(2,1)} custom-call(s32[1]{0:T(128)} %bitcast.16.scalar_ref, bf16[480,2048]{1,0:T(8,128)(2,1)} %get-tuple-element.152.refs_0_, bf16[480,2048]{1,0:T(8,128)(2,1)} %collective-permute-done.7.refs_1_, bf16[480,1024]{1,0:T(8,128)(2,1)} %bitcast.87, ...), custom_call_target="tpu_custom_call" | custom-call | flops 1000 | bytes 1000 | tf_op jit(solution)/shard_map/grad_down/pallas_call | solution.py:52
  188.8 6.0 grad_up.3.refs_4_.refs_6_
  198.2 29.6 %attend_back.2 = (bf16[480,256]{1,0:T(8,128)(2,1)}, bf16[480,256]{1,0:T(8,128)(2,1)}, bf16[2432,256]{1,0:T(8,128)(2,1)}, bf16[2432,256]{1,0:T(8,128)(2,1)}, bf16...) custom-call(s32[1]{0:T(128)} %bitcast.scalar_ref, ...), custom_call_target="tpu_custom_call" | custom-call | flops 1000 | bytes 1000 | tf_op jit(solution)/shard_map/attend_back/pallas_call | solution.py:52
  229.2 6.9 %sum_middle.4 = (bf16[512,1024]{1,0:T(8,128)(2,1)}, bf16[512,1024]{1,0:T(8,128)(2,1)}, bf16[256,2048]{1,0:T(8,128)(2,1)}, bf16[256,2048]{1,0:T(8,128)(2,1)}, bf1...) custom-call(s32[3]{0:T(128)} %pad_add_fusion.2.scalar_ref, bf16[1024,1024]{1,0:T(8,128)(2,1)} %grad_down.3.refs_4_.refs_0_.refs_2_, ...), custom_call_target="tpu_custom_call" | custom-call | flops 1000 | bytes 1000 | tf_op jit(solution)/shard_map/sum_middle/pallas_call | solution.py:52
  242.2 29.3 %attend_back.3 = (bf16[480,256]{1,0:T(8,128)(2,1)}, bf16[480,256]{1,0:T(8,128)(2,1)}, bf16[2432,256]{1,0:T(8,128)(2,1)}, bf16[2432,256]{1,0:T(8,128)(2,1)}, bf16...) custom-call(s32[1]{0:T(128)} %bitcast.scalar_ref, ...), custom_call_target="tpu_custom_call" | custom-call | flops 1000 | bytes 1000 | tf_op jit(solution)/shard_map/attend_back/pallas_call | solution.py:52
  285.3 20.9 %grad_heads.1 = (bf16[4352,512]{1,0:T(8,128)(2,1)}, f32[1024,1]{1,0:T(8,128)}, f32[1024,1]{1,0:T(8,128)}) custom-call(s32[1]{0:T(128)} %bitcast.scalar_ref, bf16[256,1024]{1,0:T(8,128)(2,1)} %get-tuple-element.165.refs_0_, bf16[480,1024]{1,0:T(8,128)(2,1)} %get-tuple-element.166.refs_1_, bf16[480,1024]{1,0:T(8,128)(2,1)} %get-tuple-element.167.refs_2_, ...), custom_call_target="tpu_custom_call" | custom-call | flops 1000 | bytes 1000 | tf_op jit(solution)/shard_map/grad_heads/pallas_call | solution.py:52
  307.0 10.8 %collective-permute-done.16.refs_5_.refs_7_ = bf16[128,2048]{1,0:T(8,128)(2,1)S(1)} collective-permute-done((bf16[128,2048]{1,0:T(8,128)(2,1)}, bf16[128,2048]{1,0:T(8,128)(2,1)S(1)}, u32[]{:S(2)}, u32[]{:S(2)}) %collective-permute-start.16) | collective-permute-done | bytes 524320 | tf_op jit(solution)/shard_map/ppermute | solution.py:75
  330.5 8.7 %segment_back.1 = (f32[480,1024]{1,0:T(8,128)}, bf16[480,1024]{1,0:T(8,128)(2,1)}) custom-call(s32[1]{0:T(128)} %bitcast.scalar_ref, bf16[480,256]{1,0:T(8,128)(2,1)} %get-tuple-element.155.refs_7_.refs_0_, bf16[480,256]{1,0:T(8,128)(2,1)} %get-tuple-element.158.refs_8_.refs_1_, bf16[480,256]{1,0:T(8,128)(2,1)} %get-tuple-element.159.refs_9_.refs_2_, ...), custom_call_target="tpu_custom_call" | custom-call | flops 1000 | bytes 1000 | tf_op jit(solution)/shard_map/segment_back/pallas_call | solution.py:52
  356.7 20.3 %collective-permute-done.24.refs_5_ = bf16[32,1024]{1,0:T(8,128)(2,1)S(1)} collective-permute-done((bf16[32,1024]{1,0:T(8,128)(2,1)}, bf16[32,1024]{1,0:T(8,128)(2,1)S(1)}, u32[]{:S(2)}, u32[]{:S(2)}) %collective-permute-start.24) | collective-permute-done | bytes 65568 | tf_op jit(solution)/shard_map/ppermute | solution.py:75
  377.1 9.0 %collective-permute-done.22.refs_1_ = bf16[128,1024]{1,0:T(8,128)(2,1)S(1)} collective-permute-done((bf16[128,1024]{1,0:T(8,128)(2,1)}, bf16[128,1024]{1,0:T(8,128)(2,1)S(1)}, u32[]{:S(2)}, u32[]{:S(2)}) %collective-permute-start.22) | collective-permute-done | bytes 262176 | tf_op jit(solution)/shard_map/ppermute | solution.py:75
  386.1 10.4 %collective-permute-done.23.refs_3_ = bf16[64,2048]{1,0:T(8,128)(2,1)S(1)} collective-permute-done((bf16[64,2048]{1,0:T(8,128)(2,1)}, bf16[64,2048]{1,0:T(8,128)(2,1)S(1)}, u32[]{:S(2)}, u32[]{:S(2)}) %collective-permute-start.23) | collective-permute-done | bytes 262176 | tf_op jit(solution)/shard_map/ppermute | solution.py:75
  408.0 7.9 %full_comp.1.refs_6_ = f32[3072,1024]{1,0:T(8,128)} custom-call(s32[1]{0:T(128)} %constant.12.clone.1.scalar_ref, bf16[3072,1024]{1,0:T(8,128)(2,1)} %all-gather.3.cloned.1.call-done.refs_0_, bf16[480,1024]{1,0:T(8,128)(2,1)} %finish.1.refs_1_), custom_call_target="tpu_custom_call" | custom-call | flops 1000 | bytes 1000 | tf_op jit(solution)/shard_map/full_comp/pallas_call | solution.py:52
  420.8 11.1 %collective-permute-done.26.refs_3_ = bf16[128,2048]{1,0:T(8,128)(2,1)S(1)} collective-permute-done((bf16[128,2048]{1,0:T(8,128)(2,1)}, bf16[128,2048]{1,0:T(8,128)(2,1)S(1)}, u32[]{:S(2)}, u32[]{:S(2)}) %collective-permute-start.26) | collective-permute-done | bytes 524320 | tf_op jit(solution)/shard_map/ppermute | solution.py:75
  439.5 17.1 %collective-permute-done.30.refs_5_ = bf16[128,1024]{1,0:T(8,128)(2,1)S(1)} collective-permute-done((bf16[128,1024]{1,0:T(8,128)(2,1)}, bf16[128,1024]{1,0:T(8,128)(2,1)S(1)}, u32[]{:S(2)}, u32[]{:S(2)}) %collective-permute-start.30) | collective-permute-done | bytes 262176 | tf_op jit(solution)/shard_map/ppermute | solution.py:75
  456.6 6.6 %collective-permute-done.28.refs_1_ = bf16[512,1024]{1,0:T(8,128)(2,1)S(1)} collective-permute-done((bf16[512,1024]{1,0:T(8,128)(2,1)}, bf16[512,1024]{1,0:T(8,128)(2,1)S(1)}, u32[]{:S(2)}, u32[]{:S(2)}) %collective-permute-start.28) | collective-permute-done | bytes 1048608 | tf_op jit(solution)/shard_map/ppermute | solution.py:75
  472.1 62.7 %collective-permute-done.34.refs_1_ = bf16[1024,1024]{1,0:T(8,128)(2,1)} collective-permute-done((bf16[1024,1024]{1,0:T(8,128)(2,1)}, bf16[1024,1024]{1,0:T(8,128)(2,1)}, u32[]{:S(2)}, u32[]{:S(2)}) %collective-permute-start.34) | collective-permute-done | bytes 2097184 | tf_op jit(solution)/shard_map/ppermute | solution.py:75
  535.8 5.6 collective-permute-done.38.refs_2_
  542.9 12.7 %collective-permute-done.37.refs_1_ = bf16[256,1024]{1,0:T(8,128)(2,1)S(1)} collective-permute-done((bf16[256,1024]{1,0:T(8,128)(2,1)}, bf16[256,1024]{1,0:T(8,128)(2,1)S(1)}, u32[]{:S(2)}, u32[]{:S(2)}) %collective-permute-start.37) | collective-permute-done | bytes 524320 | tf_op jit(solution)/shard_map/ppermute | solution.py:75
  557.7 7.1 %full_out.1.refs_4_ = f32[1024,1024]{1,0:T(8,128)} custom-call(s32[2]{0:T(128)} %pad_add_fusion.7.scalar_ref, bf16[256,1024]{1,0:T(8,128)(2,1)} %get-tuple-element.215.refs_0_.refs_4_, bf16[256,1024]{1,0:T(8,128)(2,1)} %copy-done.22, bf16[256,1024]{1,0:T(8,128)(2,1)} %copy-done.21, bf16[256,1024]{1,0:T(8,128)(2,1)} %collective-permute-done.39.refs_3_, ...), custom_call_target="tpu_custom_call" | custom-call | flops 1000 | bytes 1000 | tf_op jit(solution)/shard_map/full_out/pallas_call | solution.py:52
  564.7 12.1 %full_down.1.refs_4_ = f32[4096,1024]{1,0:T(8,128)} custom-call(s32[2]{0:T(128)} %pad_add_fusion.6.scalar_ref, bf16[1024,1024]{1,0:T(8,128)(2,1)} %get-tuple-element.214.refs_0_, bf16[1024,1024]{1,0:T(8,128)(2,1)} %collective-permute-done.34.refs_1_, bf16[1024,1024]{1,0:T(8,128)(2,1)} %collective-permute-done.35.refs_2_, ...), custom_call_target="tpu_custom_call" | custom-call | flops 1000 | bytes 1000 | tf_op jit(solution)/shard_map/full_down/pallas_call | solution.py:52
  576.9 12.2 %full_up.1.refs_1_ = f32[1024,4096]{1,0:T(8,128)} custom-call(s32[2]{0:T(128)} %pad_add_fusion.5.scalar_ref, bf16[512,2048]{1,0:T(8,128)(2,1)} %get-tuple-element.213.refs_0_, bf16[512,2048]{1,0:T(8,128)(2,1)} %copy-done.8, bf16[512,2048]{1,0:T(8,128)(2,1)} %collective-permute-done.32.refs_2_, bf16[512,2048]{1,0:T(8,128)(2,1)} %collective-permute-done.33.refs_3_, ...), custom_call_target="tpu_custom_call" | custom-call | flops 1000 | bytes 1000 | tf_op jit(solution)/shard_map/full_up/pallas_call | solution.py:52
  595.6 10.7 %full_heads.1 = (f32[1024,1024]{1,0:T(8,128)}, f32[1024,1024]{1,0:T(8,128)}, f32[1024,1024]{1,0:T(8,128)}, f32[1024,1024]{1,0:T(8,128)}) custom-call(s32[1]{0:T(128)} %constant.12.clone.1.scalar_ref, bf16[8704,512]{1,0:T(8,128)(2,1)} %bitcast.78, f32[1024,4096]{1,0:T(8,128)} %full_up.1.refs_1_), custom_call_target="tpu_custom_call" | custom-call | flops 1000 | bytes 1000 | tf_op jit(solution)/shard_map/full_heads/pallas_call | solution.py:52
  (266 shorter events, 150.3 us)
Async XLA Ops:
  7.2 228.9 %reduce-scatter.3.cloned.1.call-start = ((), (), s32[]{:S(2)}) async-start(), calls=%async_computation.2 | async-start | bytes 6488064 | tf_op jit(solution)/shard_map/reduce_scatter | solution.py:884
  7.3 36.6 %collective-permute-start = (bf16[480,1024]{1,0:T(8,128)(2,1)}, bf16[480,1024]{1,0:T(8,128)(2,1)}, u32[]{:S(2)}, u32[]{:S(2)}) collective-permute-start(bf16[480,1024]{1,0:T(8,128)(2,1)} %bitcast.79), channel_id=1, source_target_pairs={{0,1},{1,0},{2,3},{3,2},{4,5},{5,4},{6,7},{7,6},{8,9},{9,8},{10,11... | collective-permute-start | bytes 2949128 | tf_op jit(solution)/shard_map/ppermute | solution.py:75
  12.9 51.8 %collective-permute-start.1 = (bf16[736,1024]{1,0:T(8,128)(2,1)}, bf16[736,1024]{1,0:T(8,128)(2,1)}, u32[]{:S(2)}, u32[]{:S(2)}) collective-permute-start(bf16[736,1024]{1,0:T(8,128)(2,1)} %pad_maximum_fusion.1), channel_id=1, source_target_pairs={{0,1},{1,0},{2,3},{3,2},{4,5},{5,4},{6,7},{7,6},{8,9},{9,8},{10,11... | collective-permute-start | bytes 4521992 | tf_op jit(solution)/shard_map/ppermute | solution.py:75
  69.7 338.3 %all-gather.3.cloned.1.call-start = ((), (), s32[]{:S(2)}) async-start(), calls=%async_computation.4 | async-start | bytes 6488064 | tf_op jit(solution)/shard_map/all_gather | solution.py:939
  89.7 23.0 %collective-permute-start.2 = (bf16[480,256]{1,0:T(8,128)(2,1)}, bf16[480,256]{1,0:T(8,128)(2,1)S(1)}, u32[]{:S(2)}, u32[]{:S(2)}) collective-permute-start(bf16[480,256]{1,0:T(8,128)(2,1)} %get-tuple-element.141), channel_id=1, source_target_pairs={{0,1},{1,0},{2,3},{3,2},{4,5},{5,4},{6,7},{7,6},{8,9},{9,8},{10,11... | collective-permute-start | bytes 737288 | tf_op jit(solution)/shard_map/ppermute | solution.py:75
  149.7 19.6 %collective-permute-start.5 = (bf16[480,2560]{1,0:T(8,128)(2,1)}, bf16[480,2560]{1,0:T(8,128)(2,1)S(1)}, u32[]{:S(2)}, u32[]{:S(2)}) collective-permute-start(bf16[480,2560]{1,0:T(8,128)(2,1)} %get-tuple-element.149.refs_0_.refs_2_), channel_id=1, source_target_pairs={{0,2},{2,0},{4,6},{6,4},{8,10},{10,8},{12,14},{14,12},{16,18},{18,... | collective-permute-start | bytes 7372808 | tf_op jit(solution)/shard_map/ppermute | solution.py:75
  166.3 61.5 %collective-permute-start.9 = (bf16[1024,1024]{1,0:T(8,128)(2,1)}, bf16[1024,1024]{1,0:T(8,128)(2,1)}, u32[]{:S(2)}, u32[]{:S(2)}) collective-permute-start(bf16[1024,1024]{1,0:T(8,128)(2,1)} %grad_down.2.refs_5_), channel_id=1, source_target_pairs={{0,4},{2,6},{4,0},{6,2},{8,12},{10,14},{12,8},{14,10},{16,20},{18,... | collective-permute-start | bytes 6291464 | tf_op jit(solution)/shard_map/ppermute | solution.py:75
  176.7 51.1 %collective-permute-start.10 = (bf16[512,2048]{1,0:T(8,128)(2,1)}, bf16[512,2048]{1,0:T(8,128)(2,1)S(1)}, u32[]{:S(2)}, u32[]{:S(2)}) collective-permute-start(bf16[512,2048]{1,0:T(8,128)(2,1)} %grad_up.2.refs_4_), channel_id=1, source_target_pairs={{0,1},{1,0},{2,3},{3,2},{4,5},{5,4},{6,7},{7,6},{8,9},{9,8},{10,11... | collective-permute-start | bytes 6291464 | tf_op jit(solution)/shard_map/ppermute | solution.py:75
  180.3 47.4 %collective-permute-start.11 = (bf16[256,1024]{1,0:T(8,128)(2,1)}, bf16[256,1024]{1,0:T(8,128)(2,1)S(1)}, u32[]{:S(2)}, u32[]{:S(2)}) collective-permute-start(bf16[256,1024]{1,0:T(8,128)(2,1)} %grad_out.2.refs_4_), channel_id=1, source_target_pairs={{0,8},{2,10},{4,12},{6,14},{8,0},{10,2},{12,4},{14,6},{16,24},{18,... | collective-permute-start | bytes 1572872 | tf_op jit(solution)/shard_map/ppermute | solution.py:75
  236.2 199.6 %reduce-scatter.5.cloned.1.call-start = ((), (), s32[]{:S(2)}) async-start(), calls=%async_computation.3 | async-start | bytes 4734976 | tf_op jit(solution)/shard_map/reduce_scatter | solution.py:976
  236.2 35.3 %collective-permute-start.12 = (bf16[512,1024]{1,0:T(8,128)(2,1)}, bf16[512,1024]{1,0:T(8,128)(2,1)S(1)}, u32[]{:S(2)}, u32[]{:S(2)}) collective-permute-start(bf16[512,1024]{1,0:T(8,128)(2,1)} %get-tuple-element.174), channel_id=1, source_target_pairs={{0,1},{1,0},{2,3},{3,2},{4,5},{5,4},{6,7},{7,6},{8,9},{9,8},{10,11... | collective-permute-start | bytes 3145736 | tf_op jit(solution)/shard_map/ppermute | solution.py:75
  237.8 33.8 %collective-permute-start.13 = (bf16[256,2048]{1,0:T(8,128)(2,1)}, bf16[256,2048]{1,0:T(8,128)(2,1)S(1)}, u32[]{:S(2)}, u32[]{:S(2)}) collective-permute-start(bf16[256,2048]{1,0:T(8,128)(2,1)} %get-tuple-element.176), channel_id=1, source_target_pairs={{0,4},{2,6},{4,0},{6,2},{8,12},{10,14},{12,8},{14,10},{16,20},{18,... | collective-permute-start | bytes 3145736 | tf_op jit(solution)/shard_map/ppermute | solution.py:75
  239.2 32.3 %collective-permute-start.14 = (bf16[128,1024]{1,0:T(8,128)(2,1)}, bf16[128,1024]{1,0:T(8,128)(2,1)S(1)}, u32[]{:S(2)}, u32[]{:S(2)}) collective-permute-start(bf16[128,1024]{1,0:T(8,128)(2,1)} %get-tuple-element.177), channel_id=1, source_target_pairs={{0,16},{2,18},{4,20},{6,22},{8,24},{10,26},{12,28},{14,30},{16,0},... | collective-permute-start | bytes 786440 | tf_op jit(solution)/shard_map/ppermute | solution.py:75
  277.4 29.7 %collective-permute-start.15 = (bf16[256,1024]{1,0:T(8,128)(2,1)}, bf16[256,1024]{1,0:T(8,128)(2,1)S(1)}, u32[]{:S(2)}, u32[]{:S(2)}) collective-permute-start(bf16[256,1024]{1,0:T(8,128)(2,1)} %get-tuple-element.184), channel_id=1, source_target_pairs={{0,8},{2,10},{4,12},{6,14},{8,0},{10,2},{12,4},{14,6},{16,24},{18,... | collective-permute-start | bytes 1572872 | tf_op jit(solution)/shard_map/ppermute | solution.py:75
  277.9 39.9 %collective-permute-start.16 = (bf16[128,2048]{1,0:T(8,128)(2,1)}, bf16[128,2048]{1,0:T(8,128)(2,1)S(1)}, u32[]{:S(2)}, u32[]{:S(2)}) collective-permute-start(bf16[128,2048]{1,0:T(8,128)(2,1)} %get-tuple-element.186), channel_id=1, source_target_pairs={{0,8},{2,10},{4,12},{6,14},{8,0},{10,2},{12,4},{14,6},{16,24},{18,... | collective-permute-start | bytes 1572872 | tf_op jit(solution)/shard_map/ppermute | solution.py:75
  284.4 22.6 %collective-permute-start.17 = (bf16[64,1024]{1,0:T(8,128)(2,1)S(1)}, bf16[64,1024]{1,0:T(8,128)(2,1)S(1)}, u32[]{:S(2)}, u32[]{:S(2)}) collective-permute-start(bf16[64,1024]{1,0:T(8,128)(2,1)S(1)} %copy-done.52), channel_id=1, source_target_pairs={{0,4},{2,6},{4,0},{6,2},{8,12},{10,14},{12,8},{14,10},{16,20},{18,... | collective-permute-start | bytes 393224 | tf_op jit(solution)/shard_map/ppermute | solution.py:75
  326.5 262.6 %all-gather.5.cloned.1.call-start = ((), (), s32[]{:S(2)}) async-start(), calls=%async_computation.5 | async-start | bytes 9191424 | tf_op jit(solution)/shard_map/all_gather | solution.py:990
  327.0 22.0 %collective-permute-start.19 = (bf16[64,2048]{1,0:T(8,128)(2,1)S(1)}, bf16[64,2048]{1,0:T(8,128)(2,1)S(1)}, u32[]{:S(2)}, u32[]{:S(2)}) collective-permute-start(bf16[64,2048]{1,0:T(8,128)(2,1)S(1)} %copy-done.50), channel_id=1, source_target_pairs={{0,16},{2,18},{4,20},{6,22},{8,24},{10,26},{12,28},{14,30},{16,0},... | collective-permute-start | bytes 786440 | tf_op jit(solution)/shard_map/ppermute | solution.py:75
  351.8 50.2 %collective-permute-start.21 = (bf16[480,1024]{1,0:T(8,128)(2,1)}, bf16[480,1024]{1,0:T(8,128)(2,1)S(1)}, u32[]{:S(2)}, u32[]{:S(2)}) collective-permute-start(bf16[480,1024]{1,0:T(8,128)(2,1)} %gate.8.refs_6_), channel_id=1, source_target_pairs={{0,1},{1,0},{2,3},{3,2},{4,5},{5,4},{6,7},{7,6},{8,9},{9,8},{10,11... | collective-permute-start | bytes 2949128 | tf_op jit(solution)/shard_map/ppermute | solution.py:75
  353.2 32.9 %collective-permute-start.22 = (bf16[128,1024]{1,0:T(8,128)(2,1)}, bf16[128,1024]{1,0:T(8,128)(2,1)S(1)}, u32[]{:S(2)}, u32[]{:S(2)}) collective-permute-start(bf16[128,1024]{1,0:T(8,128)(2,1)} %get-tuple-element.198.refs_0_), channel_id=1, source_target_pairs={{0,16},{2,18},{4,20},{6,22},{8,24},{10,26},{12,28},{14,30},{16,0},... | collective-permute-start | bytes 786440 | tf_op jit(solution)/shard_map/ppermute | solution.py:75
  353.2 43.2 %collective-permute-start.23 = (bf16[64,2048]{1,0:T(8,128)(2,1)}, bf16[64,2048]{1,0:T(8,128)(2,1)S(1)}, u32[]{:S(2)}, u32[]{:S(2)}) collective-permute-start(bf16[64,2048]{1,0:T(8,128)(2,1)} %get-tuple-element.199.refs_2_), channel_id=1, source_target_pairs={{0,16},{2,18},{4,20},{6,22},{8,24},{10,26},{12,28},{14,30},{16,0},... | collective-permute-start | bytes 786440 | tf_op jit(solution)/shard_map/ppermute | solution.py:75
  356.1 21.0 %collective-permute-start.24 = (bf16[32,1024]{1,0:T(8,128)(2,1)}, bf16[32,1024]{1,0:T(8,128)(2,1)S(1)}, u32[]{:S(2)}, u32[]{:S(2)}) collective-permute-start(bf16[32,1024]{1,0:T(8,128)(2,1)} %get-tuple-element.197.refs_1_.refs_4_), channel_id=1, source_target_pairs={{0,1},{1,0},{2,3},{3,2},{4,5},{5,4},{6,7},{7,6},{8,9},{9,8},{10,11... | collective-permute-start | bytes 196616 | tf_op jit(solution)/shard_map/ppermute | solution.py:75
  399.4 21.4 %collective-permute-start.25 = (bf16[256,1024]{1,0:T(8,128)(2,1)}, bf16[256,1024]{1,0:T(8,128)(2,1)S(1)}, u32[]{:S(2)}, u32[]{:S(2)}) collective-permute-start(bf16[256,1024]{1,0:T(8,128)(2,1)} %get-tuple-element.208.refs_0_), channel_id=1, source_target_pairs={{0,8},{2,10},{4,12},{6,14},{8,0},{10,2},{12,4},{14,6},{16,24},{18,... | collective-permute-start | bytes 1572872 | tf_op jit(solution)/shard_map/ppermute | solution.py:75
  399.4 32.6 %collective-permute-start.26 = (bf16[128,2048]{1,0:T(8,128)(2,1)}, bf16[128,2048]{1,0:T(8,128)(2,1)S(1)}, u32[]{:S(2)}, u32[]{:S(2)}) collective-permute-start(bf16[128,2048]{1,0:T(8,128)(2,1)} %get-tuple-element.209.refs_2_), channel_id=1, source_target_pairs={{0,8},{2,10},{4,12},{6,14},{8,0},{10,2},{12,4},{14,6},{16,24},{18,... | collective-permute-start | bytes 1572872 | tf_op jit(solution)/shard_map/ppermute | solution.py:75
  435.8 27.3 %collective-permute-start.28 = (bf16[512,1024]{1,0:T(8,128)(2,1)}, bf16[512,1024]{1,0:T(8,128)(2,1)S(1)}, u32[]{:S(2)}, u32[]{:S(2)}) collective-permute-start(bf16[512,1024]{1,0:T(8,128)(2,1)} %get-tuple-element.211.refs_0_), channel_id=1, source_target_pairs={{0,1},{1,0},{2,3},{3,2},{4,5},{5,4},{6,7},{7,6},{8,9},{9,8},{10,11... | collective-permute-start | bytes 3145736 | tf_op jit(solution)/shard_map/ppermute | solution.py:75
  437.4 26.9 %collective-permute-start.29 = (bf16[256,2048]{1,0:T(8,128)(2,1)}, bf16[256,2048]{1,0:T(8,128)(2,1)S(1)}, u32[]{:S(2)}, u32[]{:S(2)}) collective-permute-start(bf16[256,2048]{1,0:T(8,128)(2,1)} %get-tuple-element.212.refs_2_), channel_id=1, source_target_pairs={{0,4},{2,6},{4,0},{6,2},{8,12},{10,14},{12,8},{14,10},{16,20},{18,... | collective-permute-start | bytes 3145736 | tf_op jit(solution)/shard_map/ppermute | solution.py:75
  469.9 64.9 %collective-permute-start.34 = (bf16[1024,1024]{1,0:T(8,128)(2,1)}, bf16[1024,1024]{1,0:T(8,128)(2,1)}, u32[]{:S(2)}, u32[]{:S(2)}) collective-permute-start(bf16[1024,1024]{1,0:T(8,128)(2,1)} %get-tuple-element.214.refs_0_), channel_id=1, source_target_pairs={{0,4},{2,6},{4,0},{6,2},{8,12},{10,14},{12,8},{14,10},{16,20},{18,... | collective-permute-start | bytes 6291464 | tf_op jit(solution)/shard_map/ppermute | solution.py:75
  471.2 64.2 %collective-permute-start.31 = (bf16[512,2048]{1,0:T(8,128)(2,1)}, bf16[512,2048]{1,0:T(8,128)(2,1)S(1)}, u32[]{:S(2)}, u32[]{:S(2)}) collective-permute-start(bf16[512,2048]{1,0:T(8,128)(2,1)} %get-tuple-element.213.refs_0_), channel_id=1, source_target_pairs={{0,1},{1,0},{2,3},{3,2},{4,5},{5,4},{6,7},{7,6},{8,9},{9,8},{10,11... | collective-permute-start | bytes 6291464 | tf_op jit(solution)/shard_map/ppermute | solution.py:75
  472.1 92.6 %collective-permute-start.35 = (bf16[1024,1024]{1,0:T(8,128)(2,1)}, bf16[1024,1024]{1,0:T(8,128)(2,1)}, u32[]{:S(2)}, u32[]{:S(2)}) collective-permute-start(bf16[1024,1024]{1,0:T(8,128)(2,1)} %get-tuple-element.214.refs_0_), channel_id=1, source_target_pairs={{0,2},{2,0},{4,6},{6,4},{8,10},{10,8},{12,14},{14,12},{16,18},{18,... | collective-permute-start | bytes 6291464 | tf_op jit(solution)/shard_map/ppermute | solution.py:75
  534.8 29.9 %collective-permute-start.36 = (bf16[1024,1024]{1,0:T(8,128)(2,1)}, bf16[1024,1024]{1,0:T(8,128)(2,1)}, u32[]{:S(2)}, u32[]{:S(2)}) collective-permute-start(bf16[1024,1024]{1,0:T(8,128)(2,1)} %collective-permute-done.34.refs_1_), channel_id=1, source_target_pairs={{0,2},{2,0},{4,6},{6,4},{8,10},{10,8},{12,14},{14,12},{16,18},{18,... | collective-permute-start | bytes 6291464 | tf_op jit(solution)/shard_map/ppermute | solution.py:75
  534.8 42.1 %collective-permute-start.32 = (bf16[512,2048]{1,0:T(8,128)(2,1)}, bf16[512,2048]{1,0:T(8,128)(2,1)}, u32[]{:S(2)}, u32[]{:S(2)}) collective-permute-start(bf16[512,2048]{1,0:T(8,128)(2,1)} %get-tuple-element.213.refs_0_), channel_id=1, source_target_pairs={{0,2},{2,0},{4,6},{6,4},{8,10},{10,8},{12,14},{14,12},{16,18},{18,... | collective-permute-start | bytes 6291464 | tf_op jit(solution)/shard_map/ppermute | solution.py:75
  535.3 41.6 %collective-permute-start.33 = (bf16[512,2048]{1,0:T(8,128)(2,1)S(1)}, bf16[512,2048]{1,0:T(8,128)(2,1)}, u32[]{:S(2)}, u32[]{:S(2)}) collective-permute-start(bf16[512,2048]{1,0:T(8,128)(2,1)S(1)} %collective-permute-done.31.refs_1_), channel_id=1, source_target_pairs={{0,2},{2,0},{4,6},{6,4},{8,10},{10,8},{12,14},{14,12},{16,18},{18,... | collective-permute-start | bytes 6291464 | tf_op jit(solution)/shard_map/ppermute | solution.py:75
  (66 other events, 615.9 us)
Sparse Core Ops, SparseCore 0:
  69.8 122.0 reduce-scatter.2
  236.3 78.7 all-gather.2
  326.6 91.1 reduce-scatter.4
  436.0 99.8 all-gather.4

commit v3 on v2

--- a/solution.py
+++ b/solution.py
@@ -205,52 +205,47 @@
             self.send()
 
 
-def two_pieces(value, first):
-    return [value, swap(value, *first)]
-
-
-def four_pieces(value, first, second):
-    beside = swap(value, *second)
-    return [value, beside, swap(value, *first), swap(beside, *first)]
-
-
-def assemble(order, pieces, blocks, places, outs, out_block, index, inside, splits, name):
+def assemble(order, pieces, whose, blocks, places, out_shape, out_block, index, inside, splits, name, before=None):
     rows, cols = pieces[0].shape
     chunk, part = rows // blocks, cols // splits
     count = len(pieces)
 
     def kernel(ids, *refs):
-        ins, out_refs = refs[:count], refs[count:]
-        piece = pl.program_id(0)
-
-        def copy(ref, out):
+        out = refs[-1]
+        number = pl.program_id(0)
+
+        def copy(ref):
             for r in range(blocks):
                 row, col = inside(r ^ ids[1])
                 out[pl.ds(pl.multiple_of(row, 8), chunk), pl.ds(pl.multiple_of(col, 128), part)] = ref[
                     r * chunk : (r + 1) * chunk, :
                 ].astype(wide)
 
-        for p, ref in enumerate(ins):
-            for o, out in enumerate(out_refs):
-                here = piece == p
-                if len(out_refs) > 1:
-                    here = here & ((p ^ ids[0]) == o)
-                pl.when(here)(partial(copy, ref, out))
-
-    def piece_spec(p):
+        for n, ref in enumerate(refs[:count]):
+            pl.when(number == n)(partial(copy, ref))
+
+    def piece_spec(n):
         return pl.BlockSpec(
-            (rows, part), lambda i, j, ids: (0, jnp.where(i == p, j, jnp.where(i < p, 0, splits - 1)))
+            (rows, part), lambda i, j, ids: (0, jnp.where(i == n, j, jnp.where(i < n, 0, splits - 1)))
         )
 
+    def out_index(i, j, ids):
+        outer_place = whose[0]
+        for n, place in enumerate(whose[1:]):
+            outer_place = jnp.where(i == n + 1, place, outer_place)
+        return index(outer_place ^ ids[0], j)
+
+    more = [] if before is None else [before]
     return order.call(
         kernel,
         name,
         places,
-        pieces,
+        list(pieces) + more,
         (count, splits),
-        [piece_spec(p) for p in range(count)],
-        [pl.BlockSpec(out_block, lambda i, j, ids: index(i ^ ids[0], j))] * len(outs),
-        [shape(*out, wide) for out in outs],
+        [piece_spec(n) for n in range(count)] + [pl.BlockSpec(memory_space=pl.ANY)] * len(more),
+        pl.BlockSpec(out_block, out_index),
+        shape(*out_shape, wide),
+        aliases=[(count, 0)] if more else [],
     )
 
 
@@ -265,7 +260,7 @@
     return order.call(kernel, name, [0], [value], (steps,), [at], at, shape(rows, cols, wide))
 
 
-def widen_heads(order, gathered, chunk, extra, width, cols, name):
+def widen_heads(order, gathered, chunk, extra, width, cols, name, after):
     arrays = 4
     rows = gathered.shape[0] // arrays
     count = rows // (chunk + extra)
@@ -289,6 +284,7 @@
         [pl.BlockSpec((rows, cols), lambda i, ids: (i, 0))],
         [whole(width, width)] * arrays,
         [shape(width, width, wide)] * arrays,
+        after=after,
     )
 
 
@@ -343,17 +339,19 @@
     return tiles
 
 
+def turned(values):
+    order = 7 - lax.broadcasted_iota(jnp.int32, (8, values.shape[1]), 0)
+    parts = [jnp.take_along_axis(values[at : at + 8], order, 0) for at in range(0, values.shape[0], 8)]
+    return jnp.concatenate(parts, 0)
+
+
 def unskew(grid, tile, cols, pad):
     parts = []
-    for group in range(tile // 8):
-        shift = tile - 1 + pad - 8 * group - 7
-        rows = grid[8 * group : 8 * group + 8]
-        parts.append(pltpu.roll(rows, shift, 1) if shift else rows)
-    moved = jnp.concatenate(parts, 0)
-    left = 7 - (lax.broadcasted_iota(jnp.int32, (tile, cols), 0) & 7)
-    for bit in range(3):
-        moved = jnp.where((left & (1 << bit)) != 0, pltpu.roll(moved, 1 << bit, 1), moved)
-    return moved
+    order = 7 - lax.broadcasted_iota(jnp.int32, (8, cols), 0)
+    for at in range(0, tile, 8):
+        rows = jnp.take_along_axis(grid[at : at + 8], order, 0)
+        parts.append(pltpu.roll(rows, tile - 1 + pad - at - 7, 1, stride=1, stride_axis=0))
+    return jnp.concatenate(parts, 0)
 
 
 def spans(parts, here):
@@ -470,13 +468,13 @@
         d_low = d_scores.astype(narrow)
         d_table = unskew(d_scores, TILE, cols, pad).astype(narrow)
         d_content = dot(d_low, ks[0:cols, :], 1, 0)
-        d_position = dot(d_table, rel[base : base + cols, :], 1, 0)
+        d_position = turned(dot(d_table, rel[base : base + cols, :], 1, 0))
         grad_u += jnp.sum(d_content, 0, keepdims=True)
         grad_v += jnp.sum(d_position, 0, keepdims=True)
         dqs[rows, :] = ((d_content + d_position) * scale).astype(narrow)
         d_key = dot(qc, d_low, 0, 0)
         d_value = dot(d_out, probs, 0, 0)
-        d_rel = dot(qp, d_table, 0, 0)
+        d_rel = dot(turned(qp.astype(wide)).astype(narrow), d_table, 0, 0)
         if step == 0:
             key_sum[...] = d_key
             value_sum[...] = d_value
@@ -636,31 +634,49 @@
     )
 
 
-def outer_pair(order, l_own, l_far, r_own, r_far, which, name, after=()):
-    count, units, cols = l_own[0].shape[0], l_own[2], r_own[2]
-    rows = units // 2
-    block = 256 if rows % 256 == 0 else rows
-    steps = rows // block
-
-    def kernel(ids, lo, lf, ro, rf, out):
-        out[...] = (dot(lo[...], ro[...], 0, 0) + dot(lf[...], rf[...], 0, 0)).astype(narrow)
-
-    def left(first):
-        return pl.BlockSpec((count, block), lambda i, ids: (0, first // block + ids[0] * steps + i))
-
-    def right(first):
-        return pl.BlockSpec((count, cols), lambda i, ids: (0, first // cols))
+def outer_pairs(order, jobs, whichs, name, after=()):
+    arrays, in_specs, out_specs, out_shape, spans_of = [], [], [], [], []
+    step = 0
+    for number, job in enumerate(jobs):
+        rows, cols = job[0][2] // 2, job[2][2]
+        block = min(rows, 512)
+        first, steps = step, rows // block
+        step += steps
+        spans_of.append((first, steps))
+
+        def at(i, first=first, steps=steps):
+            return jnp.clip(i - first, 0, steps - 1)
+
+        for array, column, _ in job[:2]:
+            arrays.append(array)
+            in_specs.append(
+                pl.BlockSpec(
+                    (array.shape[0], block),
+                    lambda i, ids, n=number, c=column // block, steps=steps, at=at: (0, c + ids[n] * steps + at(i)),
+                )
+            )
+        for array, column, _ in job[2:]:
+            arrays.append(array)
+            in_specs.append(pl.BlockSpec((array.shape[0], cols), lambda i, ids, c=column // cols: (0, c)))
+        out_specs.append(pl.BlockSpec((block, cols), lambda i, ids, at=at: (at(i), 0)))
+        out_shape.append(shape(rows, cols))
+
+    def kernel(ids, *refs):
+        number = pl.program_id(0)
+        for n, (first, steps) in enumerate(spans_of):
+
+            def run(n=n):
+                lo, lf, ro, rf = refs[4 * n : 4 * n + 4]
+                total = dot(lo[...], ro[...], 0, 0) + dot(lf[...], rf[...], 0, 0)
+                refs[4 * len(jobs) + n][...] = total.astype(narrow)
+
+            if len(jobs) == 1:
+                run()
+            else:
+                pl.when((number >= first) & (number < first + steps))(run)
 
     return order.call(
-        kernel,
-        name,
-        [which],
-        [l_own[0], l_far[0], r_own[0], r_far[0]],
-        (steps,),
-        [left(l_own[1]), left(l_far[1]), right(r_own[1]), right(r_far[1])],
-        pl.BlockSpec((block, cols), lambda i, ids: (i, 0)),
-        shape(rows, cols),
-        after=after,
+        kernel, name, whichs, arrays, (step,), in_specs, out_specs, out_shape, after=after
     )
 
 
@@ -868,7 +884,7 @@
     grad_b_comp = jnp.sum(cot_comp.astype(wide), 0)
     grad_comp = outer(windows, cot_comp).astype(narrow)
 
-    sinus = sinus_table()
+    sinus = gate(order, sinus_table())
     relative = matmul(sinus, lax.dynamic_slice_in_dim(w_rel, here * cols, cols, 1)).astype(narrow)
 
     own_seg, own_mem, own_comp, q_own = project(
@@ -920,14 +936,14 @@
     units = gelu_mine.shape[1]
     jobs = (
         ("grad_down", near + [blk] + rest, (gelu_mine, 0, units), (gelu_mate, 0, units), (cot_out, 0, width), (cot_mate, 0, width)),
-        ("grad_up", [blk] + near + rest, (packed, 0, width), (packed_mate, 0, width), (d_pre_mine, 0, units), (d_pre_mate, 0, units)),
-        ("grad_out", rest + near + [blk], (attended_keep, 0, cols), (packed_mate, 2 * width, cols), (packed, width, width), (packed_mate, width, width)),
-    )
-    send = [
-        outer_pair(order, *job[2:], 1 - side(*job[1][0]), job[0], after=[da_far] if job is jobs[1] else [])
-        for job in jobs
-    ]
-    keep = [outer_pair(order, *job[2:], side(*job[1][0]), job[0]) for job in jobs]
+        ("grad_up", [blk] + rest[:1] + near + rest[1:], (packed, 0, width), (packed_mate, 0, width), (d_pre_mine, 0, units), (d_pre_mate, 0, units)),
+        ("grad_out", rest[:1] + near + rest[1:] + [blk], (attended_keep, 0, cols), (packed_mate, 2 * width, cols), (packed, width, width), (packed_mate, width, width)),
+    )
+    send, keep = [], []
+    for job in jobs:
+        after = [da_far] if job is jobs[1] else []
+        send += outer_pairs(order, [job[2:]], [1 - side(*job[1][0])], job[0], after)
+    keep = outer_pairs(order, [job[2:] for job in jobs], [side(*job[1][0]) for job in jobs], "grad_keep")
     middle_steps = [job[1] for job in jobs]
     middle_sum = Scatter(order, "sum_middle", list(zip(send, keep, middle_steps)))
 
@@ -979,19 +995,16 @@
         order, here, dq_own, dq_far, d_key, d_value, w_query, w_key, w_value, block
     )
     middle_sum.step()
-    d_normed_received = swap(gate(order, d_normed_far), *blk)
     middle_gather = Gather(
         order, "join_middle", [(share, steps[1:]) for share, steps in zip(middle_sum.keep, middle_steps)]
     )
     middle_gather.step()
+    d_normed_received = swap(gate(order, d_normed_far), *blk)
+    full_comp = widen(order, comp_gathered, "full_comp")
     d_segment = finish(order, segment, d_hidden, d_normed_own, d_normed_received, first_gain)
-    full_comp = widen(order, comp_gathered, "full_comp")
     middle_gather.step()
     heads_gathered = lax.all_gather(gate(order, heads_share), ("dp", "blk"), axis=0, tiled=True)
     middle_gather.step()
-    down_pieces, up_pieces, out_pieces = (
-        four_pieces(value, core, steps[0]) for value, steps in zip(middle_gather.values, middle_steps)
-    )
     sums = heads_gathered[:, chunk : chunk + per].astype(wide).reshape(shares, blocks, per, cols)
     sums = jnp.sum(sums, 1).reshape(shares * per, cols)
     small = sum(vector.shape[0] for vector in vectors) // cols
@@ -1003,46 +1016,58 @@
         at += vector.shape[0]
 
     devices = 2 << count
-
-    def gathered(share, steps):
-        return four_pieces(gather_rows(share, steps[1:]), core, steps[0])
-
-    def by_rows(pieces, outer, inner, total_rows, name):
-        blocks = 1 << len(inner)
-        chunk = total_rows // len(pieces) // blocks
-        (out,) = assemble(
+    up_rows = width * 2 // devices
+    down_value, up_value, out_value = middle_gather.values
+    down_beside, up_beside, out_beside = (
+        swap(value, *steps[0]) for value, steps in zip(middle_gather.values, middle_steps)
+    )
+
+    def by_rows(pieces, whose, steps, total_rows, name, before=None):
+        blocks = devices // 4
+        chunk = total_rows // devices
+        return assemble(
             order,
             pieces,
+            whose,
             blocks,
-            [place_of(outer), place_of(inner)],
-            [(total_rows, width)],
-            (total_rows // len(pieces), width // 2),
+            [place_of([core, steps[0]]), place_of(steps[1:])],
+            (total_rows, width),
+            (total_rows // 4, width // 2),
             lambda outer_place, part: (outer_place, part),
             lambda inner_place: (inner_place * chunk, 0),
             2,
             name,
+            before,
         )
-        return out
-
-    full_out = by_rows(out_pieces, [core, middle_steps[2][0]], middle_steps[2][1:], width, "full_out")
-    full_down = by_rows(down_pieces, [core, middle_steps[0][0]], middle_steps[0][1:], FF, "full_down")
-    up_rows = width * 2 // devices
-    (full_up,) = assemble(
-        order,
-        up_pieces,
-        devices // 4,
-        [place_of([core, middle_steps[1][0]]), place_of(middle_steps[1][1:])],
-        [(width, FF)],
-        (width // 2, FF // 4),
-        lambda outer_place, part: (outer_place % 2, outer_place // 2 * 2 + part),
-        lambda inner_place: (inner_place * up_rows, 0),
-        2,
-        "full_up",
-    )
+
+    def up_out(pieces, whose, before=None):
+        return assemble(
+            order,
+            pieces,
+            whose,
+            devices // 4,
+            [place_of([core, middle_steps[1][0]]), place_of(middle_steps[1][1:])],
+            (width, FF),
+            (width // 2, FF // 4),
+            lambda outer_place, part: (outer_place % 2, outer_place // 2 * 2 + part),
+            lambda inner_place: (inner_place * up_rows, 0),
+            2,
+            "full_up",
+            before,
+        )
+
+    full_down = by_rows([down_value, swap(down_value, *core)], (0, 2), middle_steps[0], FF, "full_down")
+    full_up = up_out([up_value, swap(up_value, *core)], (0, 2))
+    out_beside = gate(order, out_beside)
+    out_pieces = [out_value, out_beside, swap(out_value, *core), swap(out_beside, *core)]
+    full_out = by_rows(out_pieces, (0, 1, 2, 3), middle_steps[2], width, "full_out")
+    down_beside, up_beside = gate(order, down_beside, up_beside)
+    down_far, up_far = swap(down_beside, *core), swap(up_beside, *core)
     full_query, full_key, full_value, full_rel = widen_heads(
-        order, heads_gathered.reshape(-1, cols), chunk, extra, width, cols, "full_heads"
-    )
-
+        order, heads_gathered.reshape(-1, cols), chunk, extra, width, cols, "full_heads", [sums]
+    )
+    full_down = by_rows([down_beside, down_far], (1, 3), middle_steps[0], FF, "full_down", full_down)
+    full_up = up_out([up_beside, up_far], (1, 3), full_up)
     return (
         layer_out[None],
         d_segment[None],

time: 624 us -> 571 us (0.915)
  waiting for transfers between devices: 211 us -> 171 us
  Pallas kernels: 287 us -> 271 us
    ppermute x40, waiting for transfers between devices: 211 us -> 148 us  [swap(): return lax.ppermute(value, axis, pairs)]
    pallas_call x34 -> x37, Pallas kernels: 287 us -> 271 us  [call(): pl.pallas_call(body, grid_spec=pltpu.PrefetchScalarGridSpec(num_scalar_pr...]
    reduce_scatter x1, waiting for transfers between devices: 0.01 us -> 15.1 us  [on_device(): heads_share = lax.psum_scatter(grads, 'dp', scatter_dimension=0, tiled=True)]
    all_gather x1, waiting for transfers between devices: 0.01 us -> 7.05 us  [on_device(): lax.all_gather(gate(order, heads_share), ('dp', 'blk'), axis=0, tiled=True)]
    unnamed x126 -> x132, local copies, waits for them, and re-layouts: 15.4 us -> 20.1 us
  transfers between devices with their start and end apart: 44 -> 44, of which waited for: 19 -> 21; matrix products, arithmetic and copies ran while one was open for 7% -> 8% of each run, Pallas kernels for 44% -> 46%
where the time goes in v3:
time: 571 us; the launch traced here: 562 us
  Pallas kernels  271 us (47%)
  waiting for transfers between devices  171 us (30%)
  starting transfers between devices  44.1 us (8%)
  local copies, waits for them, and re-layouts  29.5 us (5%)
  other arithmetic  17.2 us (3%)
  between operations  15.6 us (3%)
  matrix products  13.9 us (2%)
    pallas_call x37, Pallas kernels, call(): pl.pallas_call(body, grid_spec=pltpu.PrefetchScalarGridSpec(num_scalar_pr...  271 us
    ppermute x40, waiting for transfers between devices, swap(): return lax.ppermute(value, axis, pairs)  148 us
    ppermute x40, starting transfers between devices, swap(): return lax.ppermute(value, axis, pairs)  43.5 us
    unnamed x132, local copies, waits for them, and re-layouts  20.1 us
    reduce_scatter x1, waiting for transfers between devices, on_device(): heads_share = lax.psum_scatter(grads, 'dp', scatter_dimension=0, tiled=True)  15.1 us
  transfers between devices with their start and end apart: 44, of which 21 were waited for; matrix products, arithmetic and copies ran while one was open for 8% of the time, Pallas kernels for 46%

profile of v3, /device:TPU:0, one launch (start us, length us, event | category | flops | bytes accessed | tf_op | source)
XLA Modules:
  0.0 561.7 jit_solution(5388694875921362574)
XLA Ops:
  21.3 7.2 %project.3 = (bf16[480,1024]{1,0:T(8,128)(2,1)}, bf16[480,512]{1,0:T(8,128)(2,1)}, bf16[480,512]{1,0:T(8,128)(2,1)}, bf16[480,1024]{1,0:T(8,128)(2,1)}, bf16[480...) custom-call(s32[1]{0:T(128)} %bitcast.scalar_ref, ...), custom_call_target="tpu_custom_call" | custom-call | flops 1000 | bytes 1000 | tf_op jit(solution)/shard_map/project/pallas_call | solution.py:52
  42.4 5.3 project.4
  47.7 17.0 %collective-permute-done.1.refs_0_ = bf16[736,1024]{1,0:T(8,128)(2,1)} collective-permute-done((bf16[736,1024]{1,0:T(8,128)(2,1)}, bf16[736,1024]{1,0:T(8,128)(2,1)}, u32[]{:S(2)}, u32[]{:S(2)}) %collective-permute-start.1) | collective-permute-done | bytes 1507360 | tf_op jit(solution)/shard_map/ppermute | solution.py:75
  72.2 17.5 %attend.2 = (bf16[480,256]{1,0:T(8,128)(2,1)}, bf16[480,256]{1,0:T(8,128)(2,1)}, bf16[2,960,2432]{2,1,0:T(8,128)(2,1)}) custom-call(s32[2]{0:T(128)} %pad_add_fusion.1.scalar_ref, f32[480,512]{1,0:T(8,128)} %get-tuple-element.129.refs_9_.refs_0_.refs_1_, f32[480,512]{1,0:T(8,128)} %get-tuple-element.130.refs_6_.refs_1_.refs_2_, ...), custom_call_target="tpu_custom_call" | custom-call | flops 1000 | bytes 1000 | tf_op jit(solution)/shard_map/attend/pallas_call | solution.py:52
  89.8 18.0 %attend.3 = (bf16[480,256]{1,0:T(8,128)(2,1)}, bf16[480,256]{1,0:T(8,128)(2,1)}, bf16[2,960,2432]{2,1,0:T(8,128)(2,1)}) custom-call(s32[2]{0:T(128)} %pad_add_fusion.1.scalar_ref, f32[480,512]{1,0:T(8,128)} %get-tuple-element.129.refs_9_.refs_0_.refs_1_, f32[480,512]{1,0:T(8,128)} %get-tuple-element.130.refs_6_.refs_1_.refs_2_, ...), custom_call_target="tpu_custom_call" | custom-call | flops 1000 | bytes 1000 | tf_op jit(solution)/shard_map/attend/pallas_call | solution.py:52
  121.1 32.9 %middle.1 = (bf16[480,1024]{1,0:T(8,128)(2,1)}, bf16[480,2560]{1,0:T(8,128)(2,1)}, bf16[480,512]{1,0:T(8,128)(2,1)}, bf16[480,2048]{1,0:T(8,128)(2,1)}, bf16[480...) custom-call(s32[2]{0:T(128)} %pad_add_fusion.scalar_ref, ...), custom_call_target="tpu_custom_call" | custom-call | flops 1000 | bytes 1000 | tf_op jit(solution)/shard_map/middle/pallas_call | solution.py:52
  156.5 7.9 %collective-permute-done.6.refs_3_ = bf16[480,1024]{1,0:T(8,128)(2,1)} collective-permute-done((bf16[480,1024]{1,0:T(8,128)(2,1)S(1)}, bf16[480,1024]{1,0:T(8,128)(2,1)}, u32[]{:S(2)}, u32[]{:S(2)}) %collective-permute-start.6) | collective-permute-done | bytes 983072 | tf_op jit(solution)/shard_map/ppermute | solution.py:75
  164.4 5.4 grad_down.1.refs_5_
  172.7 6.2 %grad_up.1.refs_4_ = bf16[512,2048]{1,0:T(8,128)(2,1)} custom-call(s32[1]{0:T(128)} %bitcast.18.scalar_ref, bf16[480,2560]{1,0:T(8,128)(2,1)} %get-tuple-element.155.refs_0_.refs_2_.refs_4_.refs_10_, bf16[480,2560]{1,0:T(8,128)(2,1)} %copy-done.2, bf16[480,2048]{1,0:T(8,128)(2,1)} %get-tuple-element.156.refs_2_.refs_6_, ...), custom_call_target="tpu_custom_call" | custom-call | flops 1000 | bytes 1000 | tf_op jit(solution)/shard_map/grad_up/pallas_call | solution.py:52
  186.5 13.2 %grad_keep.1 = (bf16[1024,1024]{1,0:T(8,128)(2,1)}, bf16[512,2048]{1,0:T(8,128)(2,1)}, bf16[256,1024]{1,0:T(8,128)(2,1)}) custom-call(s32[3]{0:T(128)} %pad_add_fusion.2.scalar_ref, bf16[480,2048]{1,0:T(8,128)(2,1)} %get-tuple-element.153.refs_0_, bf16[480,2048]{1,0:T(8,128)(2,1)} %collective-permute-done.5.refs_1_, bf16[480,1024]{1,0:T(8,128)(2,1)} %bitcast.84, ...), custom_call_target="tpu_custom_call" | custom-call | flops 1000 | bytes 1000 | tf_op jit(solution)/shard_map/grad_keep/pallas_call | solution.py:52
  199.6 21.0 %attend_back.2 = (bf16[480,256]{1,0:T(8,128)(2,1)}, bf16[480,256]{1,0:T(8,128)(2,1)}, bf16[2432,256]{1,0:T(8,128)(2,1)}, bf16[2432,256]{1,0:T(8,128)(2,1)}, bf16...) custom-call(s32[1]{0:T(128)} %bitcast.scalar_ref, ...), custom_call_target="tpu_custom_call" | custom-call | flops 1000 | bytes 1000 | tf_op jit(solution)/shard_map/attend_back/pallas_call | solution.py:52
  220.7 5.9 %collective-permute-done.10.refs_5_.refs_7_ = bf16[512,2048]{1,0:T(8,128)(2,1)S(1)} collective-permute-done((bf16[512,2048]{1,0:T(8,128)(2,1)}, bf16[512,2048]{1,0:T(8,128)(2,1)S(1)}, u32[]{:S(2)}, u32[]{:S(2)}) %collective-permute-start.10) | collective-permute-done | bytes 2097184 | tf_op jit(solution)/shard_map/ppermute | solution.py:75
  227.9 6.9 %sum_middle.4 = (bf16[512,1024]{1,0:T(8,128)(2,1)}, bf16[512,1024]{1,0:T(8,128)(2,1)}, bf16[256,2048]{1,0:T(8,128)(2,1)}, bf16[256,2048]{1,0:T(8,128)(2,1)}, bf1...) custom-call(s32[3]{0:T(128)} %pad_add_fusion.3.scalar_ref, bf16[1024,1024]{1,0:T(8,128)(2,1)} %get-tuple-element.162.refs_0_.refs_2_, ...), custom_call_target="tpu_custom_call" | custom-call | flops 1000 | bytes 1000 | tf_op jit(solution)/shard_map/sum_middle/pallas_call | solution.py:52
  239.3 20.9 %attend_back.3 = (bf16[480,256]{1,0:T(8,128)(2,1)}, bf16[480,256]{1,0:T(8,128)(2,1)}, bf16[2432,256]{1,0:T(8,128)(2,1)}, bf16[2432,256]{1,0:T(8,128)(2,1)}, bf16...) custom-call(s32[1]{0:T(128)} %bitcast.scalar_ref, ...), custom_call_target="tpu_custom_call" | custom-call | flops 1000 | bytes 1000 | tf_op jit(solution)/shard_map/attend_back/pallas_call | solution.py:52
  260.8 5.7 %collective-permute-done.13.refs_5_.refs_7_ = bf16[256,2048]{1,0:T(8,128)(2,1)S(1)} collective-permute-done((bf16[256,2048]{1,0:T(8,128)(2,1)}, bf16[256,2048]{1,0:T(8,128)(2,1)S(1)}, u32[]{:S(2)}, u32[]{:S(2)}) %collective-permute-start.13) | collective-permute-done | bytes 1048608 | tf_op jit(solution)/shard_map/ppermute | solution.py:75
  278.6 21.4 %grad_heads.1 = (bf16[4352,512]{1,0:T(8,128)(2,1)}, f32[1024,1]{1,0:T(8,128)}, f32[1024,1]{1,0:T(8,128)}) custom-call(s32[1]{0:T(128)} %bitcast.scalar_ref, bf16[256,1024]{1,0:T(8,128)(2,1)} %get-tuple-element.173.refs_0_, bf16[480,1024]{1,0:T(8,128)(2,1)} %get-tuple-element.174.refs_1_, bf16[480,1024]{1,0:T(8,128)(2,1)} %get-tuple-element.175.refs_2_, ...), custom_call_target="tpu_custom_call" | custom-call | flops 1000 | bytes 1000 | tf_op jit(solution)/shard_map/grad_heads/pallas_call | solution.py:52
  312.9 8.2 %segment_back.1 = (f32[480,1024]{1,0:T(8,128)}, bf16[480,1024]{1,0:T(8,128)(2,1)}) custom-call(s32[1]{0:T(128)} %bitcast.scalar_ref, bf16[480,256]{1,0:T(8,128)(2,1)} %get-tuple-element.161.refs_7_.refs_0_, bf16[480,256]{1,0:T(8,128)(2,1)} %get-tuple-element.166.refs_8_.refs_1_, bf16[480,256]{1,0:T(8,128)(2,1)} %get-tuple-element.167.refs_9_.refs_2_, ...), custom_call_target="tpu_custom_call" | custom-call | flops 1000 | bytes 1000 | tf_op jit(solution)/shard_map/segment_back/pallas_call | solution.py:52
  340.7 11.7 %collective-permute-done.21.refs_1_ = bf16[128,1024]{1,0:T(8,128)(2,1)S(1)} collective-permute-done((bf16[128,1024]{1,0:T(8,128)(2,1)}, bf16[128,1024]{1,0:T(8,128)(2,1)S(1)}, u32[]{:S(2)}, u32[]{:S(2)}) %collective-permute-start.21) | collective-permute-done | bytes 262176 | tf_op jit(solution)/shard_map/ppermute | solution.py:75
  352.4 5.6 collective-permute-done.22.refs_3_
  367.2 7.8 %full_comp.1.refs_5_ = f32[3072,1024]{1,0:T(8,128)} custom-call(s32[1]{0:T(128)} %constant.6.clone.1.scalar_ref, bf16[3072,1024]{1,0:T(8,128)(2,1)} %all-gather.3.cloned.1.call-done.refs_0_, bf16[480,1024]{1,0:T(8,128)(2,1)} %gate.12.refs_1_), custom_call_target="tpu_custom_call" | custom-call | flops 1000 | bytes 1000 | tf_op jit(solution)/shard_map/full_comp/pallas_call | solution.py:52
  375.0 9.8 %collective-permute-done.24.refs_3_ = bf16[480,1024]{1,0:T(8,128)(2,1)S(1)} collective-permute-done((bf16[480,1024]{1,0:T(8,128)(2,1)}, bf16[480,1024]{1,0:T(8,128)(2,1)S(1)}, u32[]{:S(2)}, u32[]{:S(2)}) %collective-permute-start.24) | collective-permute-done | bytes 983072 | tf_op jit(solution)/shard_map/ppermute | solution.py:75
  395.4 15.1 %reduce-scatter.5.cloned.1.call-done.refs_0_ = bf16[1,272,512]{2,1,0:T(8,128)(2,1)} async-done(((bf16[16,272,512]{2,1,0:T(8,128)(2,1)}), bf16[1,272,512]{2,1,0:T(8,128)(2,1)}) %reduce-scatter.5.cloned.1.call-update) | async-done | bytes 278544 | tf_op jit(solution)/shard_map/reduce_scatter | solution.py:992
  414.5 5.2 collective-permute-done.30.refs_5_
  419.7 17.1 %collective-permute-done.28.refs_1_ = bf16[512,1024]{1,0:T(8,128)(2,1)S(1)} collective-permute-done((bf16[512,1024]{1,0:T(8,128)(2,1)}, bf16[512,1024]{1,0:T(8,128)(2,1)S(1)}, u32[]{:S(2)}, u32[]{:S(2)}) %collective-permute-start.28) | collective-permute-done | bytes 1048608 | tf_op jit(solution)/shard_map/ppermute | solution.py:75
  452.1 7.1 %full_down.2.refs_2_ = f32[4096,1024]{1,0:T(8,128)} custom-call(s32[2]{0:T(128)} %pad_add_fusion.8.scalar_ref, bf16[1024,1024]{1,0:T(8,128)(2,1)} %get-tuple-element.221.refs_0_, bf16[1024,1024]{1,0:T(8,128)(2,1)} %collective-permute-done.35.refs_1_, bf16[256,1024]{1,0:T(8,128)(2,1)} %get-tuple-element.223.refs_2_.refs_0_), custom_call_target="tpu_custom_call" | custom-call | flops 1000 | bytes 1000 | tf_op jit(solution)/shard_map/full_down/pallas_call | solution.py:52
  459.2 7.0 %full_up.2.refs_1_.refs_2_ = f32[1024,4096]{1,0:T(8,128)} custom-call(s32[2]{0:T(128)} %pad_add_fusion.7.scalar_ref, bf16[512,2048]{1,0:T(8,128)(2,1)} %get-tuple-element.222.refs_0_, bf16[512,2048]{1,0:T(8,128)(2,1)} %collective-permute-done.34.refs_1_, f32[4096,1024]{1,0:T(8,128)} %full_down.2.refs_2_), custom_call_target="tpu_custom_call" | custom-call | flops 1000 | bytes 1000 | tf_op jit(solution)/shard_map/full_up/pallas_call | solution.py:52
  472.2 7.1 %full_out.1.refs_2_ = f32[1024,1024]{1,0:T(8,128)} custom-call(s32[2]{0:T(128)} %pad_add_fusion.6.scalar_ref, bf16[256,1024]{1,0:T(8,128)(2,1)} %get-tuple-element.223.refs_2_.refs_0_, bf16[256,1024]{1,0:T(8,128)(2,1)} %gate.14.refs_1_.refs_4_, bf16[256,1024]{1,0:T(8,128)(2,1)} %copy-done.22, bf16[256,1024]{1,0:T(8,128)(2,1)} %copy-done.23, ...), custom_call_target="tpu_custom_call" | custom-call | flops 1000 | bytes 1000 | tf_op jit(solution)/shard_map/full_out/pallas_call | solution.py:52
  479.3 33.3 %collective-permute-done.31.refs_0_ = bf16[1024,1024]{1,0:T(8,128)(2,1)S(1)} collective-permute-done((bf16[1024,1024]{1,0:T(8,128)(2,1)}, bf16[1024,1024]{1,0:T(8,128)(2,1)S(1)}, u32[]{:S(2)}, u32[]{:S(2)}) %collective-permute-start.31) | collective-permute-done | bytes 2097184 | tf_op jit(solution)/shard_map/ppermute | solution.py:75
  514.4 7.0 %all-gather.5.cloned.1.call-done = bf16[32,272,512]{2,1,0:T(8,128)(2,1)} async-done(((bf16[1,272,512]{2,1,0:T(8,128)(2,1)}), bf16[32,272,512]{2,1,0:T(8,128)(2,1)}) %all-gather.5.cloned.1.call-update) | async-done | bytes 8912912 | tf_op jit(solution)/shard_map/all_gather | solution.py:1006
  523.2 10.6 %full_heads.1 = (f32[1024,1024]{1,0:T(8,128)}, f32[1024,1024]{1,0:T(8,128)}, f32[1024,1024]{1,0:T(8,128)}, f32[1024,1024]{1,0:T(8,128)}) custom-call(s32[1]{0:T(128)} %constant.6.clone.1.scalar_ref, bf16[8704,512]{1,0:T(8,128)(2,1)} %bitcast.79, f32[12288]{0:T(1024)} %add.74.refs_1_, bf16[512,2048]{1,0:T(8,128)(2,1)} %get-tuple-element.224.refs_2_.refs_0_), custom_call_target="tpu_custom_call" | custom-call | flops 1000 | bytes 1000 | tf_op jit(solution)/shard_map/full_heads/pallas_call | solution.py:52
  535.1 7.0 %full_down.3.refs_3_ = f32[4096,1024]{1,0:T(8,128)} custom-call(s32[2]{0:T(128)} %pad_add_fusion.8.scalar_ref, bf16[1024,1024]{1,0:T(8,128)(2,1)} %get-tuple-element.229.refs_0_, bf16[1024,1024]{1,0:T(8,128)(2,1)} %copy-done.9, f32[4096,1024]{1,0:T(8,128)} %full_down.2.refs_2_, f32[1024,1024]{1,0:T(8,128)} %get-tuple-element.113.refs_3_), custom_call_target="tpu_custom_call", output_to_operand_aliasing={{}: (3, {})} | custom-call | flops 1000 | bytes 1000 | tf_op jit(solution)/shard_map/full_down/pallas_call | solution.py:52
  547.5 7.2 %full_up.3 = f32[1024,4096]{1,0:T(8,128)} custom-call(s32[2]{0:T(128)} %pad_add_fusion.7.scalar_ref, bf16[512,2048]{1,0:T(8,128)(2,1)} %get-tuple-element.224.refs_2_.refs_0_, bf16[512,2048]{1,0:T(8,128)(2,1)} %collective-permute-done.38.refs_1_, f32[1024,4096]{1,0:T(8,128)} %full_up.2.refs_1_.refs_2_, ...), custom_call_target="tpu_custom_call", output_to_operand_aliasing={{}: (3, {})} | custom-call | flops 1000 | bytes 1000 | tf_op jit(solution)/shard_map/full_up/pallas_call | solution.py:52
  (278 shorter events, 167.0 us)
Async XLA Ops:
  7.2 227.5 %reduce-scatter.3.cloned.1.call-start = ((), (), s32[]{:S(2)}) async-start(), calls=%async_computation.2 | async-start | bytes 6488064 | tf_op jit(solution)/shard_map/reduce_scatter | solution.py:900
  7.3 35.1 %collective-permute-start = (bf16[480,1024]{1,0:T(8,128)(2,1)}, bf16[480,1024]{1,0:T(8,128)(2,1)}, u32[]{:S(2)}, u32[]{:S(2)}) collective-permute-start(bf16[480,1024]{1,0:T(8,128)(2,1)} %bitcast.86), channel_id=1, source_target_pairs={{0,1},{1,0},{2,3},{3,2},{4,5},{5,4},{6,7},{7,6},{8,9},{9,8},{10,11... | collective-permute-start | bytes 2949128 | tf_op jit(solution)/shard_map/ppermute | solution.py:75
  12.9 51.8 %collective-permute-start.1 = (bf16[736,1024]{1,0:T(8,128)(2,1)}, bf16[736,1024]{1,0:T(8,128)(2,1)}, u32[]{:S(2)}, u32[]{:S(2)}) collective-permute-start(bf16[736,1024]{1,0:T(8,128)(2,1)} %pad_maximum_fusion.1), channel_id=1, source_target_pairs={{0,1},{1,0},{2,3},{3,2},{4,5},{5,4},{6,7},{7,6},{8,9},{9,8},{10,11... | collective-permute-start | bytes 4521992 | tf_op jit(solution)/shard_map/ppermute | solution.py:75
  69.7 297.5 %all-gather.3.cloned.1.call-start = ((), (), s32[]{:S(2)}) async-start(), calls=%async_computation.3 | async-start | bytes 6488064 | tf_op jit(solution)/shard_map/all_gather | solution.py:955
  154.0 17.3 %collective-permute-start.7 = (bf16[480,2560]{1,0:T(8,128)(2,1)}, bf16[480,2560]{1,0:T(8,128)(2,1)S(1)}, u32[]{:S(2)}, u32[]{:S(2)}) collective-permute-start(bf16[480,2560]{1,0:T(8,128)(2,1)} %get-tuple-element.155.refs_0_.refs_2_.refs_4_.refs_10_), channel_id=1, source_target_pairs={{0,2},{2,0},{4,6},{6,4},{8,10},{10,8},{12,14},{14,12},{16,18},{18,... | collective-permute-start | bytes 7372808 | tf_op jit(solution)/shard_map/ppermute | solution.py:75
  154.6 16.7 %collective-permute-start.8 = (bf16[480,2048]{1,0:T(8,128)(2,1)}, bf16[480,2048]{1,0:T(8,128)(2,1)}, u32[]{:S(2)}, u32[]{:S(2)}) collective-permute-start(bf16[480,2048]{1,0:T(8,128)(2,1)} %get-tuple-element.157), channel_id=1, source_target_pairs={{0,2},{2,0},{4,6},{6,4},{8,10},{10,8},{12,14},{14,12},{16,18},{18,... | collective-permute-start | bytes 5898248 | tf_op jit(solution)/shard_map/ppermute | solution.py:75
  169.9 50.8 %collective-permute-start.9 = (bf16[1024,1024]{1,0:T(8,128)(2,1)}, bf16[1024,1024]{1,0:T(8,128)(2,1)}, u32[]{:S(2)}, u32[]{:S(2)}) collective-permute-start(bf16[1024,1024]{1,0:T(8,128)(2,1)} %grad_down.1.refs_5_), channel_id=1, source_target_pairs={{0,4},{2,6},{4,0},{6,2},{8,12},{10,14},{12,8},{14,10},{16,20},{18,... | collective-permute-start | bytes 6291464 | tf_op jit(solution)/shard_map/ppermute | solution.py:75
  178.9 47.6 %collective-permute-start.10 = (bf16[512,2048]{1,0:T(8,128)(2,1)}, bf16[512,2048]{1,0:T(8,128)(2,1)S(1)}, u32[]{:S(2)}, u32[]{:S(2)}) collective-permute-start(bf16[512,2048]{1,0:T(8,128)(2,1)} %grad_up.1.refs_4_), channel_id=1, source_target_pairs={{0,1},{1,0},{2,3},{3,2},{4,5},{5,4},{6,7},{7,6},{8,9},{9,8},{10,11... | collective-permute-start | bytes 6291464 | tf_op jit(solution)/shard_map/ppermute | solution.py:75
  183.8 36.9 %collective-permute-start.11 = (bf16[256,1024]{1,0:T(8,128)(2,1)}, bf16[256,1024]{1,0:T(8,128)(2,1)S(1)}, u32[]{:S(2)}, u32[]{:S(2)}) collective-permute-start(bf16[256,1024]{1,0:T(8,128)(2,1)} %grad_out.1.refs_12_), channel_id=1, source_target_pairs={{0,8},{2,10},{4,12},{6,14},{8,0},{10,2},{12,4},{14,6},{16,24},{18,... | collective-permute-start | bytes 1572872 | tf_op jit(solution)/shard_map/ppermute | solution.py:75
  234.8 175.8 %reduce-scatter.5.cloned.1.call-start = ((), (), s32[]{:S(2)}) async-start(), calls=%async_computation.4 | async-start | bytes 4734976 | tf_op jit(solution)/shard_map/reduce_scatter | solution.py:992
  235.0 25.8 %collective-permute-start.12 = (bf16[512,1024]{1,0:T(8,128)(2,1)}, bf16[512,1024]{1,0:T(8,128)(2,1)S(1)}, u32[]{:S(2)}, u32[]{:S(2)}) collective-permute-start(bf16[512,1024]{1,0:T(8,128)(2,1)} %get-tuple-element.182), channel_id=1, source_target_pairs={{0,1},{1,0},{2,3},{3,2},{4,5},{5,4},{6,7},{7,6},{8,9},{9,8},{10,11... | collective-permute-start | bytes 3145736 | tf_op jit(solution)/shard_map/ppermute | solution.py:75
  236.7 29.9 %collective-permute-start.13 = (bf16[256,2048]{1,0:T(8,128)(2,1)}, bf16[256,2048]{1,0:T(8,128)(2,1)S(1)}, u32[]{:S(2)}, u32[]{:S(2)}) collective-permute-start(bf16[256,2048]{1,0:T(8,128)(2,1)} %get-tuple-element.184), channel_id=1, source_target_pairs={{0,8},{2,10},{4,12},{6,14},{8,0},{10,2},{12,4},{14,6},{16,24},{18,... | collective-permute-start | bytes 3145736 | tf_op jit(solution)/shard_map/ppermute | solution.py:75
  238.2 22.0 %collective-permute-start.14 = (bf16[128,1024]{1,0:T(8,128)(2,1)}, bf16[128,1024]{1,0:T(8,128)(2,1)S(1)}, u32[]{:S(2)}, u32[]{:S(2)}) collective-permute-start(bf16[128,1024]{1,0:T(8,128)(2,1)} %get-tuple-element.185), channel_id=1, source_target_pairs={{0,4},{2,6},{4,0},{6,2},{8,12},{10,14},{12,8},{14,10},{16,20},{18,... | collective-permute-start | bytes 786440 | tf_op jit(solution)/shard_map/ppermute | solution.py:75
  271.9 28.6 %collective-permute-start.15 = (bf16[256,1024]{1,0:T(8,128)(2,1)}, bf16[256,1024]{1,0:T(8,128)(2,1)S(1)}, u32[]{:S(2)}, u32[]{:S(2)}) collective-permute-start(bf16[256,1024]{1,0:T(8,128)(2,1)} %get-tuple-element.192), channel_id=1, source_target_pairs={{0,8},{2,10},{4,12},{6,14},{8,0},{10,2},{12,4},{14,6},{16,24},{18,... | collective-permute-start | bytes 1572872 | tf_op jit(solution)/shard_map/ppermute | solution.py:75
  274.3 26.2 %collective-permute-start.16 = (bf16[128,2048]{1,0:T(8,128)(2,1)}, bf16[128,2048]{1,0:T(8,128)(2,1)S(1)}, u32[]{:S(2)}, u32[]{:S(2)}) collective-permute-start(bf16[128,2048]{1,0:T(8,128)(2,1)} %get-tuple-element.194), channel_id=1, source_target_pairs={{0,4},{2,6},{4,0},{6,2},{8,12},{10,14},{12,8},{14,10},{16,20},{18,... | collective-permute-start | bytes 1572872 | tf_op jit(solution)/shard_map/ppermute | solution.py:75
  274.4 26.1 %collective-permute-start.17 = (bf16[64,1024]{1,0:T(8,128)(2,1)}, bf16[64,1024]{1,0:T(8,128)(2,1)S(1)}, u32[]{:S(2)}, u32[]{:S(2)}) collective-permute-start(bf16[64,1024]{1,0:T(8,128)(2,1)} %get-tuple-element.195), channel_id=1, source_target_pairs={{0,16},{2,18},{4,20},{6,22},{8,24},{10,26},{12,28},{14,30},{16,0},... | collective-permute-start | bytes 393224 | tf_op jit(solution)/shard_map/ppermute | solution.py:75
  309.5 211.9 %all-gather.5.cloned.1.call-start = ((), (), s32[]{:S(2)}) async-start(), calls=%async_computation.5 | async-start | bytes 9191424 | tf_op jit(solution)/shard_map/all_gather | solution.py:1006
  309.9 20.6 %collective-permute-start.19 = (bf16[64,2048]{1,0:T(8,128)(2,1)S(1)}, bf16[64,2048]{1,0:T(8,128)(2,1)S(1)}, u32[]{:S(2)}, u32[]{:S(2)}) collective-permute-start(bf16[64,2048]{1,0:T(8,128)(2,1)S(1)} %copy-done.51), channel_id=1, source_target_pairs={{0,16},{2,18},{4,20},{6,22},{8,24},{10,26},{12,28},{14,30},{16,0},... | collective-permute-start | bytes 786440 | tf_op jit(solution)/shard_map/ppermute | solution.py:75
  333.3 19.1 %collective-permute-start.21 = (bf16[128,1024]{1,0:T(8,128)(2,1)}, bf16[128,1024]{1,0:T(8,128)(2,1)S(1)}, u32[]{:S(2)}, u32[]{:S(2)}) collective-permute-start(bf16[128,1024]{1,0:T(8,128)(2,1)} %get-tuple-element.205.refs_0_), channel_id=1, source_target_pairs={{0,16},{2,18},{4,20},{6,22},{8,24},{10,26},{12,28},{14,30},{16,0},... | collective-permute-start | bytes 786440 | tf_op jit(solution)/shard_map/ppermute | solution.py:75
  333.3 24.7 %collective-permute-start.22 = (bf16[64,2048]{1,0:T(8,128)(2,1)}, bf16[64,2048]{1,0:T(8,128)(2,1)S(1)}, u32[]{:S(2)}, u32[]{:S(2)}) collective-permute-start(bf16[64,2048]{1,0:T(8,128)(2,1)} %get-tuple-element.206.refs_2_), channel_id=1, source_target_pairs={{0,16},{2,18},{4,20},{6,22},{8,24},{10,26},{12,28},{14,30},{16,0},... | collective-permute-start | bytes 786440 | tf_op jit(solution)/shard_map/ppermute | solution.py:75
  360.9 23.8 %collective-permute-start.24 = (bf16[480,1024]{1,0:T(8,128)(2,1)}, bf16[480,1024]{1,0:T(8,128)(2,1)S(1)}, u32[]{:S(2)}, u32[]{:S(2)}) collective-permute-start(bf16[480,1024]{1,0:T(8,128)(2,1)} %gate.12.refs_1_), channel_id=1, source_target_pairs={{0,1},{1,0},{2,3},{3,2},{4,5},{5,4},{6,7},{7,6},{8,9},{9,8},{10,11... | collective-permute-start | bytes 2949128 | tf_op jit(solution)/shard_map/ppermute | solution.py:75
  362.3 28.5 %collective-permute-start.25 = (bf16[256,1024]{1,0:T(8,128)(2,1)}, bf16[256,1024]{1,0:T(8,128)(2,1)S(1)}, u32[]{:S(2)}, u32[]{:S(2)}) collective-permute-start(bf16[256,1024]{1,0:T(8,128)(2,1)} %get-tuple-element.216.refs_0_), channel_id=1, source_target_pairs={{0,8},{2,10},{4,12},{6,14},{8,0},{10,2},{12,4},{14,6},{16,24},{18,... | collective-permute-start | bytes 1572872 | tf_op jit(solution)/shard_map/ppermute | solution.py:75
  362.9 27.9 %collective-permute-start.26 = (bf16[128,2048]{1,0:T(8,128)(2,1)}, bf16[128,2048]{1,0:T(8,128)(2,1)S(1)}, u32[]{:S(2)}, u32[]{:S(2)}) collective-permute-start(bf16[128,2048]{1,0:T(8,128)(2,1)} %get-tuple-element.217.refs_2_), channel_id=1, source_target_pairs={{0,4},{2,6},{4,0},{6,2},{8,12},{10,14},{12,8},{14,10},{16,20},{18,... | collective-permute-start | bytes 1572872 | tf_op jit(solution)/shard_map/ppermute | solution.py:75
  362.9 27.9 %collective-permute-start.27 = (bf16[64,1024]{1,0:T(8,128)(2,1)}, bf16[64,1024]{1,0:T(8,128)(2,1)S(1)}, u32[]{:S(2)}, u32[]{:S(2)}) collective-permute-start(bf16[64,1024]{1,0:T(8,128)(2,1)} %get-tuple-element.208.refs_1_.refs_4_), channel_id=1, source_target_pairs={{0,16},{2,18},{4,20},{6,22},{8,24},{10,26},{12,28},{14,30},{16,0},... | collective-permute-start | bytes 393224 | tf_op jit(solution)/shard_map/ppermute | solution.py:75
  410.6 26.1 %collective-permute-start.28 = (bf16[512,1024]{1,0:T(8,128)(2,1)}, bf16[512,1024]{1,0:T(8,128)(2,1)S(1)}, u32[]{:S(2)}, u32[]{:S(2)}) collective-permute-start(bf16[512,1024]{1,0:T(8,128)(2,1)} %get-tuple-element.219.refs_0_), channel_id=1, source_target_pairs={{0,1},{1,0},{2,3},{3,2},{4,5},{5,4},{6,7},{7,6},{8,9},{9,8},{10,11... | collective-permute-start | bytes 3145736 | tf_op jit(solution)/shard_map/ppermute | solution.py:75
  412.1 29.7 %collective-permute-start.29 = (bf16[256,2048]{1,0:T(8,128)(2,1)}, bf16[256,2048]{1,0:T(8,128)(2,1)S(1)}, u32[]{:S(2)}, u32[]{:S(2)}) collective-permute-start(bf16[256,2048]{1,0:T(8,128)(2,1)} %get-tuple-element.220.refs_2_), channel_id=1, source_target_pairs={{0,8},{2,10},{4,12},{6,14},{8,0},{10,2},{12,4},{14,6},{16,24},{18,... | collective-permute-start | bytes 3145736 | tf_op jit(solution)/shard_map/ppermute | solution.py:75
  448.0 64.7 %collective-permute-start.31 = (bf16[1024,1024]{1,0:T(8,128)(2,1)}, bf16[1024,1024]{1,0:T(8,128)(2,1)S(1)}, u32[]{:S(2)}, u32[]{:S(2)}) collective-permute-start(bf16[1024,1024]{1,0:T(8,128)(2,1)} %get-tuple-element.221.refs_0_), channel_id=1, source_target_pairs={{0,4},{2,6},{4,0},{6,2},{8,12},{10,14},{12,8},{14,10},{16,20},{18,... | collective-permute-start | bytes 6291464 | tf_op jit(solution)/shard_map/ppermute | solution.py:75
  448.8 63.8 %collective-permute-start.32 = (bf16[512,2048]{1,0:T(8,128)(2,1)}, bf16[512,2048]{1,0:T(8,128)(2,1)}, u32[]{:S(2)}, u32[]{:S(2)}) collective-permute-start(bf16[512,2048]{1,0:T(8,128)(2,1)} %get-tuple-element.222.refs_0_), channel_id=1, source_target_pairs={{0,1},{1,0},{2,3},{3,2},{4,5},{5,4},{6,7},{7,6},{8,9},{9,8},{10,11... | collective-permute-start | bytes 6291464 | tf_op jit(solution)/shard_map/ppermute | solution.py:75
  449.6 18.8 %collective-permute-start.33 = (bf16[256,1024]{1,0:T(8,128)(2,1)}, bf16[256,1024]{1,0:T(8,128)(2,1)S(1)}, u32[]{:S(2)}, u32[]{:S(2)}) collective-permute-start(bf16[256,1024]{1,0:T(8,128)(2,1)} %get-tuple-element.223.refs_2_.refs_0_), channel_id=1, source_target_pairs={{0,8},{2,10},{4,12},{6,14},{8,0},{10,2},{12,4},{14,6},{16,24},{18,... | collective-permute-start | bytes 1572872 | tf_op jit(solution)/shard_map/ppermute | solution.py:75
  452.1 17.8 %collective-permute-start.36 = (bf16[256,1024]{1,0:T(8,128)(2,1)}, bf16[256,1024]{1,0:T(8,128)(2,1)S(1)}, u32[]{:S(2)}, u32[]{:S(2)}) collective-permute-start(bf16[256,1024]{1,0:T(8,128)(2,1)} %get-tuple-element.223.refs_2_.refs_0_), channel_id=1, source_target_pairs={{0,2},{2,0},{4,6},{6,4},{8,10},{10,8},{12,14},{14,12},{16,18},{18,... | collective-permute-start | bytes 1572872 | tf_op jit(solution)/shard_map/ppermute | solution.py:75
  513.9 19.8 %collective-permute-start.39 = (bf16[1024,1024]{1,0:T(8,128)(2,1)}, bf16[1024,1024]{1,0:T(8,128)(2,1)S(1)}, u32[]{:S(2)}, u32[]{:S(2)}) collective-permute-start(bf16[1024,1024]{1,0:T(8,128)(2,1)} %get-tuple-element.229.refs_0_), channel_id=1, source_target_pairs={{0,2},{2,0},{4,6},{6,4},{8,10},{10,8},{12,14},{14,12},{16,18},{18,... | collective-permute-start | bytes 6291464 | tf_op jit(solution)/shard_map/ppermute | solution.py:75
  513.9 33.6 %collective-permute-start.38 = (bf16[512,2048]{1,0:T(8,128)(2,1)}, bf16[512,2048]{1,0:T(8,128)(2,1)}, u32[]{:S(2)}, u32[]{:S(2)}) collective-permute-start(bf16[512,2048]{1,0:T(8,128)(2,1)} %get-tuple-element.224.refs_2_.refs_0_), channel_id=1, source_target_pairs={{0,2},{2,0},{4,6},{6,4},{8,10},{10,8},{12,14},{14,12},{16,18},{18,... | collective-permute-start | bytes 6291464 | tf_op jit(solution)/shard_map/ppermute | solution.py:75
  (69 other events, 558.9 us)
Sparse Core Ops, SparseCore 0:
  69.8 116.9 reduce-scatter.2
  234.9 75.3 all-gather.2
  315.3 95.2 reduce-scatter.4
  413.3 108.0 all-gather.4

commit v4 on v3

--- a/solution.py
+++ b/solution.py
@@ -36,6 +36,10 @@
 
 def whole(rows, cols):
     return pl.BlockSpec((rows, cols), lambda *_: (0, 0))
+
+
+def numbers(values):
+    return jnp.stack([jnp.asarray(value, jnp.int32) for value in values])
 
 
 class Order:
@@ -65,7 +69,7 @@
                 flops=1000, bytes_accessed=1000, transcendentals=0
             ),
             name=name,
-        )(jnp.stack([jnp.asarray(s, jnp.int32) for s in scalars]), *arrays, *after)
+        )(scalars if hasattr(scalars, "ndim") else numbers(scalars), *arrays, *after)
         self.last = [out[-1] if isinstance(out, (list, tuple)) else out]
         return out
 
@@ -119,7 +123,7 @@
     return order.call(
         kernel,
         name,
-        [0],
+        order.zero,
         arrays,
         (1,),
         [whole(*a.shape) for a in arrays],
@@ -133,7 +137,7 @@
     out = order.call(
         lambda ids, *refs: None,
         "gate",
-        [0],
+        order.zero,
         values,
         (1,),
         [place] * len(values),
@@ -180,7 +184,7 @@
     return order.call(
         kernel,
         name,
-        [0],
+        order.zero,
         arrays,
         (1,),
         [whole(*a.shape) for a in arrays],
@@ -260,6 +264,28 @@
     return order.call(kernel, name, [0], [value], (steps,), [at], at, shape(rows, cols, wide))
 
 
+def take_apart(order, values, lengths):
+    width = values.shape[1]
+
+    def kernel(ids, ref, *outs):
+        row = 0
+        for out, length in zip(outs, lengths):
+            for at in range(0, length, width):
+                out[at : at + width] = ref[row, :]
+                row += 1
+
+    return order.call(
+        kernel,
+        "take_apart",
+        order.zero,
+        [values],
+        (1,),
+        [whole(*values.shape)],
+        [pl.BlockSpec((length,), lambda *_: (0,)) for length in lengths],
+        [jax.ShapeDtypeStruct((length,), wide) for length in lengths],
+    )
+
+
 def widen_heads(order, gathered, chunk, extra, width, cols, name, after):
     arrays = 4
     rows = gathered.shape[0] // arrays
@@ -278,7 +304,7 @@
     return order.call(
         kernel,
         name,
-        [0],
+        order.zero,
         [gathered],
         (arrays,),
         [pl.BlockSpec((rows, cols), lambda i, ids: (i, 0))],
@@ -318,7 +344,7 @@
     out = order.call(
         partial(project_kernel, len(parts), lengths),
         "project",
-        [here],
+        order.here,
         list(parts) + [gain[None], bias[None], wq, wk, wv],
         (1,),
         [whole(*p.shape) for p in parts] + [whole(1, width)] * 2 + [weight if query else unused, weight, weight],
@@ -427,8 +453,8 @@
     return order.call(
         partial(attend_kernel, parts),
         "attend",
-        [here, start],
-        [q_own, q_far, u[None], v[None], *k_own, *k_far, *v_own, *v_far, rel],
+        order.attend,
+        [q_own, q_far, u, v, *k_own, *k_far, *v_own, *v_far, rel],
         (heads,),
         [query, query, bias, bias]
         + part_specs(parts, first) * 4
@@ -510,8 +536,8 @@
     return order.call(
         partial(attend_back_kernel, parts),
         "attend_back",
-        [here],
-        [probs, q_own, q_far, u[None], v[None], *k_own, *k_far, *v_own, *v_far, rel, da_own, da_far],
+        order.here,
+        [probs, q_own, q_far, u, v, *k_own, *k_far, *v_own, *v_far, rel, da_own, da_far],
         (heads,),
         [pl.BlockSpec((1, seg, keys), lambda h, ids: (h, 0, 0)), query, query, bias, bias]
         + part_specs(parts, first) * 4
@@ -617,8 +643,8 @@
     return order.call(
         partial(middle_kernel, len(mine), len(received)),
         "middle",
-        [here, core],
-        list(mine) + list(received) + [segment, cot, w_out, gain[None], bias[None], w_up, b_up[None], w_down, b_down[None]],
+        order.both,
+        list(mine) + list(received) + [segment, cot, w_out, gain, bias, w_up, b_up, w_down, b_down],
         (steps,),
         [whole(*a.shape) for a in list(mine) + list(received)]
         + [row, row, whole(width, width), vector, vector, up, unit, down, vector],
@@ -702,7 +728,7 @@
     return order.call(
         partial(segment_back_kernel, len(dk), block),
         "segment_back",
-        [here],
+        order.here,
         arrays + [wq, wk, wv],
         (1,),
         [whole(*a.shape) for a in arrays] + [weight] * 3,
@@ -772,7 +798,7 @@
     return order.call(
         partial(grad_heads_kernel, parts, len(dk), chunk, extra),
         "grad_heads",
-        [here],
+        order.here,
         arrays + [wq, wk, wv],
         (4,),
         [whole(*a.shape) for a in arrays] + [weight] * 3,
@@ -801,7 +827,7 @@
     return order.call(
         finish_kernel,
         "finish",
-        [0],
+        order.zero,
         arrays,
         (1,),
         [whole(*a.shape) for a in arrays],
@@ -873,6 +899,14 @@
     mate = side(*core)
 
     order = Order()
+    order.zero = jnp.zeros((1,), jnp.int32)
+    order.here, order.attend, order.both, u_row, v_row, gain_row, bias_row, up_row, down_row = gate(
+        order,
+        numbers([here]),
+        numbers([here, mem_start[0]]),
+        numbers([here, mate]),
+        *(vector[None] for vector in (u_bias, v_bias, second_gain, second_bias, b_up, b_down)),
+    )
     weights = (first_gain, first_bias, w_query, w_key, w_value)
 
     windows = memory.reshape(parts[1] // RATE, RATE * width)
@@ -898,7 +932,7 @@
     )
     own, other = (own_comp, own_mem, own_seg), (far_comp, far_mem, far_seg)
     comp_share = lax.psum_scatter(gate(order, grad_comp), ("dp", "blk"), scatter_dimension=0, tiled=True)
-    inputs = [q_own, q_far, u_bias, v_bias]
+    inputs = [q_own, q_far, u_row, v_row]
     for part in (1, 2):
         inputs += [[t[part] for t in own], [t[part] for t in other]]
     inputs += [relative]
@@ -926,7 +960,7 @@
         grad_second_bias,
         grad_b_down,
     ) = middle(
-        order, here, mate, mine, received, segment, cot_out, w_out, second_gain, second_bias, w_up, b_up, w_down, b_down
+        order, here, mate, mine, received, segment, cot_out, w_out, gain_row, bias_row, w_up, up_row, w_down, down_row
     )
 
     gelu_mate = swap(gelu_theirs, *core)
@@ -1009,11 +1043,6 @@
     sums = jnp.sum(sums, 1).reshape(shares * per, cols)
     small = sum(vector.shape[0] for vector in vectors) // cols
     sums = (sums[:small] + sums[small : 2 * small]).reshape(-1)
-    split = []
-    at = 0
-    for vector in vectors:
-        split.append(sums[at : at + vector.shape[0]])
-        at += vector.shape[0]
 
     devices = 2 << count
     up_rows = width * 2 // devices
@@ -1063,6 +1092,7 @@
     full_out = by_rows(out_pieces, (0, 1, 2, 3), middle_steps[2], width, "full_out")
     down_beside, up_beside = gate(order, down_beside, up_beside)
     down_far, up_far = swap(down_beside, *core), swap(up_beside, *core)
+    split = take_apart(order, sums.reshape(-1, width), [vector.shape[0] for vector in vectors])
     full_query, full_key, full_value, full_rel = widen_heads(
         order, heads_gathered.reshape(-1, cols), chunk, extra, width, cols, "full_heads", [sums]
     )

time: 571 us -> 567 us (level)
  Pallas kernels: 271 us -> 279 us
  waiting for transfers between devices: 171 us -> 164 us
    pallas_call x37 -> x39, Pallas kernels: 271 us -> 279 us  [call(): pl.pallas_call(body, grid_spec=pltpu.PrefetchScalarGridSpec(num_scalar_pr...]
    ppermute x40, waiting for transfers between devices: 148 us -> 142 us  [swap(): return lax.ppermute(value, axis, pairs)]
    unnamed x132 -> x121, local copies, waits for them, and re-layouts: 20.1 us -> 14.8 us
  transfers between devices with their start and end apart: 44 -> 44, of which waited for: 21 -> 21; matrix products, arithmetic and copies ran while one was open for 8% -> 7% of each run, Pallas kernels for 46% -> 48%
where the time goes in v4:
time: 567 us; the launch traced here: 557 us
  Pallas kernels  279 us (49%)
  waiting for transfers between devices  164 us (29%)
  starting transfers between devices  43.1 us (8%)
  local copies, waits for them, and re-layouts  24.8 us (4%)
  other arithmetic  16.5 us (3%)
  between operations  15.6 us (3%)
  matrix products  13.9 us (2%)
    pallas_call x39, Pallas kernels, call(): pl.pallas_call(body, grid_spec=pltpu.PrefetchScalarGridSpec(num_scalar_pr...  279 us
    ppermute x40, waiting for transfers between devices, swap(): return lax.ppermute(value, axis, pairs)  142 us
    ppermute x40, starting transfers between devices, swap(): return lax.ppermute(value, axis, pairs)  42.5 us
    unnamed x121, local copies, waits for them, and re-layouts  14.8 us
    reduce_scatter x1, waiting for transfers between devices, on_device(): heads_share = lax.psum_scatter(grads, 'dp', scatter_dimension=0, tiled=True)  14.4 us
  transfers between devices with their start and end apart: 44, of which 21 were waited for; matrix products, arithmetic and copies ran while one was open for 7% of the time, Pallas kernels for 48%

profile of v4, /device:TPU:0, one launch (start us, length us, event | category | flops | bytes accessed | tf_op | source)
XLA Modules:
  0.0 556.7 jit_solution(15824375185625881227)
XLA Ops:
  26.7 7.9 %project.3 = (bf16[480,1024]{1,0:T(8,128)(2,1)}, bf16[480,512]{1,0:T(8,128)(2,1)}, bf16[480,512]{1,0:T(8,128)(2,1)}, bf16[480,1024]{1,0:T(8,128)(2,1)}, bf16[480...) custom-call(s32[1]{0:T(128)} %get-tuple-element.145.scalar_ref, ...), custom_call_target="tpu_custom_call" | custom-call | flops 1000 | bytes 1000 | tf_op jit(solution)/shard_map/project/pallas_call | solution.py:56
  48.5 5.9 %project.4 = (bf16[480,1024]{1,0:T(8,128)(2,1)}, bf16[480,512]{1,0:T(8,128)(2,1)}, bf16[480,512]{1,0:T(8,128)(2,1)}, f32[480,512]{1,0:T(8,128)}) custom-call(s32[1]{0:T(128)} %get-tuple-element.145.scalar_ref, bf16[480,1024]{1,0:T(8,128)(2,1)} %collective-permute-done.refs_0_, bf16[1,1024]{1,0:T(2,128)(2,1)} %broadcast_in_dim.51.refs_3_.refs_1_.refs_4_, ...), custom_call_target="tpu_custom_call" | custom-call | flops 1000 | bytes 1000 | tf_op jit(solution)/shard_map/project/pallas_call | solution.py:56
  54.4 10.4 %collective-permute-done.1.refs_0_ = bf16[736,1024]{1,0:T(8,128)(2,1)} collective-permute-done((bf16[736,1024]{1,0:T(8,128)(2,1)}, bf16[736,1024]{1,0:T(8,128)(2,1)}, u32[]{:S(2)}, u32[]{:S(2)}) %collective-permute-start.1) | collective-permute-done | bytes 1507360 | tf_op jit(solution)/shard_map/ppermute | solution.py:79
  64.8 5.6 %project.5 = (bf16[480,1024]{1,0:T(8,128)(2,1)}, bf16[480,512]{1,0:T(8,128)(2,1)}, bf16[480,512]{1,0:T(8,128)(2,1)}, bf16[256,1024]{1,0:T(8,128)(2,1)}, bf16[256...) custom-call(s32[1]{0:T(128)} %get-tuple-element.145.scalar_ref, bf16[736,1024]{1,0:T(8,128)(2,1)} %collective-permute-done.1.refs_0_, ...), custom_call_target="tpu_custom_call" | custom-call | flops 1000 | bytes 1000 | tf_op jit(solution)/shard_map/project/pallas_call | solution.py:56
  70.4 17.5 %attend.2 = (bf16[480,256]{1,0:T(8,128)(2,1)}, bf16[480,256]{1,0:T(8,128)(2,1)}, bf16[2,960,2432]{2,1,0:T(8,128)(2,1)}) custom-call(s32[2]{0:T(128)} %get-tuple-element.144.scalar_ref, f32[480,512]{1,0:T(8,128)} %get-tuple-element.151.refs_9_.refs_0_.refs_1_, f32[480,512]{1,0:T(8,128)} %get-tuple-element.152.refs_6_.refs_1_.refs_2_, ...), custom_call_target="tpu_custom_call" | custom-call | flops 1000 | bytes 1000 | tf_op jit(solution)/shard_map/attend/pallas_call | solution.py:56
  88.0 18.0 %attend.3 = (bf16[480,256]{1,0:T(8,128)(2,1)}, bf16[480,256]{1,0:T(8,128)(2,1)}, bf16[2,960,2432]{2,1,0:T(8,128)(2,1)}) custom-call(s32[2]{0:T(128)} %get-tuple-element.144.scalar_ref, f32[480,512]{1,0:T(8,128)} %get-tuple-element.151.refs_9_.refs_0_.refs_1_, f32[480,512]{1,0:T(8,128)} %get-tuple-element.152.refs_6_.refs_1_.refs_2_, ...), custom_call_target="tpu_custom_call" | custom-call | flops 1000 | bytes 1000 | tf_op jit(solution)/shard_map/attend/pallas_call | solution.py:56
  108.0 7.1 %collective-permute-done.3.refs_3_ = bf16[480,256]{1,0:T(8,128)(2,1)S(1)} collective-permute-done((bf16[480,256]{1,0:T(8,128)(2,1)}, bf16[480,256]{1,0:T(8,128)(2,1)S(1)}, u32[]{:S(2)}, u32[]{:S(2)}) %collective-permute-start.3) | collective-permute-done | bytes 245792 | tf_op jit(solution)/shard_map/ppermute | solution.py:79
  119.3 33.7 %middle.1 = (bf16[480,1024]{1,0:T(8,128)(2,1)}, bf16[480,2560]{1,0:T(8,128)(2,1)}, bf16[480,512]{1,0:T(8,128)(2,1)}, bf16[480,2048]{1,0:T(8,128)(2,1)}, bf16[480...) custom-call(s32[2]{0:T(128)} %get-tuple-element.143.scalar_ref, ...), custom_call_target="tpu_custom_call" | custom-call | flops 1000 | bytes 1000 | tf_op jit(solution)/shard_map/middle/pallas_call | solution.py:56
  155.6 7.9 %collective-permute-done.6.refs_3_ = bf16[480,1024]{1,0:T(8,128)(2,1)} collective-permute-done((bf16[480,1024]{1,0:T(8,128)(2,1)S(1)}, bf16[480,1024]{1,0:T(8,128)(2,1)}, u32[]{:S(2)}, u32[]{:S(2)}) %collective-permute-start.6) | collective-permute-done | bytes 983072 | tf_op jit(solution)/shard_map/ppermute | solution.py:79
  163.5 5.5 grad_down.1.refs_5_
  171.8 6.2 %grad_up.1.refs_4_ = bf16[512,2048]{1,0:T(8,128)(2,1)} custom-call(s32[1]{0:T(128)} %bitcast.18.scalar_ref, bf16[480,2560]{1,0:T(8,128)(2,1)} %get-tuple-element.182.refs_0_.refs_2_.refs_4_.refs_10_, bf16[480,2560]{1,0:T(8,128)(2,1)} %copy-done.2, bf16[480,2048]{1,0:T(8,128)(2,1)} %get-tuple-element.183.refs_2_.refs_6_, ...), custom_call_target="tpu_custom_call" | custom-call | flops 1000 | bytes 1000 | tf_op jit(solution)/shard_map/grad_up/pallas_call | solution.py:56
  185.5 13.2 %grad_keep.1 = (bf16[1024,1024]{1,0:T(8,128)(2,1)}, bf16[512,2048]{1,0:T(8,128)(2,1)}, bf16[256,1024]{1,0:T(8,128)(2,1)}) custom-call(s32[3]{0:T(128)} %pad_add_fusion.2.scalar_ref, bf16[480,2048]{1,0:T(8,128)(2,1)} %get-tuple-element.180.refs_0_, bf16[480,2048]{1,0:T(8,128)(2,1)} %collective-permute-done.5.refs_1_, bf16[480,1024]{1,0:T(8,128)(2,1)} %bitcast.57, ...), custom_call_target="tpu_custom_call" | custom-call | flops 1000 | bytes 1000 | tf_op jit(solution)/shard_map/grad_keep/pallas_call | solution.py:56
  198.7 21.6 %attend_back.2 = (bf16[480,256]{1,0:T(8,128)(2,1)}, bf16[480,256]{1,0:T(8,128)(2,1)}, bf16[2432,256]{1,0:T(8,128)(2,1)}, bf16[2432,256]{1,0:T(8,128)(2,1)}, bf16...) custom-call(s32[1]{0:T(128)} %get-tuple-element.145.scalar_ref, ...), custom_call_target="tpu_custom_call" | custom-call | flops 1000 | bytes 1000 | tf_op jit(solution)/shard_map/attend_back/pallas_call | solution.py:56
  226.8 6.9 %sum_middle.4 = (bf16[512,1024]{1,0:T(8,128)(2,1)}, bf16[512,1024]{1,0:T(8,128)(2,1)}, bf16[256,2048]{1,0:T(8,128)(2,1)}, bf16[256,2048]{1,0:T(8,128)(2,1)}, bf1...) custom-call(s32[3]{0:T(128)} %pad_add_fusion.3.scalar_ref, bf16[1024,1024]{1,0:T(8,128)(2,1)} %get-tuple-element.189.refs_0_.refs_2_, ...), custom_call_target="tpu_custom_call" | custom-call | flops 1000 | bytes 1000 | tf_op jit(solution)/shard_map/sum_middle/pallas_call | solution.py:56
  238.3 21.6 %attend_back.3 = (bf16[480,256]{1,0:T(8,128)(2,1)}, bf16[480,256]{1,0:T(8,128)(2,1)}, bf16[2432,256]{1,0:T(8,128)(2,1)}, bf16[2432,256]{1,0:T(8,128)(2,1)}, bf16...) custom-call(s32[1]{0:T(128)} %get-tuple-element.145.scalar_ref, ...), custom_call_target="tpu_custom_call" | custom-call | flops 1000 | bytes 1000 | tf_op jit(solution)/shard_map/attend_back/pallas_call | solution.py:56
  259.9 5.6 collective-permute-done.13.refs_5_.refs_7_
  277.7 22.5 %grad_heads.1 = (bf16[4352,512]{1,0:T(8,128)(2,1)}, f32[1024,1]{1,0:T(8,128)}, f32[1024,1]{1,0:T(8,128)}) custom-call(s32[1]{0:T(128)} %get-tuple-element.145.scalar_ref, bf16[256,1024]{1,0:T(8,128)(2,1)} %get-tuple-element.200.refs_0_, bf16[480,1024]{1,0:T(8,128)(2,1)} %get-tuple-element.201.refs_1_, bf16[480,1024]{1,0:T(8,128)(2,1)} %get-tuple-element.202.refs_2_, ...), custom_call_target="tpu_custom_call" | custom-call | flops 1000 | bytes 1000 | tf_op jit(solution)/shard_map/grad_heads/pallas_call | solution.py:56
  312.9 8.9 %segment_back.1 = (f32[480,1024]{1,0:T(8,128)}, bf16[480,1024]{1,0:T(8,128)(2,1)}) custom-call(s32[1]{0:T(128)} %get-tuple-element.145.scalar_ref, bf16[480,256]{1,0:T(8,128)(2,1)} %get-tuple-element.188.refs_7_.refs_0_, bf16[480,256]{1,0:T(8,128)(2,1)} %get-tuple-element.193.refs_8_.refs_1_, bf16[480,256]{1,0:T(8,128)(2,1)} %get-tuple-element.194.refs_9_.refs_2_, ...), custom_call_target="tpu_custom_call" | custom-call | flops 1000 | bytes 1000 | tf_op jit(solution)/shard_map/segment_back/pallas_call | solution.py:56
  339.5 11.5 %collective-permute-done.21.refs_1_ = bf16[128,1024]{1,0:T(8,128)(2,1)S(1)} collective-permute-done((bf16[128,1024]{1,0:T(8,128)(2,1)}, bf16[128,1024]{1,0:T(8,128)(2,1)S(1)}, u32[]{:S(2)}, u32[]{:S(2)}) %collective-permute-start.21) | collective-permute-done | bytes 262176 | tf_op jit(solution)/shard_map/ppermute | solution.py:79
  351.0 5.7 %collective-permute-done.22.refs_3_ = bf16[64,2048]{1,0:T(8,128)(2,1)S(1)} collective-permute-done((bf16[64,2048]{1,0:T(8,128)(2,1)}, bf16[64,2048]{1,0:T(8,128)(2,1)S(1)}, u32[]{:S(2)}, u32[]{:S(2)}) %collective-permute-start.22) | collective-permute-done | bytes 262176 | tf_op jit(solution)/shard_map/ppermute | solution.py:79
  365.6 7.8 %full_comp.1.refs_5_ = f32[3072,1024]{1,0:T(8,128)} custom-call(s32[1]{0:T(128)} %constant.15.clone.1.scalar_ref, bf16[3072,1024]{1,0:T(8,128)(2,1)} %all-gather.3.cloned.1.call-done.refs_0_, bf16[480,1024]{1,0:T(8,128)(2,1)} %gate.14.refs_1_), custom_call_target="tpu_custom_call" | custom-call | flops 1000 | bytes 1000 | tf_op jit(solution)/shard_map/full_comp/pallas_call | solution.py:56
  373.4 9.9 %collective-permute-done.24.refs_3_ = bf16[480,1024]{1,0:T(8,128)(2,1)S(1)} collective-permute-done((bf16[480,1024]{1,0:T(8,128)(2,1)}, bf16[480,1024]{1,0:T(8,128)(2,1)S(1)}, u32[]{:S(2)}, u32[]{:S(2)}) %collective-permute-start.24) | collective-permute-done | bytes 983072 | tf_op jit(solution)/shard_map/ppermute | solution.py:79
  394.0 14.4 %reduce-scatter.5.cloned.1.call-done.refs_0_ = bf16[1,272,512]{2,1,0:T(8,128)(2,1)} async-done(((bf16[16,272,512]{2,1,0:T(8,128)(2,1)}), bf16[1,272,512]{2,1,0:T(8,128)(2,1)}) %reduce-scatter.5.cloned.1.call-update) | async-done | bytes 278544 | tf_op jit(solution)/shard_map/reduce_scatter | solution.py:1026
  417.5 17.1 %collective-permute-done.28.refs_1_ = bf16[512,1024]{1,0:T(8,128)(2,1)S(1)} collective-permute-done((bf16[512,1024]{1,0:T(8,128)(2,1)}, bf16[512,1024]{1,0:T(8,128)(2,1)S(1)}, u32[]{:S(2)}, u32[]{:S(2)}) %collective-permute-start.28) | collective-permute-done | bytes 1048608 | tf_op jit(solution)/shard_map/ppermute | solution.py:79
  449.9 7.1 %full_down.2.refs_2_ = f32[4096,1024]{1,0:T(8,128)} custom-call(s32[2]{0:T(128)} %pad_add_fusion.8.scalar_ref, bf16[1024,1024]{1,0:T(8,128)(2,1)} %get-tuple-element.248.refs_0_, bf16[1024,1024]{1,0:T(8,128)(2,1)} %collective-permute-done.35.refs_1_, bf16[256,1024]{1,0:T(8,128)(2,1)} %get-tuple-element.250.refs_2_.refs_0_), custom_call_target="tpu_custom_call" | custom-call | flops 1000 | bytes 1000 | tf_op jit(solution)/shard_map/full_down/pallas_call | solution.py:56
  457.1 7.0 %full_up.2.refs_1_.refs_2_ = f32[1024,4096]{1,0:T(8,128)} custom-call(s32[2]{0:T(128)} %pad_add_fusion.7.scalar_ref, bf16[512,2048]{1,0:T(8,128)(2,1)} %get-tuple-element.249.refs_0_, bf16[512,2048]{1,0:T(8,128)(2,1)} %collective-permute-done.34.refs_1_, f32[4096,1024]{1,0:T(8,128)} %full_down.2.refs_2_), custom_call_target="tpu_custom_call" | custom-call | flops 1000 | bytes 1000 | tf_op jit(solution)/shard_map/full_up/pallas_call | solution.py:56
  470.1 7.1 %full_out.1.refs_2_ = f32[1024,1024]{1,0:T(8,128)} custom-call(s32[2]{0:T(128)} %pad_add_fusion.6.scalar_ref, bf16[256,1024]{1,0:T(8,128)(2,1)} %get-tuple-element.250.refs_2_.refs_0_, bf16[256,1024]{1,0:T(8,128)(2,1)} %gate.16.refs_1_.refs_4_, bf16[256,1024]{1,0:T(8,128)(2,1)} %copy-done.22, bf16[256,1024]{1,0:T(8,128)(2,1)} %copy-done.23, ...), custom_call_target="tpu_custom_call" | custom-call | flops 1000 | bytes 1000 | tf_op jit(solution)/shard_map/full_out/pallas_call | solution.py:56
  477.2 33.3 %collective-permute-done.31.refs_0_ = bf16[1024,1024]{1,0:T(8,128)(2,1)S(1)} collective-permute-done((bf16[1024,1024]{1,0:T(8,128)(2,1)}, bf16[1024,1024]{1,0:T(8,128)(2,1)S(1)}, u32[]{:S(2)}, u32[]{:S(2)}) %collective-permute-start.31) | collective-permute-done | bytes 2097184 | tf_op jit(solution)/shard_map/ppermute | solution.py:79
  512.3 7.4 %all-gather.5.cloned.1.call-done = bf16[32,272,512]{2,1,0:T(8,128)(2,1)} async-done(((bf16[1,272,512]{2,1,0:T(8,128)(2,1)}), bf16[32,272,512]{2,1,0:T(8,128)(2,1)}) %all-gather.5.cloned.1.call-update) | async-done | bytes 8912912 | tf_op jit(solution)/shard_map/all_gather | solution.py:1040
  523.6 10.6 %full_heads.1 = (f32[1024,1024]{1,0:T(8,128)}, f32[1024,1024]{1,0:T(8,128)}, f32[1024,1024]{1,0:T(8,128)}, f32[1024,1024]{1,0:T(8,128)}) custom-call(s32[1]{0:T(128)} %constant.15.clone.1.scalar_ref, bf16[8704,512]{1,0:T(8,128)(2,1)} %bitcast.52, f32[12288]{0:T(1024)} %add.84.refs_1_, f32[1024]{0:T(1024)} %get-tuple-element.142.refs_2_), custom_call_target="tpu_custom_call" | custom-call | flops 1000 | bytes 1000 | tf_op jit(solution)/shard_map/full_heads/pallas_call | solution.py:56
  535.5 7.0 %full_down.3.refs_3_ = f32[4096,1024]{1,0:T(8,128)} custom-call(s32[2]{0:T(128)} %pad_add_fusion.8.scalar_ref, bf16[1024,1024]{1,0:T(8,128)(2,1)} %get-tuple-element.263.refs_0_, bf16[1024,1024]{1,0:T(8,128)(2,1)} %copy-done.9, f32[4096,1024]{1,0:T(8,128)} %full_down.2.refs_2_, f32[1024,1024]{1,0:T(8,128)} %get-tuple-element.131.refs_3_), custom_call_target="tpu_custom_call", output_to_operand_aliasing={{}: (3, {})} | custom-call | flops 1000 | bytes 1000 | tf_op jit(solution)/shard_map/full_down/pallas_call | solution.py:56
  542.5 7.2 %full_up.3 = f32[1024,4096]{1,0:T(8,128)} custom-call(s32[2]{0:T(128)} %pad_add_fusion.7.scalar_ref, bf16[512,2048]{1,0:T(8,128)(2,1)} %get-tuple-element.251.refs_1_.refs_0_, bf16[512,2048]{1,0:T(8,128)(2,1)} %collective-permute-done.38.refs_1_, f32[1024,4096]{1,0:T(8,128)} %full_up.2.refs_1_.refs_2_, ...), custom_call_target="tpu_custom_call", output_to_operand_aliasing={{}: (3, {})} | custom-call | flops 1000 | bytes 1000 | tf_op jit(solution)/shard_map/full_up/pallas_call | solution.py:56
  (269 shorter events, 162.1 us)
Async XLA Ops:
  7.3 226.4 %reduce-scatter.3.cloned.1.call-start = ((), (), s32[]{:S(2)}) async-start(), calls=%async_computation.2 | async-start | bytes 6488064 | tf_op jit(solution)/shard_map/reduce_scatter | solution.py:934
  7.3 41.1 %collective-permute-start = (bf16[480,1024]{1,0:T(8,128)(2,1)}, bf16[480,1024]{1,0:T(8,128)(2,1)}, u32[]{:S(2)}, u32[]{:S(2)}) collective-permute-start(bf16[480,1024]{1,0:T(8,128)(2,1)} %bitcast.59), channel_id=1, source_target_pairs={{0,1},{1,0},{2,3},{3,2},{4,5},{5,4},{6,7},{7,6},{8,9},{9,8},{10,11... | collective-permute-start | bytes 2949128 | tf_op jit(solution)/shard_map/ppermute | solution.py:79
  13.0 51.8 %collective-permute-start.1 = (bf16[736,1024]{1,0:T(8,128)(2,1)}, bf16[736,1024]{1,0:T(8,128)(2,1)}, u32[]{:S(2)}, u32[]{:S(2)}) collective-permute-start(bf16[736,1024]{1,0:T(8,128)(2,1)} %pad_maximum_fusion.1), channel_id=1, source_target_pairs={{0,1},{1,0},{2,3},{3,2},{4,5},{5,4},{6,7},{7,6},{8,9},{9,8},{10,11... | collective-permute-start | bytes 4521992 | tf_op jit(solution)/shard_map/ppermute | solution.py:79
  70.4 295.2 %all-gather.3.cloned.1.call-start = ((), (), s32[]{:S(2)}) async-start(), calls=%async_computation.3 | async-start | bytes 6488064 | tf_op jit(solution)/shard_map/all_gather | solution.py:989
  153.1 17.3 %collective-permute-start.7 = (bf16[480,2560]{1,0:T(8,128)(2,1)}, bf16[480,2560]{1,0:T(8,128)(2,1)S(1)}, u32[]{:S(2)}, u32[]{:S(2)}) collective-permute-start(bf16[480,2560]{1,0:T(8,128)(2,1)} %get-tuple-element.182.refs_0_.refs_2_.refs_4_.refs_10_), channel_id=1, source_target_pairs={{0,2},{2,0},{4,6},{6,4},{8,10},{10,8},{12,14},{14,12},{16,18},{18,... | collective-permute-start | bytes 7372808 | tf_op jit(solution)/shard_map/ppermute | solution.py:79
  153.6 16.7 %collective-permute-start.8 = (bf16[480,2048]{1,0:T(8,128)(2,1)}, bf16[480,2048]{1,0:T(8,128)(2,1)}, u32[]{:S(2)}, u32[]{:S(2)}) collective-permute-start(bf16[480,2048]{1,0:T(8,128)(2,1)} %get-tuple-element.184), channel_id=1, source_target_pairs={{0,2},{2,0},{4,6},{6,4},{8,10},{10,8},{12,14},{14,12},{16,18},{18,... | collective-permute-start | bytes 5898248 | tf_op jit(solution)/shard_map/ppermute | solution.py:79
  168.9 51.4 %collective-permute-start.9 = (bf16[1024,1024]{1,0:T(8,128)(2,1)}, bf16[1024,1024]{1,0:T(8,128)(2,1)}, u32[]{:S(2)}, u32[]{:S(2)}) collective-permute-start(bf16[1024,1024]{1,0:T(8,128)(2,1)} %grad_down.1.refs_5_), channel_id=1, source_target_pairs={{0,4},{2,6},{4,0},{6,2},{8,12},{10,14},{12,8},{14,10},{16,20},{18,... | collective-permute-start | bytes 6291464 | tf_op jit(solution)/shard_map/ppermute | solution.py:79
  178.0 47.5 %collective-permute-start.10 = (bf16[512,2048]{1,0:T(8,128)(2,1)}, bf16[512,2048]{1,0:T(8,128)(2,1)S(1)}, u32[]{:S(2)}, u32[]{:S(2)}) collective-permute-start(bf16[512,2048]{1,0:T(8,128)(2,1)} %grad_up.1.refs_4_), channel_id=1, source_target_pairs={{0,1},{1,0},{2,3},{3,2},{4,5},{5,4},{6,7},{7,6},{8,9},{9,8},{10,11... | collective-permute-start | bytes 6291464 | tf_op jit(solution)/shard_map/ppermute | solution.py:79
  182.7 37.6 %collective-permute-start.11 = (bf16[256,1024]{1,0:T(8,128)(2,1)}, bf16[256,1024]{1,0:T(8,128)(2,1)S(1)}, u32[]{:S(2)}, u32[]{:S(2)}) collective-permute-start(bf16[256,1024]{1,0:T(8,128)(2,1)} %grad_out.1.refs_12_), channel_id=1, source_target_pairs={{0,8},{2,10},{4,12},{6,14},{8,0},{10,2},{12,4},{14,6},{16,24},{18,... | collective-permute-start | bytes 1572872 | tf_op jit(solution)/shard_map/ppermute | solution.py:79
  233.7 174.7 %reduce-scatter.5.cloned.1.call-start = ((), (), s32[]{:S(2)}) async-start(), calls=%async_computation.4 | async-start | bytes 4734976 | tf_op jit(solution)/shard_map/reduce_scatter | solution.py:1026
  234.0 26.0 %collective-permute-start.12 = (bf16[512,1024]{1,0:T(8,128)(2,1)}, bf16[512,1024]{1,0:T(8,128)(2,1)S(1)}, u32[]{:S(2)}, u32[]{:S(2)}) collective-permute-start(bf16[512,1024]{1,0:T(8,128)(2,1)} %get-tuple-element.209), channel_id=1, source_target_pairs={{0,1},{1,0},{2,3},{3,2},{4,5},{5,4},{6,7},{7,6},{8,9},{9,8},{10,11... | collective-permute-start | bytes 3145736 | tf_op jit(solution)/shard_map/ppermute | solution.py:79
  235.5 29.9 %collective-permute-start.13 = (bf16[256,2048]{1,0:T(8,128)(2,1)}, bf16[256,2048]{1,0:T(8,128)(2,1)S(1)}, u32[]{:S(2)}, u32[]{:S(2)}) collective-permute-start(bf16[256,2048]{1,0:T(8,128)(2,1)} %get-tuple-element.211), channel_id=1, source_target_pairs={{0,8},{2,10},{4,12},{6,14},{8,0},{10,2},{12,4},{14,6},{16,24},{18,... | collective-permute-start | bytes 3145736 | tf_op jit(solution)/shard_map/ppermute | solution.py:79
  237.1 22.8 %collective-permute-start.14 = (bf16[128,1024]{1,0:T(8,128)(2,1)}, bf16[128,1024]{1,0:T(8,128)(2,1)S(1)}, u32[]{:S(2)}, u32[]{:S(2)}) collective-permute-start(bf16[128,1024]{1,0:T(8,128)(2,1)} %get-tuple-element.212), channel_id=1, source_target_pairs={{0,4},{2,6},{4,0},{6,2},{8,12},{10,14},{12,8},{14,10},{16,20},{18,... | collective-permute-start | bytes 786440 | tf_op jit(solution)/shard_map/ppermute | solution.py:79
  270.8 29.8 %collective-permute-start.15 = (bf16[256,1024]{1,0:T(8,128)(2,1)}, bf16[256,1024]{1,0:T(8,128)(2,1)S(1)}, u32[]{:S(2)}, u32[]{:S(2)}) collective-permute-start(bf16[256,1024]{1,0:T(8,128)(2,1)} %get-tuple-element.219), channel_id=1, source_target_pairs={{0,8},{2,10},{4,12},{6,14},{8,0},{10,2},{12,4},{14,6},{16,24},{18,... | collective-permute-start | bytes 1572872 | tf_op jit(solution)/shard_map/ppermute | solution.py:79
  273.3 27.4 %collective-permute-start.16 = (bf16[128,2048]{1,0:T(8,128)(2,1)}, bf16[128,2048]{1,0:T(8,128)(2,1)S(1)}, u32[]{:S(2)}, u32[]{:S(2)}) collective-permute-start(bf16[128,2048]{1,0:T(8,128)(2,1)} %get-tuple-element.221), channel_id=1, source_target_pairs={{0,4},{2,6},{4,0},{6,2},{8,12},{10,14},{12,8},{14,10},{16,20},{18,... | collective-permute-start | bytes 1572872 | tf_op jit(solution)/shard_map/ppermute | solution.py:79
  273.9 26.7 %collective-permute-start.17 = (bf16[64,1024]{1,0:T(8,128)(2,1)}, bf16[64,1024]{1,0:T(8,128)(2,1)S(1)}, u32[]{:S(2)}, u32[]{:S(2)}) collective-permute-start(bf16[64,1024]{1,0:T(8,128)(2,1)} %get-tuple-element.222), channel_id=1, source_target_pairs={{0,16},{2,18},{4,20},{6,22},{8,24},{10,26},{12,28},{14,30},{16,0},... | collective-permute-start | bytes 393224 | tf_op jit(solution)/shard_map/ppermute | solution.py:79
  309.6 210.1 %all-gather.5.cloned.1.call-start = ((), (), s32[]{:S(2)}) async-start(), calls=%async_computation.5 | async-start | bytes 9191424 | tf_op jit(solution)/shard_map/all_gather | solution.py:1040
  310.0 19.3 %collective-permute-start.19 = (bf16[64,2048]{1,0:T(8,128)(2,1)S(1)}, bf16[64,2048]{1,0:T(8,128)(2,1)S(1)}, u32[]{:S(2)}, u32[]{:S(2)}) collective-permute-start(bf16[64,2048]{1,0:T(8,128)(2,1)S(1)} %copy-done.51), channel_id=1, source_target_pairs={{0,16},{2,18},{4,20},{6,22},{8,24},{10,26},{12,28},{14,30},{16,0},... | collective-permute-start | bytes 786440 | tf_op jit(solution)/shard_map/ppermute | solution.py:79
  332.1 18.9 %collective-permute-start.21 = (bf16[128,1024]{1,0:T(8,128)(2,1)}, bf16[128,1024]{1,0:T(8,128)(2,1)S(1)}, u32[]{:S(2)}, u32[]{:S(2)}) collective-permute-start(bf16[128,1024]{1,0:T(8,128)(2,1)} %get-tuple-element.232.refs_0_), channel_id=1, source_target_pairs={{0,16},{2,18},{4,20},{6,22},{8,24},{10,26},{12,28},{14,30},{16,0},... | collective-permute-start | bytes 786440 | tf_op jit(solution)/shard_map/ppermute | solution.py:79
  332.1 24.6 %collective-permute-start.22 = (bf16[64,2048]{1,0:T(8,128)(2,1)}, bf16[64,2048]{1,0:T(8,128)(2,1)S(1)}, u32[]{:S(2)}, u32[]{:S(2)}) collective-permute-start(bf16[64,2048]{1,0:T(8,128)(2,1)} %get-tuple-element.233.refs_2_), channel_id=1, source_target_pairs={{0,16},{2,18},{4,20},{6,22},{8,24},{10,26},{12,28},{14,30},{16,0},... | collective-permute-start | bytes 786440 | tf_op jit(solution)/shard_map/ppermute | solution.py:79
  359.7 23.7 %collective-permute-start.24 = (bf16[480,1024]{1,0:T(8,128)(2,1)}, bf16[480,1024]{1,0:T(8,128)(2,1)S(1)}, u32[]{:S(2)}, u32[]{:S(2)}) collective-permute-start(bf16[480,1024]{1,0:T(8,128)(2,1)} %gate.14.refs_1_), channel_id=1, source_target_pairs={{0,1},{1,0},{2,3},{3,2},{4,5},{5,4},{6,7},{7,6},{8,9},{9,8},{10,11... | collective-permute-start | bytes 2949128 | tf_op jit(solution)/shard_map/ppermute | solution.py:79
  361.0 28.3 %collective-permute-start.25 = (bf16[256,1024]{1,0:T(8,128)(2,1)}, bf16[256,1024]{1,0:T(8,128)(2,1)S(1)}, u32[]{:S(2)}, u32[]{:S(2)}) collective-permute-start(bf16[256,1024]{1,0:T(8,128)(2,1)} %get-tuple-element.243.refs_0_), channel_id=1, source_target_pairs={{0,8},{2,10},{4,12},{6,14},{8,0},{10,2},{12,4},{14,6},{16,24},{18,... | collective-permute-start | bytes 1572872 | tf_op jit(solution)/shard_map/ppermute | solution.py:79
  361.8 27.6 %collective-permute-start.26 = (bf16[128,2048]{1,0:T(8,128)(2,1)}, bf16[128,2048]{1,0:T(8,128)(2,1)S(1)}, u32[]{:S(2)}, u32[]{:S(2)}) collective-permute-start(bf16[128,2048]{1,0:T(8,128)(2,1)} %get-tuple-element.244.refs_2_), channel_id=1, source_target_pairs={{0,4},{2,6},{4,0},{6,2},{8,12},{10,14},{12,8},{14,10},{16,20},{18,... | collective-permute-start | bytes 1572872 | tf_op jit(solution)/shard_map/ppermute | solution.py:79
  361.9 27.5 %collective-permute-start.27 = (bf16[64,1024]{1,0:T(8,128)(2,1)}, bf16[64,1024]{1,0:T(8,128)(2,1)S(1)}, u32[]{:S(2)}, u32[]{:S(2)}) collective-permute-start(bf16[64,1024]{1,0:T(8,128)(2,1)} %get-tuple-element.235.refs_1_.refs_4_), channel_id=1, source_target_pairs={{0,16},{2,18},{4,20},{6,22},{8,24},{10,26},{12,28},{14,30},{16,0},... | collective-permute-start | bytes 393224 | tf_op jit(solution)/shard_map/ppermute | solution.py:79
  408.5 26.1 %collective-permute-start.28 = (bf16[512,1024]{1,0:T(8,128)(2,1)}, bf16[512,1024]{1,0:T(8,128)(2,1)S(1)}, u32[]{:S(2)}, u32[]{:S(2)}) collective-permute-start(bf16[512,1024]{1,0:T(8,128)(2,1)} %get-tuple-element.246.refs_0_), channel_id=1, source_target_pairs={{0,1},{1,0},{2,3},{3,2},{4,5},{5,4},{6,7},{7,6},{8,9},{9,8},{10,11... | collective-permute-start | bytes 3145736 | tf_op jit(solution)/shard_map/ppermute | solution.py:79
  410.0 29.7 %collective-permute-start.29 = (bf16[256,2048]{1,0:T(8,128)(2,1)}, bf16[256,2048]{1,0:T(8,128)(2,1)S(1)}, u32[]{:S(2)}, u32[]{:S(2)}) collective-permute-start(bf16[256,2048]{1,0:T(8,128)(2,1)} %get-tuple-element.247.refs_2_), channel_id=1, source_target_pairs={{0,8},{2,10},{4,12},{6,14},{8,0},{10,2},{12,4},{14,6},{16,24},{18,... | collective-permute-start | bytes 3145736 | tf_op jit(solution)/shard_map/ppermute | solution.py:79
  445.8 64.7 %collective-permute-start.31 = (bf16[1024,1024]{1,0:T(8,128)(2,1)}, bf16[1024,1024]{1,0:T(8,128)(2,1)S(1)}, u32[]{:S(2)}, u32[]{:S(2)}) collective-permute-start(bf16[1024,1024]{1,0:T(8,128)(2,1)} %get-tuple-element.248.refs_0_), channel_id=1, source_target_pairs={{0,4},{2,6},{4,0},{6,2},{8,12},{10,14},{12,8},{14,10},{16,20},{18,... | collective-permute-start | bytes 6291464 | tf_op jit(solution)/shard_map/ppermute | solution.py:79
  446.7 63.8 %collective-permute-start.32 = (bf16[512,2048]{1,0:T(8,128)(2,1)}, bf16[512,2048]{1,0:T(8,128)(2,1)}, u32[]{:S(2)}, u32[]{:S(2)}) collective-permute-start(bf16[512,2048]{1,0:T(8,128)(2,1)} %get-tuple-element.249.refs_0_), channel_id=1, source_target_pairs={{0,1},{1,0},{2,3},{3,2},{4,5},{5,4},{6,7},{7,6},{8,9},{9,8},{10,11... | collective-permute-start | bytes 6291464 | tf_op jit(solution)/shard_map/ppermute | solution.py:79
  447.5 18.8 %collective-permute-start.33 = (bf16[256,1024]{1,0:T(8,128)(2,1)}, bf16[256,1024]{1,0:T(8,128)(2,1)S(1)}, u32[]{:S(2)}, u32[]{:S(2)}) collective-permute-start(bf16[256,1024]{1,0:T(8,128)(2,1)} %get-tuple-element.250.refs_2_.refs_0_), channel_id=1, source_target_pairs={{0,8},{2,10},{4,12},{6,14},{8,0},{10,2},{12,4},{14,6},{16,24},{18,... | collective-permute-start | bytes 1572872 | tf_op jit(solution)/shard_map/ppermute | solution.py:79
  449.8 17.9 %collective-permute-start.36 = (bf16[256,1024]{1,0:T(8,128)(2,1)}, bf16[256,1024]{1,0:T(8,128)(2,1)S(1)}, u32[]{:S(2)}, u32[]{:S(2)}) collective-permute-start(bf16[256,1024]{1,0:T(8,128)(2,1)} %get-tuple-element.250.refs_2_.refs_0_), channel_id=1, source_target_pairs={{0,2},{2,0},{4,6},{6,4},{8,10},{10,8},{12,14},{14,12},{16,18},{18,... | collective-permute-start | bytes 1572872 | tf_op jit(solution)/shard_map/ppermute | solution.py:79
  511.8 22.4 %collective-permute-start.39 = (bf16[1024,1024]{1,0:T(8,128)(2,1)}, bf16[1024,1024]{1,0:T(8,128)(2,1)S(1)}, u32[]{:S(2)}, u32[]{:S(2)}) collective-permute-start(bf16[1024,1024]{1,0:T(8,128)(2,1)} %get-tuple-element.263.refs_0_), channel_id=1, source_target_pairs={{0,2},{2,0},{4,6},{6,4},{8,10},{10,8},{12,14},{14,12},{16,18},{18,... | collective-permute-start | bytes 6291464 | tf_op jit(solution)/shard_map/ppermute | solution.py:79
  511.8 30.7 %collective-permute-start.38 = (bf16[512,2048]{1,0:T(8,128)(2,1)}, bf16[512,2048]{1,0:T(8,128)(2,1)}, u32[]{:S(2)}, u32[]{:S(2)}) collective-permute-start(bf16[512,2048]{1,0:T(8,128)(2,1)} %get-tuple-element.251.refs_1_.refs_0_), channel_id=1, source_target_pairs={{0,2},{2,0},{4,6},{6,4},{8,10},{10,8},{12,14},{14,12},{16,18},{18,... | collective-permute-start | bytes 6291464 | tf_op jit(solution)/shard_map/ppermute | solution.py:79
  (69 other events, 533.3 us)
Sparse Core Ops, SparseCore 0:
  70.5 118.2 reduce-scatter.2
  233.9 74.2 all-gather.2
  313.1 95.3 reduce-scatter.4
  411.2 108.4 all-gather.4
